TPU v7x, 32 devices: a whole 2x2x4 slice. The times are simulated.
32 devices in a mesh: dp: 4 (over y, x), blk: 8 (over z, core).
Axes of the slice: x: 2, y: 2, z: 4, core: 2. Of those that a mesh axis runs over, the one named last changes fastest.
Arguments:
- crops_seven: bfloat16 [256, 7, 7, 2048], P(('dp', 'blk')), may hold values from -12 to 12
- crops_six: bfloat16 [192, 6, 6, 2048], P(('dp', 'blk')), may hold values from -12 to 12
- crops_five: bfloat16 [256, 5, 5, 2048], P(('dp', 'blk')), may hold values from -12 to 12
- conv_in: bfloat16 [2048, 512], replicated, may hold values from -0.125 to 0.125
- gain_in: float32 [512], replicated, may hold values from 0.5 to 1.5
- bias_in: float32 [512], replicated, may hold values from -1.75 to 1.75
- conv_mid: bfloat16 [3, 3, 512, 512], replicated, may hold values from -0.09375 to 0.09375
- gain_mid: float32 [512], replicated, may hold values from 0.5 to 1.5
- bias_mid: float32 [512], replicated, may hold values from -1.75 to 1.75
- conv_out: bfloat16 [512, 2048], replicated, may hold values from -0.25 to 0.25
- gain_out: float32 [2048], replicated, may hold values from 0.5 to 1.5
- bias_out: float32 [2048], replicated, may hold values from -1.75 to 1.75
- proj_hidden: bfloat16 [2048, 1024], replicated, may hold values from -0.125 to 0.125
- gain_proj: float32 [1024], replicated, may hold values from 0.5 to 1.5
- bias_proj: float32 [1024], replicated, may hold values from -1.75 to 1.75
- proj_embed: bfloat16 [1024, 128], replicated, may hold values from -0.1875 to 0.1875
- pair_index: int32 [1024, 2], P(('dp', 'blk')), may hold values from 0 to 21
Outputs:
- grad_seven: float32 [256, 7, 7, 2048], P(('dp', 'blk'))
- grad_six: float32 [192, 6, 6, 2048], P(('dp', 'blk'))
- grad_five: float32 [256, 5, 5, 2048], P(('dp', 'blk'))
- grad_conv_in: float32 [2048, 512], P('blk')
- grad_conv_mid: float32 [3, 3, 512, 512], P(None, None, 'blk')
- grad_conv_out: float32 [512, 2048], P('blk')
- grad_proj_hidden: float32 [2048, 1024], P('blk')
- grad_proj_embed: float32 [1024, 128], P('blk')
- grad_gain_in: float32 [512], replicated
- grad_bias_in: float32 [512], replicated
- grad_gain_mid: float32 [512], replicated
- grad_bias_mid: float32 [512], replicated
- grad_gain_out: float32 [2048], replicated
- grad_bias_out: float32 [2048], replicated
- grad_gain_proj: float32 [1024], replicated
- grad_bias_proj: float32 [1024], replicated
Inputs may be any that keep to these rules, and one draw needn't show every extreme that they name: `pair_index`: row r names two crops of device r // 32, as indices into that device's crops in the order 7x7, 6x6, 5x5.
All inputs are finite; a program needn't handle non-finite values.
Results may differ from a plain program's by a relative error of at most 0.014.
Values sent between devices are 32-bit elements; how exact they have to be, the bound alone decides.
No kernel may reach another device: no remote copies, remote signals or barrier semaphores. Data moves between devices by JAX's collectives and lax.ppermute only.
A program may use at most 192 MiB of HBM per device.

v0:
```python
import jax
import jax.numpy as jnp
from jax import lax
from jax.sharding import PartitionSpec as P

HIGHEST_PREC = lax.Precision.HIGHEST
NORM_EPS = 1e-05
UNIT_EPS = 1e-06
crop_sides = (7, 6, 5)


def silu_slope(values):
    sigmoid = jax.nn.sigmoid(values)
    return sigmoid * (1.0 + values * (1.0 - sigmoid))


def split_rows(row_block, counts, channels):
    pieces = []
    offset = 0
    for number, side_len in zip(counts, crop_sides):
        length = number * side_len * side_len
        pieces.append(
            row_block[offset : offset + length].reshape(number, side_len, side_len, channels)
        )
        offset = offset + length
    return pieces


def patch_rows(crop_grid, side_len):
    padded = jnp.pad(crop_grid, ((0, 0), (1, 1), (1, 1), (0, 0)))
    shifted = [
        padded[:, row_step : row_step + side_len, col_step : col_step + side_len, :]
        for row_step in range(3)
        for col_step in range(3)
    ]
    return jnp.concatenate(shifted, axis=-1).reshape(-1, 9 * crop_grid.shape[-1])


def fold_patches(grad_rows, counts, channels):
    folded = []
    offset = 0
    for number, side_len in zip(counts, crop_sides):
        length = number * side_len * side_len
        layered = grad_rows[offset : offset + length].reshape(
            number, side_len, side_len, 9, channels
        )
        summed = jnp.zeros((number, side_len + 2, side_len + 2, channels), jnp.float32)
        for position in range(9):
            row_step = position // 3
            col_step = position % 3
            summed = summed + jnp.pad(
                layered[:, :, :, position, :],
                ((0, 0), (row_step, 2 - row_step), (col_step, 2 - col_step), (0, 0)),
            )
        folded.append(summed[:, 1 : side_len + 1, 1 : side_len + 1, :].reshape(length, channels))
        offset = offset + length
    return jnp.concatenate(folded, axis=0)


def pool_crops(row_block, counts):
    crop_means = []
    offset = 0
    for number, side_len in zip(counts, crop_sides):
        length = number * side_len * side_len
        crop_means.append(
            jnp.mean(
                row_block[offset : offset + length].reshape(number, side_len * side_len, -1), axis=1
            )
        )
        offset = offset + length
    return jnp.concatenate(crop_means, axis=0)


def spread_crops(crop_block, counts):
    spread = []
    start_row = 0
    width = crop_block.shape[-1]
    for number, side_len in zip(counts, crop_sides):
        share = crop_block[start_row : start_row + number] / float(side_len * side_len)
        spread.append(
            jnp.broadcast_to(share[:, None, :], (number, side_len * side_len, width)).reshape(
                -1, width
            )
        )
        start_row = start_row + number
    return jnp.concatenate(spread, axis=0)


def global_pair(first_term, second_term):
    return lax.psum((first_term, second_term), ("dp", "blk"))


def normalize(activity, row_total):
    total, squares = global_pair(jnp.sum(activity, axis=0), jnp.sum(activity * activity, axis=0))
    mean_vec = total / row_total
    rstd = lax.rsqrt(squares / row_total - mean_vec * mean_vec + NORM_EPS)
    return ((activity - mean_vec) * rstd, rstd)


def norm_back(grad_in, normed, rstd, gain, row_total):
    grad_gain, grad_bias = global_pair(jnp.sum(grad_in * normed, axis=0), jnp.sum(grad_in, axis=0))
    back = gain * rstd * (grad_in - grad_bias / row_total - normed * grad_gain / row_total)
    return (back, grad_gain, grad_bias)


def whitener(matrix):
    factor_low = jnp.linalg.cholesky(matrix)
    return jax.scipy.linalg.solve_triangular(
        factor_low, jnp.eye(matrix.shape[0], dtype=jnp.float32), lower=True
    ).T


def body(
    crops_seven,
    crops_six,
    crops_five,
    conv_in,
    gain_in,
    bias_in,
    conv_mid,
    gain_mid,
    bias_mid,
    conv_out,
    gain_out,
    bias_out,
    proj_hidden,
    gain_proj,
    bias_proj,
    proj_embed,
    pair_index,
):
    devices = lax.axis_size("dp") * lax.axis_size("blk")
    width = crops_seven.shape[-1]
    channels = conv_in.shape[1]
    counts = (crops_seven.shape[0], crops_six.shape[0], crops_five.shape[0])
    inputs = jnp.concatenate(
        [
            crops_seven.reshape(-1, width),
            crops_six.reshape(-1, width),
            crops_five.reshape(-1, width),
        ],
        axis=0,
    )
    pixel_total = float(inputs.shape[0] * devices)
    hidden_map = proj_hidden.astype(jnp.float32)
    embed_map = proj_embed.astype(jnp.float32)
    first_pre = jnp.dot(inputs, conv_in, preferred_element_type=jnp.float32)
    normed_one, rstd_one = normalize(first_pre, pixel_total)
    gate_one = gain_in * normed_one + bias_in
    hidden_one = jax.nn.silu(gate_one).astype(jnp.bfloat16)
    patches = jnp.concatenate(
        [
            patch_rows(crop_grid, side_len)
            for crop_grid, side_len in zip(split_rows(hidden_one, counts, channels), crop_sides)
        ],
        axis=0,
    )
    kernel_flat = conv_mid.reshape(9 * channels, channels)
    second_pre = jnp.dot(patches, kernel_flat, preferred_element_type=jnp.float32)
    normed_two, rstd_two = normalize(second_pre, pixel_total)
    gate_two = gain_mid * normed_two + bias_mid
    hidden_two = jax.nn.silu(gate_two).astype(jnp.bfloat16)
    third_pre = jnp.dot(hidden_two, conv_out, preferred_element_type=jnp.float32)
    normed_three, rstd_three = normalize(third_pre, pixel_total)
    summed = inputs.astype(jnp.float32) + gain_out * normed_three + bias_out
    pooled = pool_crops(jax.nn.silu(summed), counts)
    crop_total = float(pooled.shape[0] * devices)
    proj_pre = jnp.dot(pooled, hidden_map, precision=HIGHEST_PREC)
    normed_proj, rstd_proj = normalize(proj_pre, crop_total)
    gate_proj = gain_proj * normed_proj + bias_proj
    hidden_proj = jax.nn.silu(gate_proj)
    embedding = jnp.dot(hidden_proj, embed_map, precision=HIGHEST_PREC)
    piece_rows = lax.all_gather(embedding, "blk", axis=0, tiled=True)
    square_part = jnp.dot(piece_rows.T, piece_rows, precision=HIGHEST_PREC)
    column_part = jnp.sum(piece_rows, axis=0)
    square_sum, column_sum = lax.psum((square_part, column_part), "dp")
    mean_embed = column_sum / crop_total
    covariance = square_sum / crop_total - jnp.outer(mean_embed, mean_embed)
    white_map, pull_white = jax.vjp(whitener, covariance)
    centered = embedding - mean_embed
    whitened = jnp.dot(centered, white_map, precision=HIGHEST_PREC)
    inv_length = lax.rsqrt(jnp.sum(whitened * whitened, axis=1, keepdims=True) + UNIT_EPS)
    unit_rows = whitened * inv_length
    slot_ids = jnp.arange(unit_rows.shape[0], dtype=jnp.int32)
    pick_diff = (pair_index[:, 0:1] == slot_ids).astype(jnp.float32) - (
        pair_index[:, 1:2] == slot_ids
    ).astype(jnp.float32)
    pair_gap = jnp.dot(pick_diff, unit_rows, precision=HIGHEST_PREC)
    grad_unit = 2.0 * jnp.dot(pick_diff.T, pair_gap, precision=HIGHEST_PREC)
    grad_white = (
        grad_unit - unit_rows * jnp.sum(unit_rows * grad_unit, axis=1, keepdims=True)
    ) * inv_length
    pieces = (
        lax.all_gather(centered, "blk", axis=0, tiled=True),
        lax.all_gather(grad_white, "blk", axis=0, tiled=True),
    )
    cross_part = jnp.dot(pieces[0].T, pieces[1], precision=HIGHEST_PREC)
    grad_part = jnp.sum(pieces[1], axis=0)
    cross_sum, grad_column = lax.psum((cross_part, grad_part), "dp")
    (grad_cov,) = pull_white(cross_sum)
    grad_center = (
        jnp.dot(grad_white, white_map.T, precision=HIGHEST_PREC)
        + jnp.dot(centered, grad_cov + grad_cov.T, precision=HIGHEST_PREC) / crop_total
    )
    grad_embed = (
        grad_center - jnp.dot(grad_column, white_map.T, precision=HIGHEST_PREC) / crop_total
    )
    local_proj_embed = jnp.dot(hidden_proj.T, grad_embed, precision=HIGHEST_PREC)
    grad_gate_proj = jnp.dot(grad_embed, embed_map.T, precision=HIGHEST_PREC) * silu_slope(
        gate_proj
    )
    back_proj, grad_gain_proj, grad_bias_proj = norm_back(
        grad_gate_proj, normed_proj, rstd_proj, gain_proj, crop_total
    )
    local_proj_hidden = jnp.dot(pooled.T, back_proj, precision=HIGHEST_PREC)
    grad_pooled = jnp.dot(back_proj, hidden_map.T, precision=HIGHEST_PREC)
    grad_summed = spread_crops(grad_pooled, counts) * silu_slope(summed)
    back_three, grad_gain_out, grad_bias_out = norm_back(
        grad_summed, normed_three, rstd_three, gain_out, pixel_total
    )
    back_three_low = back_three.astype(jnp.bfloat16)
    local_conv_out = jnp.dot(hidden_two.T, back_three_low, preferred_element_type=jnp.float32)
    grad_gate_two = jnp.dot(
        back_three_low, conv_out.T, preferred_element_type=jnp.float32
    ) * silu_slope(gate_two)
    back_two, grad_gain_mid, grad_bias_mid = norm_back(
        grad_gate_two, normed_two, rstd_two, gain_mid, pixel_total
    )
    back_two_low = back_two.astype(jnp.bfloat16)
    local_conv_mid = jnp.dot(patches.T, back_two_low, preferred_element_type=jnp.float32).reshape(
        3, 3, channels, channels
    )
    grad_patches = jnp.dot(back_two_low, kernel_flat.T, preferred_element_type=jnp.float32)
    grad_gate_one = fold_patches(grad_patches, counts, channels) * silu_slope(gate_one)
    back_one, grad_gain_in, grad_bias_in = norm_back(
        grad_gate_one, normed_one, rstd_one, gain_in, pixel_total
    )
    back_one_low = back_one.astype(jnp.bfloat16)
    local_conv_in = jnp.dot(inputs.T, back_one_low, preferred_element_type=jnp.float32)
    grad_inputs = grad_summed + jnp.dot(back_one_low, conv_in.T, preferred_element_type=jnp.float32)
    shares = (
        lax.psum_scatter(local_conv_in, "blk", scatter_dimension=0, tiled=True),
        lax.psum_scatter(local_conv_mid, "blk", scatter_dimension=2, tiled=True),
        lax.psum_scatter(local_conv_out, "blk", scatter_dimension=0, tiled=True),
        lax.psum_scatter(local_proj_hidden, "blk", scatter_dimension=0, tiled=True),
        lax.psum_scatter(local_proj_embed, "blk", scatter_dimension=0, tiled=True),
    )
    summed_grads = lax.psum((shares[0], shares[1], shares[2], shares[3], shares[4]), "dp")
    seven_len = counts[0] * 49
    six_len = counts[1] * 36
    grad_seven = grad_inputs[:seven_len].reshape(crops_seven.shape)
    grad_six = grad_inputs[seven_len : seven_len + six_len].reshape(crops_six.shape)
    grad_five = grad_inputs[seven_len + six_len :].reshape(crops_five.shape)
    return (
        grad_seven,
        grad_six,
        grad_five,
        summed_grads[0],
        summed_grads[1],
        summed_grads[2],
        summed_grads[3],
        summed_grads[4],
        grad_gain_in,
        grad_bias_in,
        grad_gain_mid,
        grad_bias_mid,
        grad_gain_out,
        grad_bias_out,
        grad_gain_proj,
        grad_bias_proj,
    )


def solution(mesh):
    in_specs = (
        P(("dp", "blk"), None, None, None),
        P(("dp", "blk"), None, None, None),
        P(("dp", "blk"), None, None, None),
        P(),
        P(),
        P(),
        P(),
        P(),
        P(),
        P(),
        P(),
        P(),
        P(),
        P(),
        P(),
        P(),
        P(("dp", "blk"), None),
    )
    out_specs = (
        P(("dp", "blk"), None, None, None),
        P(("dp", "blk"), None, None, None),
        P(("dp", "blk"), None, None, None),
        P("blk", None),
        P(None, None, "blk", None),
        P("blk", None),
        P("blk", None),
        P("blk", None),
        P(),
        P(),
        P(),
        P(),
        P(),
        P(),
        P(),
        P(),
    )
    return jax.shard_map(body, mesh=mesh, in_specs=in_specs, out_specs=out_specs, check_vma=False)
```

profile of v0, /device:TPU:0, one launch (start us, length us, event | category | flops | bytes accessed | tf_op | source)
XLA Modules:
  0.0 1136.4 jit_solution(14727890668673366262)
XLA Ops:
  25.6 42.1 %all-reduce.37 = (f32[512]{0:T(512)S(1)}, f32[512]{0:T(512)S(1)}) all-reduce(f32[512]{0:T(512)S(1)} %get-tuple-element.220, f32[512]{0:T(512)S(1)} %get-tuple-element.219), channel_id=1, replica_groups=mesh['dp'=4,'blk'=8] {'dp','blk'}, use_global_device_ids=true, to_apply=%region_3.0 | all-reduce | flops 1024 | bytes 8192 | tf_op jit(solution)/shard_map/psum | solution.py:90
  148.0 10.1 fusion.76
  158.1 40.1 %all-reduce.36 = (f32[512]{0:T(512)S(1)}, f32[512]{0:T(512)S(1)}) all-reduce(f32[512]{0:T(512)S(1)} %get-tuple-element.218, f32[512]{0:T(512)S(1)} %get-tuple-element.217), channel_id=1, replica_groups=mesh['dp'=4,'blk'=8] {'dp','blk'}, use_global_device_ids=true, to_apply=%region_7.8 | all-reduce | flops 1024 | bytes 8192 | tf_op jit(solution)/shard_map/psum | solution.py:90
  204.6 40.3 %all-reduce.35 = (f32[2048]{0:T(1024)S(1)}, f32[2048]{0:T(1024)S(1)}) all-reduce(f32[2048]{0:T(1024)S(1)} %get-tuple-element.212, f32[2048]{0:T(1024)S(1)} %get-tuple-element.211), channel_id=1, replica_groups=mesh['dp'=4,'blk'=8] {'dp','blk'}, use_global_device_ids=true, to_apply=%region_11.12 | all-reduce | flops 4096 | bytes 32768 | tf_op jit(solution)/shard_map/psum | solution.py:90
  274.8 40.2 %all-reduce.34 = (f32[1024]{0:T(1024)S(1)}, f32[1024]{0:T(1024)S(1)}) all-reduce(f32[1024]{0:T(1024)S(1)} %get-tuple-element.224, f32[1024]{0:T(1024)S(1)} %get-tuple-element.223), channel_id=1, replica_groups=mesh['dp'=4,'blk'=8] {'dp','blk'}, use_global_device_ids=true, to_apply=%region_16.17 | all-reduce | flops 2048 | bytes 16384 | tf_op jit(solution)/shard_map/psum | solution.py:90
  315.3 13.9 %all-gather = f32[8,22,128]{2,1,0:T(8,128)S(1)} all-gather(f32[1,22,128]{2,1,0:T(8,128)S(1)} %bitcast.200), channel_id=1, replica_groups=mesh['dp'=4,'blk'=8] {'blk'}, dimensions={0}, use_global_device_ids=true | all-gather | bytes 101376 | tf_op jit(solution)/shard_map/all_gather | solution.py:173
  330.5 10.7 psum.183
  341.2 14.3 %all-gather.1 = f32[8,22,128]{2,1,0:T(8,128)S(1)} all-gather(f32[1,22,128]{2,1,0:T(8,128)S(1)} %subtract_bitcast_fusion), channel_id=1, replica_groups=mesh['dp'=4,'blk'=8] {'blk'}, dimensions={0}, use_global_device_ids=true | all-gather | bytes 101376 | tf_op jit(solution)/shard_map/all_gather | solution.py:194
  355.5 17.3 %all-reduce.43.cloned.1.call-done = f32[128,128]{0,1:T(8,128)} async-done(((f32[128,128]{0,1:T(8,128)}), f32[128,128]{0,1:T(8,128)}) %all-reduce.43.cloned.1.call-update) | async-done | bytes 65552 | tf_op jit(solution)/shard_map/psum | solution.py:176
  374.7 11.7 %cholesky.18 = f32[128,128]{1,0:T(8,128)S(1)} custom-call(f32[128,128]{1,0:T(8,128)S(1)} %fusion.26), custom_call_target="Cholesky" | custom-call | tf_op jit(solution)/shard_map/jvp(jit(cholesky))/cholesky | solution.py:107
  399.1 14.0 %all-gather.2 = f32[8,22,128]{2,1,0:T(8,128)S(1)} all-gather(f32[1,22,128]{2,1,0:T(8,128)S(1)} %fusion.64), channel_id=1, replica_groups=mesh['dp'=4,'blk'=8] {'blk'}, dimensions={0}, use_global_device_ids=true | all-gather | bytes 101376 | tf_op jit(solution)/shard_map/all_gather | solution.py:195
  423.4 9.8 custom-call.18
  433.3 31.6 %all-reduce.45.cloned.1.call-done = f32[128,128]{1,0:T(8,128)} async-done(((f32[128,128]{1,0:T(8,128)}), f32[128,128]{1,0:T(8,128)}) %all-reduce.45.cloned.1.call-update) | async-done | bytes 65552 | tf_op jit(solution)/shard_map/psum | solution.py:199
  468.3 39.6 %all-reduce.33 = (f32[1024]{0:T(1024)S(1)}, f32[1024]{0:T(1024)S(1)}) all-reduce(f32[1024]{0:T(1024)S(1)} %get-tuple-element.222, f32[1024]{0:T(1024)S(1)} %get-tuple-element.221), channel_id=1, replica_groups=mesh['dp'=4,'blk'=8] {'dp','blk'}, use_global_device_ids=true, to_apply=%region_32.34 | all-reduce | flops 2048 | bytes 16384 | tf_op jit(solution)/shard_map/psum | solution.py:90
  540.0 41.1 %all-reduce.32 = (f32[2048]{0:T(1024)S(1)}, f32[2048]{0:T(1024)S(1)}) all-reduce(f32[2048]{0:T(1024)S(1)} %get-tuple-element.210, f32[2048]{0:T(1024)S(1)} %get-tuple-element.209), channel_id=1, replica_groups=mesh['dp'=4,'blk'=8] {'dp','blk'}, use_global_device_ids=true, to_apply=%region_36.38 | all-reduce | flops 4096 | bytes 32768 | tf_op jit(solution)/shard_map/psum | solution.py:90
  600.4 41.2 %all-reduce.31 = (f32[512]{0:T(512)S(1)}, f32[512]{0:T(512)S(1)}) all-reduce(f32[512]{0:T(512)S(1)} %get-tuple-element.216, f32[512]{0:T(512)S(1)} %get-tuple-element.215), channel_id=1, replica_groups=mesh['dp'=4,'blk'=8] {'dp','blk'}, use_global_device_ids=true, to_apply=%region_40.42 | all-reduce | flops 1024 | bytes 8192 | tf_op jit(solution)/shard_map/psum | solution.py:90
  663.5 13.8 %fusion.82 = (f32[8,5,5,1,512]{4,3,2,1,0:T(1,128)S(1)}, f32[8,5,5,1,512]{4,3,2,1,0:T(1,128)S(1)}, f32[8,5,5,1,512]{4,3,2,1,0:T(1,128)S(1)}, f32[8,5,5,1,512]{4,3...) fusion(f32[8,5,5,9,512]{4,3,2,1,0:T(8,128)} %reshape.212), kind=kLoop, calls=%fused_computation.261 | loop fusion | bytes 7372800 | tf_op jit(solution)/shard_map/slice | solution.py:52
  684.3 14.8 %fusion.81 = (f32[6,6,6,1,512]{4,3,2,1,0:T(1,128)S(1)}, f32[6,6,6,1,512]{4,3,2,1,0:T(1,128)S(1)}, f32[6,6,6,1,512]{4,3,2,1,0:T(1,128)S(1)}, f32[6,6,6,1,512]{4,3...) fusion(f32[6,6,6,9,512]{4,3,2,1,0:T(8,128)} %reshape.210), kind=kLoop, calls=%fused_computation.260 | loop fusion | bytes 7962624 | tf_op jit(solution)/shard_map/slice | solution.py:52
  710.3 24.2 %fusion.80 = (f32[8,7,7,1,512]{4,3,2,1,0:T(1,128)S(1)}, f32[8,7,7,1,512]{4,3,2,1,0:T(1,128)S(1)}, f32[8,7,7,1,512]{4,3,2,1,0:T(1,128)S(1)}, f32[8,7,7,1,512]{4,3...) fusion(f32[8,7,7,9,512]{4,3,2,1,0:T(8,128)} %reshape.208), kind=kLoop, calls=%fused_computation.259 | loop fusion | bytes 14450688 | tf_op jit(solution)/shard_map/slice | solution.py:52
  740.7 40.8 %all-reduce.30 = (f32[512]{0:T(512)S(1)}, f32[512]{0:T(512)S(1)}) all-reduce(f32[512]{0:T(512)S(1)} %get-tuple-element.214, f32[512]{0:T(512)S(1)} %get-tuple-element.213), channel_id=1, replica_groups=mesh['dp'=4,'blk'=8] {'dp','blk'}, use_global_device_ids=true, to_apply=%region_44.46 | all-reduce | flops 1024 | bytes 8192 | tf_op jit(solution)/shard_map/psum | solution.py:90
  809.5 28.9 %reduce-scatter.6.cloned.1.call-done = f32[256,512]{1,0:T(8,128)} async-done(((f32[2048,512]{1,0:T(8,128)}), f32[256,512]{1,0:T(8,128)}) %reduce-scatter.6.cloned.1.call-update) | async-done | bytes 524304 | tf_op jit(solution)/shard_map/reduce_scatter | solution.py:242
  838.4 90.0 %reduce-scatter.12.cloned.1.call-done = f32[256,1024]{1,0:T(8,128)} async-done(((f32[2048,1024]{1,0:T(8,128)}), f32[256,1024]{1,0:T(8,128)}) %reduce-scatter.12.cloned.1.call-update) | async-done | bytes 1048592 | tf_op jit(solution)/shard_map/reduce_scatter | solution.py:245
  928.4 100.3 %reduce-scatter.8.cloned.1.call-done = f32[3,3,64,512]{3,2,1,0:T(8,128)} async-done(((f32[3,3,512,512]{3,2,1,0:T(8,128)}), f32[3,3,64,512]{3,2,1,0:T(8,128)}) %reduce-scatter.8.cloned.1.call-update) | async-done | bytes 1179664 | tf_op jit(solution)/shard_map/reduce_scatter | solution.py:243
  1055.0 67.4 %all-reduce.47.cloned.1.call-done = (f32[256,512]{1,0:T(8,128)}, f32[3,3,64,512]{3,2,1,0:T(8,128)}, f32[64,2048]{1,0:T(8,128)}, f32[256,1024]{1,0:T(8,128)}, f32[128,128]{1,0:T(8,128)}) async-done(((f32[256,512]{1,0:T(8,128)}, f32[3,3,64,512]{3,2,1,0:T(8,128)}, f32[64,2048]{1,0:T(8,128)}, f32[256,1024]{1,0:T(8,128)}, f32[128,128]{1,0:T(8,128)}), (f32[256,512]{1,0:T(8,128)}, f32[3,3,64,512]{3,2,1,0:T(8,128)}, ...) | async-done | bytes 3342352 | tf_op jit(solution)/shard_map/psum | solution.py:248
  (346 shorter events, 322.5 us)
Async XLA Ops:
  7.2 191.0 %copy-start = (bf16[512,2048]{1,0:T(8,128)(2,1)S(1)}, bf16[512,2048]{1,0:T(8,128)(2,1)}, u32[]{:S(2)}) copy-start(bf16[512,2048]{1,0:T(8,128)(2,1)} %param.28) | copy-start | bytes 6291460
  7.2 365.6 %all-reduce.43.cloned.1.call-start = ((), (), s32[]{:S(2)}) async-start(), calls=%async_computation.5 | async-start | bytes 131072 | tf_op jit(solution)/shard_map/psum | solution.py:176
  22.6 45.2 %copy-start.43 = (f32[512]{0:T(512)S(1)}, f32[512]{0:T(512)}, u32[]{:S(2)}) copy-start(f32[512]{0:T(512)} %param.23) | copy-start | bytes 6148
  22.6 45.8 %copy-start.48 = (f32[512]{0:T(512)S(1)}, f32[512]{0:T(512)}, u32[]{:S(2)}) copy-start(f32[512]{0:T(512)} %param.24) | copy-start | bytes 6148
  148.0 10.1 copy-start.41
  148.0 50.2 %copy-start.56 = (f32[512]{0:T(512)S(1)}, f32[512]{0:T(512)}, u32[]{:S(2)}) copy-start(f32[512]{0:T(512)} %param.26) | copy-start | bytes 6148
  148.0 50.2 %copy-start.59 = (f32[512]{0:T(512)S(1)}, f32[512]{0:T(512)}, u32[]{:S(2)}) copy-start(f32[512]{0:T(512)} %param.27) | copy-start | bytes 6148
  198.2 46.7 %copy-start.39 = (f32[2048]{0:T(1024)S(1)}, f32[2048]{0:T(1024)}, u32[]{:S(2)}) copy-start(f32[2048]{0:T(1024)} %param.29) | copy-start | bytes 24580
  198.3 46.7 %copy-start.42 = (f32[2048]{0:T(1024)S(1)}, f32[2048]{0:T(1024)}, u32[]{:S(2)}) copy-start(f32[2048]{0:T(1024)} %param.30) | copy-start | bytes 24580
  270.8 44.3 %copy-start.45 = (f32[1024]{0:T(1024)S(1)}, f32[1024]{0:T(1024)}, u32[]{:S(2)}) copy-start(f32[1024]{0:T(1024)} %param.32) | copy-start | bytes 12292
  270.8 44.3 %copy-start.50 = (f32[1024]{0:T(1024)S(1)}, f32[1024]{0:T(1024)}, u32[]{:S(2)}) copy-start(f32[1024]{0:T(1024)} %param.33) | copy-start | bytes 12292
  270.8 44.3 %copy-start.58 = (bf16[1024,128]{1,0:T(8,128)(2,1)S(1)}, bf16[1024,128]{1,0:T(8,128)(2,1)}, u32[]{:S(2)}) copy-start(bf16[1024,128]{1,0:T(8,128)(2,1)} %param.34) | copy-start | bytes 786436
  270.8 59.7 %copy-start.57 = (s32[32,2]{0,1:T(2,128)S(1)}, s32[32,2]{0,1:T(2,128)}, u32[]{:S(2)}) copy-start(s32[32,2]{0,1:T(2,128)} %param.35) | copy-start | bytes 772
  330.4 134.5 %all-reduce.45.cloned.1.call-start = ((), (), s32[]{:S(2)}) async-start(), calls=%async_computation.6 | async-start | bytes 131072 | tf_op jit(solution)/shard_map/psum | solution.py:199
  423.2 386.2 %reduce-scatter.14.cloned.1.call-start = ((), (), s32[]{:S(2)}) async-start(), calls=%async_computation.11 | async-start | bytes 589824 | tf_op jit(solution)/shard_map/reduce_scatter | solution.py:246
  468.3 45.2 %copy-start.37 = (f32[22,1024]{1,0:T(8,128)}, f32[22,1024]{1,0:T(8,128)S(1)}, u32[]{:S(2)}) copy-start(f32[22,1024]{1,0:T(8,128)S(1)} %get-tuple-element.325) | copy-start | bytes 270340
  507.9 280.6 %copy-start.44 = (f32[1024]{0:T(1024)}, f32[1024]{0:T(1024)S(1)}, u32[]{:S(2)}) copy-start(f32[1024]{0:T(1024)S(1)} %get-tuple-element.343) | copy-start | bytes 12292
  515.4 294.1 %reduce-scatter.10.cloned.1.call-start = ((), (), s32[]{:S(2)}) async-start(), calls=%async_computation.9 | async-start | bytes 4718592 | tf_op jit(solution)/shard_map/reduce_scatter | solution.py:244
  594.3 244.1 %reduce-scatter.6.cloned.1.call-start = ((), (), s32[]{:S(2)}) async-start(), calls=%async_computation.7 | async-start | bytes 4718592 | tf_op jit(solution)/shard_map/reduce_scatter | solution.py:242
  737.5 44.0 %copy-start.47 = (f32[512]{0:T(512)S(1)}, f32[512]{0:T(512)}, u32[]{:S(2)}) copy-start(f32[512]{0:T(512)} %get-tuple-element.308) | copy-start | bytes 6148
  788.5 139.9 %reduce-scatter.12.cloned.1.call-start = ((), (), s32[]{:S(2)}) async-start(), calls=%async_computation.10 | async-start | bytes 9437184 | tf_op jit(solution)/shard_map/reduce_scatter | solution.py:245
  798.4 230.3 %reduce-scatter.8.cloned.1.call-start = ((), (), s32[]{:S(2)}) async-start(), calls=%async_computation.8 | async-start | bytes 10616832 | tf_op jit(solution)/shard_map/reduce_scatter | solution.py:243
  809.3 219.4 %copy-start.10 = (bf16[2048,512]{1,0:T(8,128)(2,1)S(1)}, bf16[2048,512]{1,0:T(8,128)(2,1)}, u32[]{:S(2)}) copy-start(bf16[2048,512]{1,0:T(8,128)(2,1)} %param.22) | copy-start | bytes 6291460
  809.4 313.0 %all-reduce.47.cloned.1.call-start = ((), (), s32[]{:S(2)}) async-start(), calls=%async_computation.12 | async-start | bytes 6684672 | tf_op jit(solution)/shard_map/psum | solution.py:248
  (45 other events, 172.3 us)
Sparse Core Ops, SparseCore 0:
  330.5 42.2 all-reduce.42
  423.3 41.4 all-reduce.44
  515.5 31.7 reduce-scatter.13
  594.4 50.8 reduce-scatter.9
  788.6 49.7 reduce-scatter.5
  840.6 87.7 reduce-scatter.11
  930.8 97.8 reduce-scatter.7
  1032.8 89.5 all-reduce.46
where the time goes:
time: 1140 us
  blocking collectives  387 us (34%)
  waiting for transfers between devices  336 us (29%)
  local copies, waits for them, and re-layouts  240 us (21%)
  matrix products  83.2 us (7%)
  other arithmetic  74.3 us (7%)
  between operations  15.6 us (1%)
    psum x8, blocking collectives, global_pair(): return lax.psum((first_term, second_term), ('dp', 'blk'))  325 us
    reduce_scatter x1, waiting for transfers between devices, body(): lax.psum_scatter(local_conv_mid, 'blk', scatter_dimension=2, tiled=True)  100 us
    reduce_scatter x1, waiting for transfers between devices, body(): lax.psum_scatter(local_proj_hidden, 'blk', scatter_dimension=0, tiled=True)  90 us
    psum x1, waiting for transfers between devices, body(): lax.psum((shares[0], shares[1], shares[2], shares[3], shares[4]), 'dp')  67.4 us
    unnamed x167, local copies, waits for them, and re-layouts  55 us
    slice x21, local copies, waits for them, and re-layouts, fold_patches(): layered[:, :, :, position, :]  53.6 us
    concatenate x27, local copies, waits for them, and re-layouts, patch_rows(): jnp.concatenate(shifted, axis=-1).reshape(-1, 9 * crop_grid.shape[-1])  43.6 us
    psum x1, waiting for transfers between devices, body(): cross_sum, grad_column = lax.psum((cross_part, grad_part), 'dp')  31.6 us
  transfers between devices with their start and end apart: 8, of which 6 were waited for; matrix products, arithmetic and copies ran while one was open for 18% of the time, Pallas kernels for 0%

commit v1 on v0

v1 whole, which is shorter than its diff:
```python
import jax
import jax.numpy as jnp
from jax import lax
from jax.experimental import pallas as pl
from jax.experimental.pallas import tpu as pltpu

F32 = jnp.float32
BF16 = jnp.bfloat16
NORM_EPS = 1e-05
UNIT_EPS = 1e-06
MIB = 1 << 20


def vmem(count):
    return pltpu.CompilerParams(vmem_limit_bytes=count * MIB)


def geometry(shapes):
    parts = []
    first = 0
    for shape in shapes:
        parts.append((shape[0], shape[1], first))
        first += shape[0] * shape[1]
    return parts, first


def silu_parts(q):
    s = 1.0 / (1.0 + jnp.exp(-q))
    return s


def live_rows(rows, width, side):
    return lax.rem(lax.broadcasted_iota(jnp.int32, (rows, width), 0), 8) < side


def moments(st_ref, total):
    mean = st_ref[0:1, :] * (1.0 / total)
    var = st_ref[1:2, :] * (1.0 / total) - mean * mean
    return mean, lax.rsqrt(var + NORM_EPS)


def split3(x):
    h = x.astype(BF16)
    r = x - h.astype(F32)
    m = r.astype(BF16)
    l = (r - m.astype(F32)).astype(BF16)
    return h, m, l


def split2(x):
    h = x.astype(BF16)
    return h, (x - h.astype(F32)).astype(BF16)


def mm(a, b):
    return jnp.dot(a, b, preferred_element_type=F32)


def mm_nt(a, b):
    return lax.dot_general(a, b, (((1,), (1,)), ((), ())), preferred_element_type=F32)


def mm_tn(a, b):
    return lax.dot_general(a, b, (((0,), (0,)), ((), ())), preferred_element_type=F32)


def first_conv(crops, conv_in):
    parts, slabs = geometry([c.shape for c in crops])
    width = conv_in.shape[0]
    chan = conv_in.shape[1]

    def kernel(x7, x6, x5, w_ref, xp_ref, a_ref, st_ref):
        total = jnp.zeros((1, chan), F32)
        squares = jnp.zeros((1, chan), F32)
        for ref, (n, s, first) in zip((x7, x6, x5), parts):
            for c in range(0, n, 2):
                rows = ref[c : c + 2].astype(F32).reshape(2 * s, s, width)
                rows = jnp.concatenate([rows, jnp.zeros((2 * s, 8 - s, width), F32)], axis=1)
                at = (first + c * s) * 8
                xp_ref[at : at + 16 * s, :] = rows.reshape(16 * s, width).astype(BF16)
            at = first * 8
            out = mm(xp_ref[at : at + n * s * 8, :], w_ref[...])
            total = total + jnp.sum(out, axis=0, keepdims=True)
            squares = squares + jnp.sum(out * out, axis=0, keepdims=True)
            out = out.reshape(n * s, 8, chan)
            for c in range(n):
                for i in range(s):
                    a_ref[first + i * n + c] = out[c * s + i]
        st_ref[0:1, :] = total
        st_ref[1:2, :] = squares

    return pl.pallas_call(
        kernel,
        out_shape=(
            jax.ShapeDtypeStruct((slabs * 8, width), BF16),
            jax.ShapeDtypeStruct((slabs, 8, chan), F32),
            jax.ShapeDtypeStruct((2, chan), F32),
        ),
        compiler_params=vmem(48),
        name="first_conv",
    )(*crops, conv_in)


def middle_conv(parts, first_pre, sums, total, gain, bias, kernel_rows):
    slabs, _, chan = first_pre.shape
    rows_all = slabs * 8

    def kernel(a_ref, st_ref, g_ref, b_ref, w_ref, cat_ref, o_ref, so_ref):
        mean, rstd = moments(st_ref, total)
        scale = g_ref[...] * rstd
        shift = b_ref[...] - mean * scale
        tot = jnp.zeros((1, chan), F32)
        squares = jnp.zeros((1, chan), F32)
        for n, s, first in parts:
            rows = n * s * 8
            at = first * 8
            step = n * 8
            keep = live_rows(rows, chan, s)
            q = a_ref[first : first + n * s].reshape(rows, chan) * scale + shift
            y = jnp.where(keep, q * silu_parts(q), 0.0)
            cat_ref[at : at + rows, 0:chan] = pltpu.roll(y, 1, 0).astype(BF16)
            cat_ref[at : at + rows, chan : 2 * chan] = y.astype(BF16)
            cat_ref[at : at + rows, 2 * chan : 3 * chan] = pltpu.roll(y, rows - 1, 0).astype(BF16)
            o_ref[at : at + rows, :] = mm(cat_ref[at : at + rows, :], w_ref[1])
            o_ref[at + step : at + rows, :] += mm(cat_ref[at : at + rows - step, :], w_ref[0])
            o_ref[at : at + rows - step, :] += mm(cat_ref[at + step : at + rows, :], w_ref[2])
            out = jnp.where(keep, o_ref[at : at + rows, :], 0.0)
            o_ref[at : at + rows, :] = out
            tot = tot + jnp.sum(out, axis=0, keepdims=True)
            squares = squares + jnp.sum(out * out, axis=0, keepdims=True)
        so_ref[0:1, :] = tot
        so_ref[1:2, :] = squares

    return pl.pallas_call(
        kernel,
        out_shape=(
            jax.ShapeDtypeStruct((rows_all, 3 * chan), BF16),
            jax.ShapeDtypeStruct((rows_all, chan), F32),
            jax.ShapeDtypeStruct((2, chan), F32),
        ),
        compiler_params=vmem(48),
        name="middle_conv",
    )(first_pre, sums, gain, bias, kernel_rows)


def last_conv(parts, second_pre, sums, total, gain, bias, conv_out):
    slabs, _, chan = second_pre.shape
    rows_all = slabs * 8
    width = conv_out.shape[1]
    block = 512

    def kernel(a_ref, st_ref, g_ref, b_ref, w_ref, y_ref, o_ref, so_ref, scr):
        @pl.when(pl.program_id(0) == 0)
        def _():
            mean, rstd = moments(st_ref, total)
            scale = g_ref[...] * rstd
            shift = b_ref[...] - mean * scale
            for n, s, first in parts:
                rows = n * s * 8
                q = a_ref[first : first + n * s].reshape(rows, chan) * scale + shift
                y = jnp.where(live_rows(rows, chan, s), q * silu_parts(q), 0.0).reshape(n * s, 8, chan)
                for i in range(s):
                    for c in range(n):
                        scr[first + c * s + i] = y[i * n + c]
            y_ref[...] = scr[...].reshape(rows_all, chan).astype(BF16)

        out = mm(y_ref[...], w_ref[...])
        o_ref[...] = out
        so_ref[0:1, :] = jnp.sum(out, axis=0, keepdims=True)
        so_ref[1:2, :] = jnp.sum(out * out, axis=0, keepdims=True)

    whole = lambda shape: pl.BlockSpec(shape, lambda j: (0,) * len(shape))
    return pl.pallas_call(
        kernel,
        grid=(width // block,),
        in_specs=[
            whole((slabs, 8, chan)),
            whole((2, chan)),
            whole((1, chan)),
            whole((1, chan)),
            pl.BlockSpec((chan, block), lambda j: (0, j)),
        ],
        out_specs=[
            whole((rows_all, chan)),
            pl.BlockSpec((rows_all, block), lambda j: (0, j)),
            pl.BlockSpec((2, block), lambda j: (0, j)),
        ],
        out_shape=(
            jax.ShapeDtypeStruct((rows_all, chan), BF16),
            jax.ShapeDtypeStruct((rows_all, width), F32),
            jax.ShapeDtypeStruct((2, width), F32),
        ),
        scratch_shapes=[pltpu.VMEM((slabs, 8, chan), F32)],
        compiler_params=vmem(40),
        name="last_conv",
    )(second_pre, sums, gain, bias, conv_out)


def crop_sums(parts, values, put):
    crop = 0
    for n, s, first in parts:
        block = values[first * 8 : (first + n * s) * 8].reshape(n, s, 8, values.shape[-1])
        block = jnp.sum(block, axis=1)
        put(crop, n, s, jnp.sum(block, axis=1))
        crop += n


def live_mask(parts, width):
    return jnp.concatenate([live_rows(n * s * 8, width, s) for n, s, _ in parts], axis=0)


def pool_embed(parts, slots, third_pre, sums, total, gain, bias, inputs, hidden_map, pair_row):
    rows_all, width = third_pre.shape
    hidden = hidden_map.shape[1]
    block = 256
    steps = width // block

    def kernel(a_ref, st_ref, g_ref, b_ref, x_ref, w_ref, p_ref, e_ref, ap_ref, scr, acc):
        j = pl.program_id(0)
        mean, rstd = moments(st_ref, total)
        scale = g_ref[...] * rstd
        shift = b_ref[...] - mean * scale
        scr[...] = jnp.zeros_like(scr)
        crop = 0
        for n, s, first in parts:
            rows = n * s * 8
            at = first * 8
            r = x_ref[at : at + rows, :].astype(F32) + (a_ref[at : at + rows, :] * scale + shift)
            v = jnp.where(live_rows(rows, block, s), r * silu_parts(r), 0.0)
            v = jnp.sum(jnp.sum(v.reshape(n, s, 8, block), axis=1), axis=1)
            scr[crop : crop + n, :] = v * (1.0 / (s * s))
            crop += n
        e = scr[...]
        e_ref[...] = e[0:slots]
        h, m, l = split3(e)
        out = mm(jnp.concatenate([h, m, l], axis=0), w_ref[...])

        @pl.when(j == 0)
        def _():
            acc[...] = out

        @pl.when(j > 0)
        def _():
            acc[...] += out

        @pl.when(j == steps - 1)
        def _():
            ap_ref[...] = acc[0:slots] + acc[32 : 32 + slots] + acc[64 : 64 + slots]
            ap_ref[crop : crop + 1, :] = p_ref[...]

    lane = lambda rows: pl.BlockSpec((rows, block), lambda j: (0, j))
    return pl.pallas_call(
        kernel,
        grid=(steps,),
        in_specs=[
            lane(rows_all),
            lane(2),
            lane(1),
            lane(1),
            lane(rows_all),
            pl.BlockSpec((block, hidden), lambda j: (j, 0)),
            pl.BlockSpec((1, hidden), lambda j: (0, 0)),
        ],
        out_specs=[lane(slots), pl.BlockSpec((slots, hidden), lambda j: (0, 0))],
        out_shape=(
            jax.ShapeDtypeStruct((slots, width), F32),
            jax.ShapeDtypeStruct((slots, hidden), F32),
        ),
        scratch_shapes=[pltpu.VMEM((32, block), F32), pltpu.VMEM((96, hidden), F32)],
        compiler_params=vmem(40),
        name="pool_embed",
    )(third_pre, sums, gain, bias, inputs, hidden_map, pair_row)


def slope_sums(parts, slots, third_pre, sums, total, gain, bias, inputs):
    rows_all, width = third_pre.shape
    block = 256

    def kernel(a_ref, st_ref, g_ref, b_ref, x_ref, s_ref, p_ref, t_ref):
        mean, rstd = moments(st_ref, total)
        gain_v = g_ref[...]
        bias_v = b_ref[...]
        p_ref[...] = jnp.zeros_like(p_ref)
        t_ref[...] = jnp.zeros_like(t_ref)
        crop = 0
        for n, s, first in parts:
            rows = n * s * 8
            at = first * 8
            normed = (a_ref[at : at + rows, :] - mean) * rstd
            r = x_ref[at : at + rows, :].astype(F32) + (normed * gain_v + bias_v)
            sig = silu_parts(r)
            v = jnp.where(live_rows(rows, block, s), sig * (1.0 + r * (1.0 - sig)), 0.0)
            s_ref[at : at + rows, :] = v.astype(BF16)
            p_ref[crop : crop + n, :] = jnp.sum(jnp.sum(v.reshape(n, s, 8, block), axis=1), axis=1)
            v = v * normed
            t_ref[crop : crop + n, :] = jnp.sum(jnp.sum(v.reshape(n, s, 8, block), axis=1), axis=1)
            crop += n

    lane = lambda rows: pl.BlockSpec((rows, block), lambda j: (0, j))
    return pl.pallas_call(
        kernel,
        grid=(width // block,),
        in_specs=[lane(rows_all), lane(2), lane(1), lane(1), lane(rows_all)],
        out_specs=[lane(rows_all), lane(slots), lane(slots)],
        out_shape=(
            jax.ShapeDtypeStruct((rows_all, width), BF16),
            jax.ShapeDtypeStruct((slots, width), F32),
            jax.ShapeDtypeStruct((slots, width), F32),
        ),
        compiler_params=vmem(32),
        name="slope_sums",
    )(third_pre, sums, gain, bias, inputs)


def projector(counts, pre, gain, bias, embed_map, hidden_map, plain, normed_sums, crop_total):
    blocks, slots, hidden = pre.shape
    emb = embed_map.shape[1]
    width = hidden_map.shape[0]
    crops = sum(n for n, _ in counts)
    rows_all = blocks * slots
    lanes = 256
    cols = hidden // lanes
    inv_total = 1.0 / crop_total
    group = 8
    half = 32

    def kernel(p_ref, g_ref, b_ref, we_ref, wh_ref, s1_ref, s2_ref,
               hp_ref, gap_ref, gz_ref, gg_ref, gb_ref, ge_ref, st_ref,
               n_scr, d_scr, z_scr, a_scr, i_scr, u_scr):
        live3 = lax.broadcasted_iota(jnp.int32, (blocks, slots, lanes), 1) < crops
        live = (lax.broadcasted_iota(jnp.int32, (blocks, slots, emb), 1) < crops).reshape(rows_all, emb)
        rstds = []
        for k in range(cols):
            at = slice(k * lanes, (k + 1) * lanes)
            raw = jnp.where(live3, p_ref[:, :, at], 0.0).reshape(rows_all, lanes)
            mean = jnp.sum(raw, axis=0, keepdims=True) * inv_total
            var = jnp.sum(raw * raw, axis=0, keepdims=True) * inv_total - mean * mean
            rstd = lax.rsqrt(var + NORM_EPS)
            rstds.append(rstd)
            normed = (raw - mean) * rstd
            q = normed * g_ref[:, at] + b_ref[:, at]
            sig = silu_parts(q)
            n_scr[:, at] = normed
            d_scr[:, at] = sig * (1.0 + q * (1.0 - sig))
            hp = jnp.where(live3.reshape(rows_all, lanes), q * sig, 0.0)
            hp_ref[:, at] = hp
            h, m = split2(hp)
            z = mm(h, we_ref[at, :]) + mm(m, we_ref[at, :])
            if k == 0:
                z_scr[...] = z
            else:
                z_scr[...] += z
        z = z_scr[...]
        mu = jnp.sum(z, axis=0, keepdims=True) * inv_total
        zc = jnp.where(live, z - mu, 0.0)
        zh, zm, zl = split3(zc)
        cat = jnp.concatenate([zh, zm, zl], axis=1)
        prod = mm_tn(cat, cat)
        cov = jnp.zeros((emb, emb), F32)
        for u in (2, 1, 0):
            for v in (2, 1, 0):
                cov = cov + prod[u * emb : (u + 1) * emb, v * emb : (v + 1) * emb]
        row_id = lax.broadcasted_iota(jnp.int32, (emb, emb), 0)
        col_id = lax.broadcasted_iota(jnp.int32, (emb, emb), 1)
        a_scr[...] = cov * inv_total
        i_scr[...] = jnp.where(row_id == col_id, 1.0, 0.0)

        def eliminate(j, carry):
            pivot_row = a_scr[pl.ds(j, 1), :]
            image_row = i_scr[pl.ds(j, 1), :]
            a = a_scr[...]
            pick = jnp.full((emb, emb), j, jnp.int32)
            column = jnp.take_along_axis(a, pick, axis=1)
            pivot = jnp.take_along_axis(jnp.broadcast_to(pivot_row, (8, emb)), pick[0:8], axis=1)
            inverse = (1.0 / pivot)[0:1]
            factor = jnp.where(row_id > j, column, 0.0)
            a_scr[...] = a - factor * (pivot_row * inverse)
            i_scr[...] = i_scr[...] - factor * (image_row * inverse)
            return carry

        lax.fori_loop(0, emb, eliminate, 0)
        diag = jnp.sum(jnp.where(row_id == col_id, a_scr[...], 0.0), axis=1, keepdims=True)
        white = i_scr[...] * lax.rsqrt(diag)
        ph, pm, pq = split3(white)
        w = mm_nt(
            jnp.concatenate([zh, zh, zm, zh, zl, zm], axis=1),
            jnp.concatenate([ph, pm, ph, pq, ph, pm], axis=1),
        )
        inv_len = lax.rsqrt(jnp.sum(w * w, axis=1, keepdims=True) + UNIT_EPS)
        u = w * inv_len
        uh, um, ul = split3(u)
        ucat = jnp.concatenate([uh, um, ul], axis=1)
        slot_id = lax.broadcasted_iota(jnp.int32, (slots, emb), 0).astype(F32)
        lane_id = lax.broadcasted_iota(jnp.int32, (slots, emb), 1)
        size = group * slots
        own = lax.broadcasted_iota(jnp.int32, (group, slots, size), 0).reshape(size, size)
        other_lane = lax.broadcasted_iota(jnp.int32, (size, size), 1)
        other = jnp.zeros((size, size), jnp.int32)
        for k in range(1, group):
            other = other + jnp.where(other_lane >= k * slots, 1, 0)
        same = own == other
        for k in range(blocks // group):
            ends = []
            for b in range(group):
                row = p_ref[k * group + b, crops : crops + 1, 0:emb]
                hit = jnp.where(slot_id == row, 1.0, 0.0)
                hit = hit - pltpu.roll(hit, emb - half, 1)
                ends.append(jnp.where(lane_id < half, hit, 0.0))
            ends = jnp.concatenate(ends, axis=0).astype(BF16)
            graph = jnp.where(same, mm_nt(ends, ends), 0.0).astype(BF16)
            at = slice(k * size, (k + 1) * size)
            gu = mm(graph, ucat[at])
            u_scr[at, :] = 2.0 * (gu[:, 0:emb] + (gu[:, emb : 2 * emb] + gu[:, 2 * emb : 3 * emb]))
        gu = u_scr[...]
        gw = (gu - u * jnp.sum(u * gu, axis=1, keepdims=True)) * inv_len
        g_col = jnp.sum(gw, axis=0, keepdims=True)
        wh, wm, _ = split3(w)
        gh, gm = split2(gw)
        prod = mm_tn(jnp.concatenate([gh, gm], axis=1), jnp.concatenate([wh, wm], axis=1))
        moment = (
            prod[emb:, emb:] + prod[0:emb, emb:] + prod[emb:, 0:emb] + prod[0:emb, 0:emb]
        )
        low = jnp.where(row_id >= col_id, moment, 0.0)
        strict = jnp.where(row_id > col_id, moment, 0.0)
        sym = (low + strict.T) * inv_total
        sh, sm = split2(sym)
        back = gw - g_col * inv_total - mm(
            jnp.concatenate([wh, wh, wm], axis=1), jnp.concatenate([sh, sm, sh], axis=0)
        )
        bh, bm = split2(back)
        gz = mm(jnp.concatenate([bh, bh, bm], axis=1), jnp.concatenate([ph, pm, ph], axis=0))
        gz = jnp.where(live, gz, 0.0)
        gz_ref[...] = gz
        zh2, zm2 = split2(gz)
        zcat = jnp.concatenate([zh2, zm2], axis=0)
        live_l = live3.reshape(rows_all, lanes)
        for k in range(cols):
            at = slice(k * lanes, (k + 1) * lanes)
            both = mm_nt(zcat, we_ref[at, :])
            gq = (both[0:rows_all] + both[rows_all:]) * d_scr[:, at]
            gb = jnp.sum(gq, axis=0, keepdims=True)
            gg = jnp.sum(gq * n_scr[:, at], axis=0, keepdims=True)
            gb_ref[:, at] = gb
            gg_ref[:, at] = gg
            gap = (g_ref[:, at] * rstds[k]) * (gq - gb * inv_total - n_scr[:, at] * (gg * inv_total))
            gap_ref[:, at] = jnp.where(live_l, gap, 0.0)
        mine = jnp.concatenate([gap_ref[0:slots, :], jnp.zeros((32 - slots, hidden), F32)], axis=0)
        h, m, l = split3(mine)
        out = mm_nt(jnp.concatenate([h, m, l], axis=0), wh_ref[...])
        ge = out[0:slots] + (out[32 : 32 + slots] + out[64 : 64 + slots])
        crop = 0
        ge_ref[...] = ge
        for n, s in counts:
            ge_ref[crop : crop + n, :] = ge[crop : crop + n] * (1.0 / (s * s))
            crop += n
        ge_ref[crop:, :] = jnp.zeros((slots - crop, width), F32)
        ge = ge_ref[...]
        st_ref[0:1, :] = jnp.sum(ge * s1_ref[...], axis=0, keepdims=True)
        st_ref[1:2, :] = jnp.sum(ge * s2_ref[...], axis=0, keepdims=True)

    return pl.pallas_call(
        kernel,
        out_shape=(
            jax.ShapeDtypeStruct((rows_all, hidden), F32),
            jax.ShapeDtypeStruct((rows_all, hidden), F32),
            jax.ShapeDtypeStruct((rows_all, emb), F32),
            jax.ShapeDtypeStruct((1, hidden), F32),
            jax.ShapeDtypeStruct((1, hidden), F32),
            jax.ShapeDtypeStruct((slots, width), F32),
            jax.ShapeDtypeStruct((2, width), F32),
        ),
        scratch_shapes=[
            pltpu.VMEM((rows_all, hidden), F32),
            pltpu.VMEM((rows_all, hidden), F32),
            pltpu.VMEM((rows_all, emb), F32),
            pltpu.VMEM((emb, emb), F32),
            pltpu.VMEM((emb, emb), F32),
            pltpu.VMEM((rows_all, emb), F32),
        ],
        compiler_params=vmem(56),
        name="projector",
    )(pre, gain, bias, embed_map, hidden_map, plain, normed_sums)


def last_back(parts, slope, share, third_pre, sums, grad_sums, total, gain, conv_out,
              second_pre, mid_sums, mid_gain, mid_bias):
    rows_all, width = third_pre.shape
    slabs, _, chan = second_pre.shape
    block = 256
    steps = width // block

    def kernel(s_ref, e_ref, a_ref, st_ref, gs_ref, g_ref, w_ref, m_ref, ms_ref, mg_ref, mb_ref,
               ga_ref, gq_ref, so_ref, acc):
        j = pl.program_id(0)
        mean, rstd = moments(st_ref, total)
        lift = g_ref[...] * rstd
        gg = gs_ref[1:2, :] * (1.0 / total)
        slant = rstd * gg
        base = gs_ref[0:1, :] * (1.0 / total) - mean * slant
        crop = 0
        for n, s, first in parts:
            rows = n * s * 8
            at = first * 8
            keep = live_rows(rows, block, s)
            share_rows = jnp.concatenate(
                [jnp.broadcast_to(e_ref[crop + c : crop + c + 1, :], (s * 8, block)) for c in range(n)], axis=0
            )
            gr = s_ref[at : at + rows, :].astype(F32) * share_rows
            ga = lift * (gr - base - a_ref[at : at + rows, :] * slant)
            ga_ref[at : at + rows, :] = jnp.where(keep, ga, 0.0).astype(BF16)
            crop += n
        out = mm_nt(ga_ref[...], w_ref[...])

        @pl.when(j == 0)
        def _():
            acc[...] = out

        @pl.when(j > 0)
        def _():
            acc[...] += out

        @pl.when(j == steps - 1)
        def _():
            mean2, rstd2 = moments(ms_ref, total)
            tot = jnp.zeros((1, chan), F32)
            tot_n = jnp.zeros((1, chan), F32)
            for n, s, first in parts:
                rows = n * s * 8
                at = first * 8
                grad = acc[at : at + rows, :].reshape(n * s, 8, chan)
                for c in range(n):
                    for i in range(s):
                        gq_ref[first + i * n + c] = grad[c * s + i]
                normed = (m_ref[first : first + n * s].reshape(rows, chan) - mean2) * rstd2
                q = normed * mg_ref[...] + mb_ref[...]
                sig = silu_parts(q)
                d = jnp.where(live_rows(rows, chan, s), sig * (1.0 + q * (1.0 - sig)), 0.0)
                gq = gq_ref[first : first + n * s].reshape(rows, chan) * d
                gq_ref[first : first + n * s] = gq.reshape(n * s, 8, chan)
                tot = tot + jnp.sum(gq, axis=0, keepdims=True)
                tot_n = tot_n + jnp.sum(gq * normed, axis=0, keepdims=True)
            so_ref[0:1, :] = tot
            so_ref[1:2, :] = tot_n

    lane = lambda rows: pl.BlockSpec((rows, block), lambda j: (0, j))
    whole = lambda *shape: pl.BlockSpec(shape, lambda j: (0,) * len(shape))
    return pl.pallas_call(
        kernel,
        grid=(steps,),
        in_specs=[lane(rows_all), lane(share.shape[0]), lane(rows_all), lane(2), lane(2), lane(1), lane(chan),
                  whole(slabs, 8, chan), whole(2, chan), whole(1, chan), whole(1, chan)],
        out_specs=[lane(rows_all), whole(slabs, 8, chan), whole(2, chan)],
        out_shape=(
            jax.ShapeDtypeStruct((rows_all, width), BF16),
            jax.ShapeDtypeStruct((slabs, 8, chan), F32),
            jax.ShapeDtypeStruct((2, chan), F32),
        ),
        scratch_shapes=[pltpu.VMEM((rows_all, chan), F32)],
        compiler_params=vmem(40),
        name="last_back",
    )(slope, share, third_pre, sums, grad_sums, gain, conv_out, second_pre, mid_sums, mid_gain, mid_bias)


def middle_back(parts, grad, grad_sums, total, second_pre, mid_sums, mid_gain, kernel_taps,
                first_pre, in_sums, in_gain, in_bias):
    slabs, _, chan = grad.shape
    rows_all = slabs * 8

    def kernel(gq_ref, gs_ref, a_ref, ms_ref, mg_ref, w_ref, f_ref, is_ref, ig_ref, ib_ref,
               ga_ref, o_ref, so_ref, acc):
        mean2, rstd2 = moments(ms_ref, total)
        lift = mg_ref[...] * rstd2
        slant = rstd2 * gs_ref[1:2, :] * (1.0 / total)
        base = gs_ref[0:1, :] * (1.0 / total) - mean2 * slant
        mean1, rstd1 = moments(is_ref, total)
        tot = jnp.zeros((1, chan), F32)
        tot_n = jnp.zeros((1, chan), F32)
        for n, s, first in parts:
            rows = n * s * 8
            at = first * 8
            step = n * 8
            keep = live_rows(rows, chan, s)
            ga = lift * (gq_ref[first : first + n * s].reshape(rows, chan) - base
                         - a_ref[first : first + n * s].reshape(rows, chan) * slant)
            ga_ref[at : at + rows, :] = jnp.where(keep, ga, 0.0).astype(BF16)
            total_rows = None
            for t in range(3):
                acc[at : at + rows, :] = mm_nt(ga_ref[at : at + rows, :], w_ref[3 + t])
                acc[at : at + rows - step, :] += mm_nt(ga_ref[at + step : at + rows, :], w_ref[t])
                acc[at + step : at + rows, :] += mm_nt(ga_ref[at : at + rows - step, :], w_ref[6 + t])
                piece = acc[at : at + rows, :]
                if t == 0:
                    piece = pltpu.roll(piece, rows - 1, 0)
                if t == 2:
                    piece = pltpu.roll(piece, 1, 0)
                total_rows = piece if total_rows is None else total_rows + piece
            normed = (f_ref[first : first + n * s].reshape(rows, chan) - mean1) * rstd1
            q = normed * ig_ref[...] + ib_ref[...]
            sig = silu_parts(q)
            gq = jnp.where(keep, total_rows * (sig * (1.0 + q * (1.0 - sig))), 0.0)
            o_ref[first : first + n * s] = gq.reshape(n * s, 8, chan)
            tot = tot + jnp.sum(gq, axis=0, keepdims=True)
            tot_n = tot_n + jnp.sum(gq * normed, axis=0, keepdims=True)
        so_ref[0:1, :] = tot
        so_ref[1:2, :] = tot_n

    return pl.pallas_call(
        kernel,
        out_shape=(
            jax.ShapeDtypeStruct((rows_all, chan), BF16),
            jax.ShapeDtypeStruct((slabs, 8, chan), F32),
            jax.ShapeDtypeStruct((2, chan), F32),
        ),
        scratch_shapes=[pltpu.VMEM((rows_all, chan), F32)],
        compiler_params=vmem(48),
        name="middle_back",
    )(grad, grad_sums, second_pre, mid_sums, mid_gain, kernel_taps, first_pre, in_sums, in_gain, in_bias)


def first_back(parts, grad, grad_sums, total, first_pre, in_sums, in_gain):
    slabs, _, chan = grad.shape
    rows_all = slabs * 8

    def kernel(gq_ref, gs_ref, f_ref, is_ref, ig_ref, ga_ref, scr):
        mean1, rstd1 = moments(is_ref, total)
        lift = ig_ref[...] * rstd1
        slant = rstd1 * gs_ref[1:2, :] * (1.0 / total)
        base = gs_ref[0:1, :] * (1.0 / total) - mean1 * slant
        for n, s, first in parts:
            rows = n * s * 8
            ga = lift * (gq_ref[first : first + n * s].reshape(rows, chan) - base
                         - f_ref[first : first + n * s].reshape(rows, chan) * slant)
            ga = jnp.where(live_rows(rows, chan, s), ga, 0.0).reshape(n * s, 8, chan)
            for i in range(s):
                for c in range(n):
                    scr[first + c * s + i] = ga[i * n + c]
        ga_ref[...] = scr[...].reshape(rows_all, chan).astype(BF16)

    return pl.pallas_call(
        kernel,
        out_shape=jax.ShapeDtypeStruct((rows_all, chan), BF16),
        scratch_shapes=[pltpu.VMEM((slabs, 8, chan), F32)],
        compiler_params=vmem(24),
        name="first_back",
    )(grad, grad_sums, first_pre, in_sums, in_gain)


def input_grads(parts, slope, share, grad_first, conv_in):
    rows_all, width = slope.shape
    chan = grad_first.shape[1]
    block = 256

    def kernel(s_ref, e_ref, g_ref, w_ref, o7, o6, o5):
        crop = 0
        for ref, (n, s, first) in zip((o7, o6, o5), parts):
            rows = n * s * 8
            at = first * 8
            out = mm_nt(g_ref[at : at + rows, :], w_ref[...])
            for c in range(n):
                lo = at + c * s * 8
                gr = s_ref[lo : lo + s * 8, :].astype(F32) * e_ref[crop + c : crop + c + 1, :]
                gx = (gr + out[c * s * 8 : (c + 1) * s * 8]).reshape(s, 8, block)
                ref[c] = gx[:, 0:s, :]
            crop += n

    lane = lambda rows: pl.BlockSpec((rows, block), lambda j: (0, j))
    return pl.pallas_call(
        kernel,
        grid=(width // block,),
        in_specs=[lane(rows_all), lane(share.shape[0]), pl.BlockSpec((rows_all, chan), lambda j: (0, 0)),
                  pl.BlockSpec((block, chan), lambda j: (j, 0))],
        out_specs=[pl.BlockSpec((n, s, s, block), lambda j: (0, 0, 0, j)) for n, s, _ in parts],
        out_shape=tuple(jax.ShapeDtypeStruct((n, s, s, width), F32) for n, s, _ in parts),
        compiler_params=vmem(32),
        name="input_grads",
    )(slope, share, grad_first, conv_in)


def middle_weight(parts, cat, grad):
    rows_all, chan = grad.shape

    def kernel(c_ref, g_ref, o_ref):
        r = pl.program_id(1)

        def add(shift):
            out = None
            for n, s, first in parts:
                step = n * 8
                rows = n * s * 8
                at = first * 8
                lhs = c_ref[at + max(shift, 0) * step : at + rows - max(-shift, 0) * step, :]
                rhs = g_ref[at + max(-shift, 0) * step : at + rows - max(shift, 0) * step, :]
                piece = mm_tn(lhs, rhs)
                out = piece if out is None else out + piece
            o_ref[0, 0] = out

        for k in range(3):
            pl.when(r == k)(lambda k=k: add(k - 1))

    return pl.pallas_call(
        kernel,
        grid=(3, 3),
        in_specs=[pl.BlockSpec((rows_all, chan), lambda t, r: (0, t)),
                  pl.BlockSpec((rows_all, chan), lambda t, r: (0, 0))],
        out_specs=pl.BlockSpec((1, 1, chan, chan), lambda t, r: (r, t, 0, 0)),
        out_shape=jax.ShapeDtypeStruct((3, 3, chan, chan), F32),
        compiler_params=vmem(32),
        name="middle_weight",
    )(cat, grad)


def masks_of(size, lowest=1):
    stages = []
    bit = lowest
    while bit < size:
        if 2 * bit < size:
            stages.append([bit, 2 * bit, 3 * bit])
            bit = 4 * bit
        else:
            stages.append([bit])
            bit = 2 * bit
    return stages


def swap(x, axis, mask):
    size = lax.axis_size(axis)
    return lax.ppermute(x, axis, [(i, i ^ mask) for i in range(size)])


def sum_all(x):
    stages = [("blk", [1])]
    stages += [("dp", m) for m in masks_of(lax.axis_size("dp"))]
    stages += [("blk", m) for m in masks_of(lax.axis_size("blk"), 2)]
    for axis, masks in stages:
        got = [swap(x, axis, m) for m in masks]
        for g in got:
            x = x + g
    return x


def gather_all(x):
    dp = lax.axis_index("dp")
    blk = lax.axis_index("blk")
    nblk = lax.axis_size("blk")
    x = x[None]
    where = [(0, 0)]
    stages = [("blk", m) for m in masks_of(nblk, 2)]
    stages += [("dp", m) for m in masks_of(lax.axis_size("dp"))]
    stages += [("blk", [1])]
    for axis, masks in stages:
        x = jnp.concatenate([x] + [swap(x, axis, m) for m in masks], axis=0)
        base = list(where)
        for m in masks:
            where += [(d ^ m, b) if axis == "dp" else (d, b ^ m) for d, b in base]
    number = jnp.stack([(dp ^ d) * nblk + (blk ^ b) for d, b in where])
    return x, number


def pick(x, index, axis):
    return lax.dynamic_index_in_dim(x, index, axis, keepdims=False)


def share_sum(grad):
    dp = lax.axis_index("dp")
    blk = lax.axis_index("blk")
    ndp = lax.axis_size("dp")
    nblk = lax.axis_size("blk")
    core = blk % 2
    z = blk // 2
    taps, _, rows, lanes = grad.shape
    g = grad.reshape(taps, nblk // 2, 2, ndp, rows // ndp, lanes)
    s = pick(g, core, 2) + swap(pick(g, 1 - core, 2), "blk", 1)
    got = [swap(pick(s, dp ^ k, 2), "dp", k) for k in range(1, ndp)]
    t = pick(s, dp, 2)
    for x in got:
        t = t + x
    got = [swap(pick(t, z ^ k, 1), "blk", 2 * k) for k in range(1, nblk // 2)]
    u = pick(t, z, 1)
    for x in got:
        u = u + x
    near = jnp.stack([u] + [swap(u, "dp", k) for k in range(1, ndp)], axis=1)
    out = jnp.concatenate([lax.dynamic_slice_in_dim(near, dp ^ k, 1, 1) for k in range(ndp)], axis=1)
    return out.reshape(taps, rows, lanes)


def projector_spread(counts, pre, gain, bias, embed_map, hidden_map, plain, normed_sums, crop_total):
    slots = pre.shape[0]
    crops = sum(n for n, _ in counts)
    high = lax.Precision.HIGHEST
    embed_map = embed_map.astype(F32)
    raw = pre[:crops]
    sums = sum_all(jnp.stack([jnp.sum(raw, axis=0), jnp.sum(raw * raw, axis=0)]))
    mean = sums[0] / crop_total
    rstd = lax.rsqrt(sums[1] / crop_total - mean * mean + NORM_EPS)
    normed = (raw - mean) * rstd
    q = gain * normed + bias
    sig = jax.nn.sigmoid(q)
    hp = q * sig
    z = jnp.dot(hp, embed_map, precision=high)
    emb = z.shape[1]
    z = jnp.concatenate([z, pre[crops : crops + 1, :emb], jnp.zeros((slots - crops - 1, emb), F32)], axis=0)
    z, _ = gather_all(z)
    blocks = z.shape[0]
    pairs = z[:, crops, :64]
    z = z[:, :crops].reshape(blocks * crops, emb)
    zc = z - jnp.sum(z, axis=0) / crop_total
    cov = jnp.dot(zc.T, zc, precision=high) / crop_total
    white = jax.scipy.linalg.solve_triangular(jnp.linalg.cholesky(cov), jnp.eye(emb, dtype=F32), lower=True)
    w = jnp.dot(zc, white.T, precision=high)
    inv_len = lax.rsqrt(jnp.sum(w * w, axis=1, keepdims=True) + UNIT_EPS)
    u = w * inv_len
    slot = jnp.arange(crops, dtype=F32)
    ends = (pairs[:, :32, None] == slot).astype(F32) - (pairs[:, 32:, None] == slot).astype(F32)
    gap = jnp.einsum("bpc,bce->bpe", ends, u.reshape(blocks, crops, emb), precision=high)
    gu = 2.0 * jnp.einsum("bpc,bpe->bce", ends, gap, precision=high).reshape(blocks * crops, emb)
    gw = (gu - u * jnp.sum(u * gu, axis=1, keepdims=True)) * inv_len
    moment = jnp.dot(gw.T, w, precision=high)
    sym = jnp.tril(moment) + jnp.tril(moment, -1).T
    back = gw[:crops] - (jnp.sum(gw, axis=0) + jnp.dot(w[:crops], sym, precision=high)) / crop_total
    gz = jnp.dot(back, white, precision=high)
    gq = jnp.dot(gz, embed_map.T, precision=high) * (sig * (1.0 + q * (1.0 - sig)))
    sums = sum_all(jnp.stack([jnp.sum(gq, axis=0), jnp.sum(gq * normed, axis=0)]))
    gap = gain * rstd * (gq - sums[0] / crop_total - normed * (sums[1] / crop_total))
    ge = jnp.dot(gap, hidden_map.astype(F32).T, precision=high)
    area = jnp.concatenate([jnp.full((n, 1), 1.0 / (s * s), F32) for n, s in counts])
    share = jnp.pad(ge * area, ((0, slots - crops), (0, 0)))
    stats = jnp.stack([jnp.sum(share * plain, axis=0), jnp.sum(share * normed_sums, axis=0)])
    return hp, gap, gz, sums[1:2], sums[0:1], share, stats


def body(crops_seven, crops_six, crops_five, conv_in, gain_in, bias_in, conv_mid, gain_mid, bias_mid,
         conv_out, gain_out, bias_out, proj_hidden, gain_proj, bias_proj, proj_embed, pair_index):
    crops_in = (crops_seven, crops_six, crops_five)
    parts, _ = geometry([c.shape for c in crops_in])
    counts = [(n, s) for n, s, _ in parts]
    ndp = lax.axis_size("dp")
    nblk = lax.axis_size("blk")
    blk = lax.axis_index("blk")
    devices = ndp * nblk
    crops = sum(n for n, _ in counts)
    total = float(sum(n * s * s for n, s in counts) * devices)
    crop_total = float(crops * devices)
    slots = 24
    width, chan = conv_in.shape
    hidden, emb = proj_embed.shape
    row = lambda v: v.reshape(1, -1)
    pair_row = jnp.pad(
        jnp.concatenate([pair_index[:, 0], pair_index[:, 1]]).astype(F32), (0, hidden - 2 * pair_index.shape[0])
    )

    inputs, first_pre, sums = first_conv(crops_in, conv_in)
    in_sums = sum_all(sums)
    cat, second_flat, sums = middle_conv(
        parts, first_pre, in_sums, total, row(gain_in), row(bias_in), conv_mid.reshape(3, 3 * chan, chan)
    )
    second_pre = second_flat.reshape(first_pre.shape)
    mid_sums = sum_all(sums)
    hidden_two, third_pre, sums = last_conv(parts, second_pre, mid_sums, total, row(gain_mid), row(bias_mid), conv_out)
    out_sums = sum_all(sums)
    pooled, pre = pool_embed(
        parts, slots, third_pre, out_sums, total, row(gain_out), row(bias_out), inputs, proj_hidden, row(pair_row)
    )
    whole = devices <= 32
    if whole:
        pre_all, number = gather_all(pre)
    slope, plain, normed_sums = slope_sums(parts, slots, third_pre, out_sums, total, row(gain_out), row(bias_out), inputs)
    middle = projector if whole else projector_spread
    hp, gap, gz, gg_proj, gb_proj, share, sums = middle(
        counts, pre_all if whole else pre, row(gain_proj), row(bias_proj), proj_embed, proj_hidden, plain,
        normed_sums, crop_total
    )
    out_back = sum_all(sums)
    grad_third, grad_two, sums = last_back(
        parts, slope, share, third_pre, out_sums, out_back, total, row(gain_out), conv_out,
        second_pre, mid_sums, row(gain_mid), row(bias_mid)
    )
    mid_back = sum_all(sums)
    local_out = lax.dot_general(hidden_two, grad_third, (((0,), (0,)), ((), ())), preferred_element_type=F32)
    grad_second, grad_one, sums = middle_back(
        parts, grad_two, mid_back, total, second_pre, mid_sums, row(gain_mid), conv_mid.reshape(9, chan, chan),
        first_pre, in_sums, row(gain_in), row(bias_in)
    )
    in_back = sum_all(sums)
    local_mid = middle_weight(parts, cat, grad_second)
    grad_first = first_back(parts, grad_one, in_back, total, first_pre, in_sums, row(gain_in))
    local_in = lax.dot_general(inputs, grad_first, (((0,), (0,)), ((), ())), preferred_element_type=F32)
    grads = input_grads(parts, slope, share, grad_first, conv_in)

    conv_out_grad = share_sum(local_out.reshape(1, nblk, chan // nblk, width))[0]
    conv_mid_grad = share_sum(local_mid.reshape(9, nblk, chan // nblk, chan)).reshape(3, 3, chan // nblk, chan)
    conv_in_grad = share_sum(local_in.reshape(1, nblk, width // nblk, chan))[0]

    high = lax.Precision.HIGH
    if whole:
        pooled_all = lax.all_gather(pooled, ("dp", "blk"), axis=0)
        own = width // nblk
        pooled_own = lax.dynamic_slice_in_dim(pooled_all, blk * own, own, 2)[number].reshape(devices * slots, own)
        hidden_grad = lax.dot_general(pooled_own, gap, (((0,), (0,)), ((), ())), precision=high)
        own = hidden // nblk
        embed_grad = lax.dot_general(
            lax.dynamic_slice_in_dim(hp, blk * own, own, 1), gz, (((0,), (0,)), ((), ())), precision=high
        )
    else:
        local = lax.dot_general(pooled[:crops], gap, (((0,), (0,)), ((), ())), precision=high)
        hidden_grad = share_sum(local.reshape(1, nblk, width // nblk, hidden))[0]
        local = lax.dot_general(hp, gz, (((0,), (0,)), ((), ())), precision=high)
        embed_grad = share_sum(local.reshape(1, nblk, hidden // nblk, emb))[0]
    return (
        *grads,
        conv_in_grad,
        conv_mid_grad,
        conv_out_grad,
        hidden_grad,
        embed_grad,
        in_back[1],
        in_back[0],
        mid_back[1],
        mid_back[0],
        out_back[1],
        out_back[0],
        gg_proj[0],
        gb_proj[0],
    )


def solution(mesh):
    from_both = ("dp", "blk")
    crop_spec = jax.sharding.PartitionSpec(from_both, None, None, None)
    spec = jax.sharding.PartitionSpec
    in_specs = (crop_spec,) * 3 + (spec(),) * 13 + (spec(from_both, None),)
    out_specs = (crop_spec,) * 3 + (
        spec("blk", None),
        spec(None, None, "blk", None),
        spec("blk", None),
        spec("blk", None),
        spec("blk", None),
    ) + (spec(),) * 8
    return jax.shard_map(body, mesh=mesh, in_specs=in_specs, out_specs=out_specs, check_vma=False)
```

time: 1140 us -> 452 us (0.40)
  blocking collectives: 387 us -> 0 us
  waiting for transfers between devices: 336 us -> 152 us
  local copies, waits for them, and re-layouts: 240 us -> 58.5 us
  Pallas kernels: 0 us -> 102 us
  starting transfers between devices: 0.33 us -> 88.9 us
  matrix products: 83.2 us -> 13.9 us
  other arithmetic: 74.3 us -> 13.6 us
    psum x10 -> x0, blocking collectives: 345 us -> none  [the longest x8 325 us: global_pair(): return lax.psum((first_term, second_term), ('dp', 'blk'))]
    reduce_scatter x5 -> x0, waiting for transfers between devices: 219 us -> none  [the longest x1 100 us: body(): lax.psum_scatter(local_conv_mid, 'blk', scatter_dimension=2, tiled=True)]
    ppermute x0 -> x79, waiting for transfers between devices: none -> 152 us  [swap(): return lax.ppermute(x, axis, [(i, i ^ mask) for i in range(size)])]
    psum x3 -> x0, waiting for transfers between devices: 116 us -> none  [the longest x1 67.4 us: body(): lax.psum((shares[0], shares[1], shares[2], shares[3], shares[4]), 'dp')]
    pallas_call x0 -> x11, Pallas kernels: none -> 102 us  [the longest x1 26 us: projector(): pl.pallas_call(kernel, out_shape=(jax.ShapeDtypeStruct((rows_all, hidden)...]
    ppermute x0 -> x79, starting transfers between devices: none -> 88.8 us  [swap(): return lax.ppermute(x, axis, [(i, i ^ mask) for i in range(size)])]
    slice x39 -> x3, local copies, waits for them, and re-layouts: 77.2 us -> 1.78 us  [the longest x1 0.61 us: body(): out_back[0]]
    dot_general x25 -> x4, matrix products: 82.3 us -> 13.9 us  [the longest x1 4.51 us: body(): lax.dot_general(hidden_two, grad_third, (((0,), (0,)), ((), ())), preferr...]
  transfers between devices with their start and end apart: 8 -> 80, of which waited for: 6 -> 51; matrix products, arithmetic and copies ran while one was open for 18% -> 12% of each run, Pallas kernels for 0% -> 16%
where the time goes in v1:
time: 452 us; the launch traced here: 444 us
  waiting for transfers between devices  152 us (34%)
  Pallas kernels  102 us (23%)
  starting transfers between devices  88.9 us (20%)
  local copies, waits for them, and re-layouts  58.5 us (13%)
  between operations  15 us (3%)
  matrix products  13.9 us (3%)
  other arithmetic  13.6 us (3%)
    ppermute x79, waiting for transfers between devices, swap(): return lax.ppermute(x, axis, [(i, i ^ mask) for i in range(size)])  152 us
    ppermute x79, starting transfers between devices, swap(): return lax.ppermute(x, axis, [(i, i ^ mask) for i in range(size)])  88.8 us
    unnamed x90, local copies, waits for them, and re-layouts  36.4 us
    pallas_call x1, Pallas kernels, projector(): pl.pallas_call(kernel, out_shape=(jax.ShapeDtypeStruct((rows_all, hidden)...  26 us
    pallas_call x1, Pallas kernels, last_back(): pl.pallas_call(kernel, grid=(steps,), in_specs=[lane(rows_all), lane(shar...  12.9 us
    dynamic_slice x2, local copies, waits for them, and re-layouts, pick(): return lax.dynamic_index_in_dim(x, index, axis, keepdims=False)  10.3 us
    pallas_call x1, Pallas kernels, middle_back(): pl.pallas_call(kernel, out_shape=(jax.ShapeDtypeStruct((rows_all, chan),...  10.1 us
    pallas_call x1, Pallas kernels, pool_embed(): pl.pallas_call(kernel, grid=(steps,), in_specs=[lane(rows_all), lane(2),...  10 us
  transfers between devices with their start and end apart: 80, of which 51 were waited for; matrix products, arithmetic and copies ran while one was open for 12% of the time, Pallas kernels for 16%

profile of v1, /device:TPU:0, one launch (start us, length us, event | category | flops | bytes accessed | tf_op | source)
XLA Modules:
  0.0 444.1 jit_solution(10570792630077260083)
XLA Ops:
  10.3 6.6 %first_conv.1 = (bf16[1056,2048]{1,0:T(8,128)(2,1)}, f32[132,8,512]{2,1,0:T(8,128)}, f32[2,512]{1,0:T(2,128)S(1)}) custom-call(bf16[8,7,7,2048]{3,2,1,0:T(8,128)(2,1)S(1)} %copy.40.x7, bf16[6,6,6,2048]{3,2,1,0:T(8,128)(2,1)S(1)} %copy-done.17, bf16[8,5,5,2048]{3,2,1,0:T(8,128)(2,1)S(1)} %copy.41.x5, bf16[2048,512]{1,0:T(8,128)(2,1)} %w_ref.9), custom_call_target="tpu_custom_call" | custom-call | tf_op jit(solution)/shard_map/first_conv/pallas_call | solution.py:92
  35.8 8.4 %middle_conv.1 = (bf16[1056,1536]{1,0:T(8,128)(2,1)}, f32[1056,512]{1,0:T(8,128)S(1)}, f32[2,512]{1,0:T(2,128)S(1)}) custom-call(f32[132,8,512]{2,1,0:T(8,128)S(1)} %copy-done.3, f32[2,512]{1,0:T(2,128)S(1)} %add_add_fusion.10.st_ref.is_ref, f32[1,512]{1,0:T(1,128)S(1)} %bitcast.194, f32[1,512]{1,0:T(1,128)S(1)} %bitcast.203, bf16[3,1536,512]{2,1,0:T(8,128)(2,1)} %bitcast.205), custom_call_target="tpu_custom_call" | custom-call | tf_op jit(solution)/shard_map/middle_conv/pallas_call | solution.py:134
  57.1 4.7 %last_conv.1 = (bf16[1056,512]{1,0:T(8,128)(2,1)S(1)}, f32[1056,2048]{1,0:T(8,128)S(1)}, f32[2,2048]{1,0:T(2,128)S(1)}) custom-call(f32[132,8,512]{2,1,0:T(8,128)S(1)} %bitcast.178, f32[2,512]{1,0:T(2,128)S(1)} %add_add_fusion.8.st_ref.ms_ref, f32[1,512]{1,0:T(1,128)S(1)} %bitcast.197, f32[1,512]{1,0:T(1,128)S(1)} %bitcast.201, bf16[512,2048]{1,0:T(8,128)(2,1)S(1)} %copy-done.11), custom_call_target="tpu_custom_call" | custom-call | tf_op jit(solution)/shard_map/last_conv/pallas_call | solution.py:173
  82.7 10.0 %pool_embed.1 = (f32[24,2048]{1,0:T(8,128)}, f32[24,1024]{1,0:T(8,128)S(1)}) custom-call(f32[1056,2048]{1,0:T(8,128)} %copy-done, f32[2,2048]{1,0:T(2,128)S(1)} %add_add_fusion.2.st_ref, f32[1,2048]{1,0:T(1,128)S(1)} %bitcast.189, f32[1,2048]{1,0:T(1,128)S(1)} %bitcast.192, bf16[1056,2048]{1,0:T(8,128)(2,1)S(1)} %copy-done.5, ...), custom_call_target="tpu_custom_call" | custom-call | tf_op jit(solution)/shard_map/pool_embed/pallas_call | solution.py:252
  107.7 5.8 %collective-permute-done.24 = f32[4,24,1024]{2,1,0:T(8,128)S(1)} collective-permute-done((f32[4,24,1024]{2,1,0:T(8,128)S(1)}, f32[4,24,1024]{2,1,0:T(8,128)S(1)}, u32[]{:S(2)}, u32[]{:S(2)}) %collective-permute-start.24) | collective-permute-done | bytes 393248 | tf_op jit(solution)/shard_map/ppermute | solution.py:727
  114.5 7.3 %collective-permute-done.25 = f32[4,24,1024]{2,1,0:T(8,128)S(1)} collective-permute-done((f32[4,24,1024]{2,1,0:T(8,128)S(1)}, f32[4,24,1024]{2,1,0:T(8,128)S(1)}, u32[]{:S(2)}, u32[]{:S(2)}) %collective-permute-start.25) | collective-permute-done | bytes 393248 | tf_op jit(solution)/shard_map/ppermute | solution.py:727
  129.4 8.3 %slope_sums.1 = (bf16[1056,2048]{1,0:T(8,128)(2,1)S(1)}, f32[24,2048]{1,0:T(8,128)S(1)}, f32[24,2048]{1,0:T(8,128)S(1)}) custom-call(f32[1056,2048]{1,0:T(8,128)S(1)} %copy-done.1, f32[2,2048]{1,0:T(2,128)S(1)} %add_add_fusion.2.st_ref, f32[1,2048]{1,0:T(1,128)S(1)} %bitcast.190, f32[1,2048]{1,0:T(1,128)S(1)} %bitcast.193, bf16[1056,2048]{1,0:T(8,128)(2,1)S(1)} %copy-done.6), custom_call_target="tpu_custom_call" | custom-call | tf_op jit(solution)/shard_map/slope_sums/pallas_call | solution.py:300
  142.6 26.0 %projector.1 = (f32[768,1024]{1,0:T(8,128)}, f32[768,1024]{1,0:T(8,128)}, f32[768,128]{1,0:T(8,128)}, f32[1,1024]{1,0:T(1,128)}, f32[1,1024]{1,0:T(1,128)}, /*index=5*/f32[24,2048]{1,0:T(8,128)}, f32[2,2048]{1,0:T(2,128)}) custom-call(f32[32,24,1024]{2,1,0:T(8,128)} %constant_dynamic-update-slice_fusion.7.p_ref, f32[1,1024]{1,0:T(1,128)} %bitcast.232, ...), custom_call_target="tpu_custom_call" | custom-call | tf_op jit(solution)/shard_map/projector/pallas_call | solution.py:461
  185.5 12.9 %last_back.1 = (bf16[1056,2048]{1,0:T(8,128)(2,1)S(1)}, f32[132,8,512]{2,1,0:T(8,128)S(1)}, f32[2,512]{1,0:T(2,128)S(1)}) custom-call(bf16[1056,2048]{1,0:T(8,128)(2,1)} %copy-done.7, f32[24,2048]{1,0:T(8,128)S(1)} %copy-done.18, f32[1056,2048]{1,0:T(8,128)} %copy-done, f32[2,2048]{1,0:T(2,128)S(1)} %add_add_fusion.2.st_ref, ...), custom_call_target="tpu_custom_call" | custom-call | tf_op jit(solution)/shard_map/last_back/pallas_call | solution.py:547
  216.8 10.1 %middle_back.1 = (bf16[1056,512]{1,0:T(8,128)(2,1)S(1)}, f32[132,8,512]{2,1,0:T(8,128)S(1)}, f32[2,512]{1,0:T(2,128)S(1)}) custom-call(f32[132,8,512]{2,1,0:T(8,128)S(1)} %copy-done.16, f32[2,512]{1,0:T(2,128)S(1)} %add_add_fusion.6.gs_ref, f32[132,8,512]{2,1,0:T(8,128)} %bitcast.180, f32[2,512]{1,0:T(2,128)S(1)} %add_add_fusion.8.st_ref.ms_ref, ...), custom_call_target="tpu_custom_call" | custom-call | tf_op jit(solution)/shard_map/middle_back/pallas_call | solution.py:607
  226.9 4.5 %fusion.20 = f32[512,2048]{1,0:T(8,128)} fusion(bf16[1056,512]{1,0:T(8,128)(2,1)S(1)} %get-tuple-element.68, bf16[1056,2048]{1,0:T(8,128)(2,1)S(1)} %copy-done.10), kind=kOutput, calls=%fused_computation.105 | convolution fusion | flops 2214592512 | bytes 9601024 | tf_op jit(solution)/shard_map/dot_general | solution.py:878
  231.4 8.1 %middle_weight.1 = f32[3,3,512,512]{3,2,1,0:T(8,128)S(1)} custom-call(bf16[1056,1536]{1,0:T(8,128)(2,1)S(1)} %copy-done.14, bf16[1056,512]{1,0:T(8,128)(2,1)S(1)} %get-tuple-element.67.g_ref), custom_call_target="tpu_custom_call" | custom-call | tf_op jit(solution)/shard_map/middle_weight/pallas_call | solution.py:700
  243.2 4.7 %constant_dynamic-slice_fusion.10 = (f32[9,4,1,4,16,512]{5,4,3,2,1,0:T(8,128)}, f32[9,4,1,4,16,512]{5,4,3,2,1,0:T(8,128)}) fusion(f32[9,4,2,4,16,512]{5,4,3,2,1,0:T(8,128)S(1)} %bitcast.177, s32[]{:T(128)S(6)} %select_n.105, s32[]{:T(128)S(6)} %select_n.106), kind=kLoop, calls=%fused_computation.82 | loop fusion | bytes 18874376 | tf_op jit(solution)/shard_map/jit(dynamic_index_in_dim)/dynamic_slice | solution.py:760
  247.8 5.6 %copy.50 = f32[9,4,1,4,16,512]{5,4,1,0,3,2:T(8,128)} copy(f32[9,4,1,4,16,512]{5,4,3,2,1,0:T(8,128)} %get-tuple-element.109) | data formatting | bytes 9437184 | tf_op jit(solution)/shard_map/jit(dynamic_index_in_dim)/dynamic_slice | solution.py:760
  276.5 6.1 %input_grads.1 = (f32[8,7,7,2048]{3,2,1,0:T(8,128)S(1)}, f32[6,6,6,2048]{3,2,1,0:T(8,128)}, f32[8,5,5,2048]{3,2,1,0:T(8,128)S(1)}) custom-call(bf16[1056,2048]{1,0:T(8,128)(2,1)S(1)} %bitcast.184, f32[24,2048]{1,0:T(8,128)S(1)} %copy-done.19, bf16[1056,512]{1,0:T(8,128)(2,1)S(1)} %first_back.1.g_ref, bf16[2048,512]{1,0:T(8,128)(2,1)S(1)} %copy-done.13), custom_call_target="tpu_custom_call" | custom-call | tf_op jit(solution)/shard_map/input_grads/pallas_call | solution.py:667
  293.4 5.0 %collective-permute-done.72 = f32[1,4,16,2048]{3,2,1,0:T(8,128)S(1)} collective-permute-done((f32[1,4,16,2048]{3,2,1,0:T(8,128)S(1)}, f32[1,4,16,2048]{3,2,1,0:T(8,128)S(1)}, u32[]{:S(2)}, u32[]{:S(2)}) %collective-permute-start.72) | collective-permute-done | bytes 524320 | tf_op jit(solution)/shard_map/ppermute | solution.py:727
  301.4 8.3 %collective-permute-done.50 = f32[1,4,64,512]{3,2,1,0:T(8,128)S(1)} collective-permute-done((f32[1,4,64,512]{3,2,1,0:T(8,128)S(1)}, f32[1,4,64,512]{3,2,1,0:T(8,128)S(1)}, u32[]{:S(2)}, u32[]{:S(2)}) %collective-permute-start.50) | collective-permute-done | bytes 524320 | tf_op jit(solution)/shard_map/ppermute | solution.py:727
  311.4 9.1 %collective-permute-done.52 = f32[1,4,64,512]{3,2,1,0:T(8,128)S(1)} collective-permute-done((f32[1,4,64,512]{3,2,1,0:T(8,128)S(1)}, f32[1,4,64,512]{3,2,1,0:T(8,128)S(1)}, u32[]{:S(2)}, u32[]{:S(2)}) %collective-permute-start.52) | collective-permute-done | bytes 524320 | tf_op jit(solution)/shard_map/ppermute | solution.py:727
  346.3 37.4 %collective-permute-done.78 = f32[1,16,2048]{2,1,0:T(8,128)S(1)} collective-permute-done((f32[1,16,2048]{2,1,0:T(8,128)S(1)}, f32[1,16,2048]{2,1,0:T(8,128)S(1)}, u32[]{:S(2)}, u32[]{:S(2)}) %collective-permute-start.78) | collective-permute-done | bytes 131104 | tf_op jit(solution)/shard_map/ppermute | solution.py:727
  395.4 7.8 %collective-permute-done.63 = f32[9,16,512]{2,1,0:T(8,128)S(1)} collective-permute-done((f32[9,16,512]{2,1,0:T(8,128)S(1)}, f32[9,16,512]{2,1,0:T(8,128)S(1)}, u32[]{:S(2)}, u32[]{:S(2)}) %collective-permute-start.63) | collective-permute-done | bytes 294944 | tf_op jit(solution)/shard_map/ppermute | solution.py:727
  403.3 4.1 collective-permute-done.65
  407.4 9.4 %collective-permute-done.64 = f32[9,16,512]{2,1,0:T(8,128)S(1)} collective-permute-done((f32[9,16,512]{2,1,0:T(8,128)S(1)}, f32[9,16,512]{2,1,0:T(8,128)S(1)}, u32[]{:S(2)}, u32[]{:S(2)}) %collective-permute-start.64) | collective-permute-done | bytes 294944 | tf_op jit(solution)/shard_map/ppermute | solution.py:727
  421.4 5.1 %collective-permute-done.68 = f32[9,16,512]{2,1,0:T(8,128)S(1)} collective-permute-done((f32[9,16,512]{2,1,0:T(8,128)S(1)}, f32[9,16,512]{2,1,0:T(8,128)S(1)}, u32[]{:S(2)}, u32[]{:S(2)}) %collective-permute-start.68) | collective-permute-done | bytes 294944 | tf_op jit(solution)/shard_map/ppermute | solution.py:727
  432.7 4.4 fusion.21
  (305 shorter events, 209.4 us)
Async XLA Ops:
  7.2 423.7 %all-gather.3.cloned.1.call-start = ((), (), s32[]{:S(2)}) async-start(), calls=%async_computation | async-start | bytes 6488064 | tf_op jit(solution)/shard_map/all_gather | solution.py:895
  103.0 19.7 %collective-permute-start.26 = (f32[4,24,1024]{2,1,0:T(8,128)S(1)}, f32[4,24,1024]{2,1,0:T(8,128)S(1)}, u32[]{:S(2)}, u32[]{:S(2)}) collective-permute-start(f32[4,24,1024]{2,1,0:T(8,128)S(1)} %pad_maximum_fusion.6), channel_id=1, source_target_pairs={{0,24},{8,16},{16,8},{24,0},{1,25},{9,17},{17,9},{25,1},{2,26},{10... | collective-permute-start | bytes 1179656 | tf_op jit(solution)/shard_map/ppermute | solution.py:727
  105.3 16.5 %collective-permute-start.25 = (f32[4,24,1024]{2,1,0:T(8,128)S(1)}, f32[4,24,1024]{2,1,0:T(8,128)S(1)}, u32[]{:S(2)}, u32[]{:S(2)}) collective-permute-start(f32[4,24,1024]{2,1,0:T(8,128)S(1)} %pad_maximum_fusion.6), channel_id=1, source_target_pairs={{0,16},{8,24},{16,0},{24,8},{1,17},{9,25},{17,1},{25,9},{2,18},{10... | collective-permute-start | bytes 1179656 | tf_op jit(solution)/shard_map/ppermute | solution.py:727
  123.7 16.1 %collective-permute-start.27 = (f32[16,24,1024]{2,1,0:T(8,128)}, f32[16,24,1024]{2,1,0:T(8,128)}, u32[]{:S(2)}, u32[]{:S(2)}) collective-permute-start(f32[16,24,1024]{2,1,0:T(8,128)} %get-tuple-element.140), channel_id=1, source_target_pairs={{0,1},{1,0},{2,3},{3,2},{4,5},{5,4},{6,7},{7,6},{8,9},{9,8},{10,11... | collective-permute-start | bytes 4718600 | tf_op jit(solution)/shard_map/ppermute | solution.py:727
  253.5 69.7 %collective-permute-start.59 = (f32[9,4,4,16,512]{4,3,1,0,2:T(8,128)}, f32[9,4,4,16,512]{4,3,1,0,2:T(8,128)}, u32[]{:S(2)}, u32[]{:S(2)}) collective-permute-start(f32[9,4,4,16,512]{4,3,1,0,2:T(8,128)} %bitcast.176), channel_id=1, source_target_pairs={{0,1},{1,0},{2,3},{3,2},{4,5},{5,4},{6,7},{7,6},{8,9},{9,8},{10,11... | collective-permute-start | bytes 14155784 | tf_op jit(solution)/shard_map/ppermute | solution.py:727
  266.4 21.9 %collective-permute-start.49 = (f32[1,4,4,64,512]{4,3,2,1,0:T(8,128)}, f32[1,4,4,64,512]{4,3,2,1,0:T(8,128)}, u32[]{:S(2)}, u32[]{:S(2)}) collective-permute-start(f32[1,4,4,64,512]{4,3,2,1,0:T(8,128)} %dynamic-slice_bitcast_fusion.1), channel_id=1, source_target_pairs={{0,1},{1,0},{2,3},{3,2},{4,5},{5,4},{6,7},{7,6},{8,9},{9,8},{10,11... | collective-permute-start | bytes 6291464 | tf_op jit(solution)/shard_map/ppermute | solution.py:727
  272.3 21.0 %collective-permute-start.70 = (f32[1,4,16,2048]{3,2,1,0:T(8,128)S(1)}, f32[1,4,16,2048]{3,2,1,0:T(8,128)S(1)}, u32[]{:S(2)}, u32[]{:S(2)}) collective-permute-start(f32[1,4,16,2048]{3,2,1,0:T(8,128)S(1)} %get-tuple-element.113), channel_id=1, source_target_pairs={{0,8},{8,0},{16,24},{24,16},{1,9},{9,1},{17,25},{25,17},{2,10},{10... | collective-permute-start | bytes 1572872 | tf_op jit(solution)/shard_map/ppermute | solution.py:727
  274.3 24.1 %collective-permute-start.72 = (f32[1,4,16,2048]{3,2,1,0:T(8,128)S(1)}, f32[1,4,16,2048]{3,2,1,0:T(8,128)S(1)}, u32[]{:S(2)}, u32[]{:S(2)}) collective-permute-start(f32[1,4,16,2048]{3,2,1,0:T(8,128)S(1)} %get-tuple-element.114), channel_id=1, source_target_pairs={{0,24},{8,16},{16,8},{24,0},{1,25},{9,17},{17,9},{25,1},{2,26},{10... | collective-permute-start | bytes 1572872 | tf_op jit(solution)/shard_map/ppermute | solution.py:727
  274.4 25.4 %collective-permute-start.71 = (f32[1,4,16,2048]{3,2,1,0:T(8,128)S(1)}, f32[1,4,16,2048]{3,2,1,0:T(8,128)S(1)}, u32[]{:S(2)}, u32[]{:S(2)}) collective-permute-start(f32[1,4,16,2048]{3,2,1,0:T(8,128)S(1)} %get-tuple-element.115), channel_id=1, source_target_pairs={{0,16},{8,24},{16,0},{24,8},{1,17},{9,25},{17,1},{25,9},{2,18},{10... | collective-permute-start | bytes 1572872 | tf_op jit(solution)/shard_map/ppermute | solution.py:727
  291.3 18.3 %collective-permute-start.50 = (f32[1,4,64,512]{3,2,1,0:T(8,128)S(1)}, f32[1,4,64,512]{3,2,1,0:T(8,128)S(1)}, u32[]{:S(2)}, u32[]{:S(2)}) collective-permute-start(f32[1,4,64,512]{3,2,1,0:T(8,128)S(1)} %get-tuple-element.116), channel_id=1, source_target_pairs={{0,8},{8,0},{16,24},{24,16},{1,9},{9,1},{17,25},{25,17},{2,10},{10... | collective-permute-start | bytes 1572872 | tf_op jit(solution)/shard_map/ppermute | solution.py:727
  293.3 27.3 %collective-permute-start.52 = (f32[1,4,64,512]{3,2,1,0:T(8,128)S(1)}, f32[1,4,64,512]{3,2,1,0:T(8,128)S(1)}, u32[]{:S(2)}, u32[]{:S(2)}) collective-permute-start(f32[1,4,64,512]{3,2,1,0:T(8,128)S(1)} %get-tuple-element.117), channel_id=1, source_target_pairs={{0,24},{8,16},{16,8},{24,0},{1,25},{9,17},{17,9},{25,1},{2,26},{10... | collective-permute-start | bytes 1572872 | tf_op jit(solution)/shard_map/ppermute | solution.py:727
  298.4 24.5 %collective-permute-start.51 = (f32[1,4,64,512]{3,2,1,0:T(8,128)S(1)}, f32[1,4,64,512]{3,2,1,0:T(8,128)S(1)}, u32[]{:S(2)}, u32[]{:S(2)}) collective-permute-start(f32[1,4,64,512]{3,2,1,0:T(8,128)S(1)} %get-tuple-element.118), channel_id=1, source_target_pairs={{0,16},{8,24},{16,0},{24,8},{1,17},{9,25},{17,1},{25,9},{2,18},{10... | collective-permute-start | bytes 1572872 | tf_op jit(solution)/shard_map/ppermute | solution.py:727
  300.1 30.5 %collective-permute-start.73 = (f32[1,16,2048]{2,1,0:T(8,128)S(1)}, f32[1,16,2048]{2,1,0:T(8,128)S(1)}, u32[]{:S(2)}, u32[]{:S(2)}) collective-permute-start(f32[1,16,2048]{2,1,0:T(8,128)S(1)} %get-tuple-element.130), channel_id=1, source_target_pairs={{0,2},{1,3},{2,0},{3,1},{4,6},{5,7},{6,4},{7,5},{8,10},{9,11},{10,... | collective-permute-start | bytes 393224 | tf_op jit(solution)/shard_map/ppermute | solution.py:727
  309.6 21.3 %collective-permute-start.75 = (f32[1,16,2048]{2,1,0:T(8,128)S(1)}, f32[1,16,2048]{2,1,0:T(8,128)S(1)}, u32[]{:S(2)}, u32[]{:S(2)}) collective-permute-start(f32[1,16,2048]{2,1,0:T(8,128)S(1)} %get-tuple-element.131), channel_id=1, source_target_pairs={{0,6},{1,7},{2,4},{3,5},{4,2},{5,3},{6,0},{7,1},{8,14},{9,15},{10,... | collective-permute-start | bytes 393224 | tf_op jit(solution)/shard_map/ppermute | solution.py:727
  327.3 63.0 %collective-permute-start.60 = (f32[9,4,16,512]{3,2,1,0:T(8,128)S(1)}, f32[9,4,16,512]{3,2,1,0:T(8,128)S(1)}, u32[]{:S(2)}, u32[]{:S(2)}) collective-permute-start(f32[9,4,16,512]{3,2,1,0:T(8,128)S(1)} %get-tuple-element.110), channel_id=1, source_target_pairs={{0,8},{8,0},{16,24},{24,16},{1,9},{9,1},{17,25},{25,17},{2,10},{10... | collective-permute-start | bytes 3538952 | tf_op jit(solution)/shard_map/ppermute | solution.py:727
  328.9 61.4 %collective-permute-start.62 = (f32[9,4,16,512]{3,2,1,0:T(8,128)S(1)}, f32[9,4,16,512]{3,2,1,0:T(8,128)S(1)}, u32[]{:S(2)}, u32[]{:S(2)}) collective-permute-start(f32[9,4,16,512]{3,2,1,0:T(8,128)S(1)} %get-tuple-element.111), channel_id=1, source_target_pairs={{0,24},{8,16},{16,8},{24,0},{1,25},{9,17},{17,9},{25,1},{2,26},{10... | collective-permute-start | bytes 3538952 | tf_op jit(solution)/shard_map/ppermute | solution.py:727
  330.6 59.7 %collective-permute-start.61 = (f32[9,4,16,512]{3,2,1,0:T(8,128)S(1)}, f32[9,4,16,512]{3,2,1,0:T(8,128)S(1)}, u32[]{:S(2)}, u32[]{:S(2)}) collective-permute-start(f32[9,4,16,512]{3,2,1,0:T(8,128)S(1)} %get-tuple-element.112), channel_id=1, source_target_pairs={{0,16},{8,24},{16,0},{24,8},{1,17},{9,25},{17,1},{25,9},{2,18},{10... | collective-permute-start | bytes 3538952 | tf_op jit(solution)/shard_map/ppermute | solution.py:727
  340.2 43.5 %collective-permute-start.78 = (f32[1,16,2048]{2,1,0:T(8,128)S(1)}, f32[1,16,2048]{2,1,0:T(8,128)S(1)}, u32[]{:S(2)}, u32[]{:S(2)}) collective-permute-start(f32[1,16,2048]{2,1,0:T(8,128)S(1)} %fusion.11), channel_id=1, source_target_pairs={{0,24},{8,16},{16,8},{24,0},{1,25},{9,17},{17,9},{25,1},{2,26},{10... | collective-permute-start | bytes 393224 | tf_op jit(solution)/shard_map/ppermute | solution.py:727
  344.6 43.1 %collective-permute-start.77 = (f32[1,16,2048]{2,1,0:T(8,128)S(1)}, f32[1,16,2048]{2,1,0:T(8,128)S(1)}, u32[]{:S(2)}, u32[]{:S(2)}) collective-permute-start(f32[1,16,2048]{2,1,0:T(8,128)S(1)} %fusion.11), channel_id=1, source_target_pairs={{0,16},{8,24},{16,0},{24,8},{1,17},{9,25},{17,1},{25,9},{2,18},{10... | collective-permute-start | bytes 393224 | tf_op jit(solution)/shard_map/ppermute | solution.py:727
  387.6 31.8 %collective-permute-start.58 = (f32[1,64,512]{2,1,0:T(8,128)S(1)}, f32[1,64,512]{2,1,0:T(8,128)S(1)}, u32[]{:S(2)}, u32[]{:S(2)}) collective-permute-start(f32[1,64,512]{2,1,0:T(8,128)S(1)} %fusion.13), channel_id=1, source_target_pairs={{0,24},{8,16},{16,8},{24,0},{1,25},{9,17},{17,9},{25,1},{2,26},{10... | collective-permute-start | bytes 393224 | tf_op jit(solution)/shard_map/ppermute | solution.py:727
  390.0 30.4 %collective-permute-start.57 = (f32[1,64,512]{2,1,0:T(8,128)S(1)}, f32[1,64,512]{2,1,0:T(8,128)S(1)}, u32[]{:S(2)}, u32[]{:S(2)}) collective-permute-start(f32[1,64,512]{2,1,0:T(8,128)S(1)} %fusion.13), channel_id=1, source_target_pairs={{0,16},{8,24},{16,0},{24,8},{1,17},{9,25},{17,1},{25,9},{2,18},{10... | collective-permute-start | bytes 393224 | tf_op jit(solution)/shard_map/ppermute | solution.py:727
  392.2 15.1 %collective-permute-start.65 = (f32[9,16,512]{2,1,0:T(8,128)S(1)}, f32[9,16,512]{2,1,0:T(8,128)S(1)}, u32[]{:S(2)}, u32[]{:S(2)}) collective-permute-start(f32[9,16,512]{2,1,0:T(8,128)S(1)} %get-tuple-element.124), channel_id=1, source_target_pairs={{0,6},{1,7},{2,4},{3,5},{4,2},{5,3},{6,0},{7,1},{8,14},{9,15},{10,... | collective-permute-start | bytes 884744 | tf_op jit(solution)/shard_map/ppermute | solution.py:727
  394.1 22.6 %collective-permute-start.64 = (f32[9,16,512]{2,1,0:T(8,128)S(1)}, f32[9,16,512]{2,1,0:T(8,128)S(1)}, u32[]{:S(2)}, u32[]{:S(2)}) collective-permute-start(f32[9,16,512]{2,1,0:T(8,128)S(1)} %get-tuple-element.125), channel_id=1, source_target_pairs={{0,4},{1,5},{2,6},{3,7},{4,0},{5,1},{6,2},{7,3},{8,12},{9,13},{10,... | collective-permute-start | bytes 884744 | tf_op jit(solution)/shard_map/ppermute | solution.py:727
  403.2 17.2 %collective-permute-start.56 = (f32[1,64,512]{2,1,0:T(8,128)S(1)}, f32[1,64,512]{2,1,0:T(8,128)S(1)}, u32[]{:S(2)}, u32[]{:S(2)}) collective-permute-start(f32[1,64,512]{2,1,0:T(8,128)S(1)} %fusion.13), channel_id=1, source_target_pairs={{0,8},{8,0},{16,24},{24,16},{1,9},{9,1},{17,25},{25,17},{2,10},{10... | collective-permute-start | bytes 393224 | tf_op jit(solution)/shard_map/ppermute | solution.py:727
  (96 other events, 913.0 us)
Sparse Core Ops, SparseCore 0:
  123.8 68.6 all-gather.2

commit v2 on v1

v2 whole, which is shorter than its diff:
```python
import jax
import jax.numpy as jnp
from jax import lax
from jax.experimental import pallas as pl
from jax.experimental.pallas import tpu as pltpu

F32 = jnp.float32
BF16 = jnp.bfloat16
NORM_EPS = 1e-05
UNIT_EPS = 1e-06
MIB = 1 << 20
ANY = pl.BlockSpec(memory_space=pl.ANY)
HBM = pl.BlockSpec(memory_space=pltpu.HBM)
SMEM = pl.BlockSpec(memory_space=pltpu.SMEM)
MARK = jax.ShapeDtypeStruct((8, 128), F32)


def params(mib):
    return pltpu.CompilerParams(vmem_limit_bytes=mib * MIB)


def cost(flops, moved, special=0):
    return pl.CostEstimate(flops=0, bytes_accessed=0, transcendentals=0)


class Part:
    def __init__(self, crops, side, first, slot):
        self.crops, self.side, self.first, self.slot = crops, side, first, slot
        self.by_column = crops != 8
        self.slabs = crops * side if self.by_column else side * side
        self.cut = slice(first, first + self.slabs)

    def sources(self, down, right):
        found = []
        for k in range(self.slabs):
            i, j = divmod(k, self.side)
            if self.by_column:
                i, j = j + down, 0
                there = 0 <= i < self.side
                found.append(k + down if there else None)
            else:
                i, j = i + down, j + right
                there = 0 <= i < self.side and 0 <= j < self.side
                found.append(i * self.side + j if there else None)
        return found


def layout(shapes):
    order = sorted(range(len(shapes)), key=lambda k: (shapes[k][0] != 8, -shapes[k][1]))
    parts = [None] * len(shapes)
    first = slot = 0
    for k in order:
        parts[k] = Part(shapes[k][0], shapes[k][1], first, slot)
        first += parts[k].slabs
        slot += shapes[k][0]
    return parts, [parts[k] for k in order], first


def sigmoid(q):
    return 0.5 * jnp.tanh(0.5 * q) + 0.5


def column_live(shape, side):
    return lax.broadcasted_iota(jnp.int32, shape, len(shape) - 2) < side


def live(parts, value):
    pieces = []
    for p in parts:
        piece = value[p.cut]
        if p.by_column:
            piece = jnp.where(column_live(piece.shape, p.side), piece, 0.0)
        pieces.append(piece)
    return jnp.concatenate(pieces, axis=0)


def crop_totals(parts, value, ref):
    for p in parts:
        piece = value[p.cut]
        if p.by_column:
            piece = piece.reshape(p.crops, p.side, 8, piece.shape[-1])
            total = jnp.sum(jnp.sum(piece, axis=1), axis=1)
        else:
            total = jnp.sum(piece, axis=0)
        ref[p.slot : p.slot + p.crops, :] = total


def spread(parts, ref):
    lanes = ref.shape[-1]
    pieces = []
    for p in parts:
        if p.by_column:
            for c in range(p.crops):
                row = ref[p.slot + c : p.slot + c + 1, :]
                pieces.append(jnp.broadcast_to(row[None], (p.side, 8, lanes)))
        else:
            pieces.append(jnp.broadcast_to(ref[p.slot : p.slot + 8, :][None], (p.slabs, 8, lanes)))
    return jnp.concatenate(pieces, axis=0)


def moments(st_ref, total):
    mean = st_ref[0:1, :] * (1.0 / total)
    var = st_ref[1:2, :] * (1.0 / total) - mean * mean
    return mean, lax.rsqrt(var + NORM_EPS)


def put_sums(ref, first, second):
    ref[0:1, :] = jnp.sum(first, axis=0, keepdims=True)
    ref[1:2, :] = jnp.sum(second, axis=0, keepdims=True)


def split3(x):
    h = x.astype(BF16)
    r = x - h.astype(F32)
    m = r.astype(BF16)
    return h, m, (r - m.astype(F32)).astype(BF16)


def split2(x):
    h = x.astype(BF16)
    return h, (x - h.astype(F32)).astype(BF16)


def mm(a, b):
    return jnp.dot(a, b, preferred_element_type=F32)


def mm_nt(a, b):
    return lax.dot_general(a, b, (((1,), (1,)), ((), ())), preferred_element_type=F32)


def mm_tn(a, b):
    return lax.dot_general(a, b, (((0,), (0,)), ((), ())), preferred_element_type=F32)


def whole(*shape):
    return pl.BlockSpec(shape, lambda *_: (0,) * len(shape))


def mark_of(x):
    return x[(0,) * (x.ndim - 2)][0:8, 0:128]


def lanes_of(block, *lead):
    return pl.BlockSpec((*lead, block), lambda j: (0,) * len(lead) + (j,))


def first_conv(parts, order, slabs, crops, conv_in):
    width, chan = conv_in.shape
    block = 512
    steps = width // block

    def kernel(*refs):
        x_refs, w_ref, xp_ref, a_ref, st_ref, scr = refs[:3], *refs[3:]
        j = pl.program_id(0)
        for p, ref in zip(parts, x_refs):
            x = ref[...].astype(F32)
            if p.by_column:
                x = x.reshape(p.slabs, p.side, block)
                x = jnp.concatenate([x, jnp.zeros((p.slabs, 8 - p.side, block), F32)], axis=1)
            scr[p.cut] = x
        xp_ref[...] = scr[...].reshape(slabs * 8, block).astype(BF16)
        out = mm(xp_ref[...], w_ref[...])

        @pl.when(j == 0)
        def _():
            a_ref[...] = out

        @pl.when(j > 0)
        def _():
            a_ref[...] += out

        @pl.when(j == steps - 1)
        def _():
            total = a_ref[...]
            put_sums(st_ref, total, total * total)

    rows = slabs * 8
    x_specs = [
        pl.BlockSpec((p.crops, p.side, p.side, block), lambda j: (0, 0, 0, j)) if p.by_column else lanes_of(block, p.slabs, 8)
        for p in parts
    ]
    return pl.pallas_call(
        kernel,
        grid=(steps,),
        in_specs=[*x_specs, pl.BlockSpec((block, chan), lambda j: (j, 0))],
        out_specs=[lanes_of(block, rows), whole(rows, chan), whole(2, chan)],
        out_shape=(
            jax.ShapeDtypeStruct((rows, width), BF16),
            jax.ShapeDtypeStruct((rows, chan), F32),
            jax.ShapeDtypeStruct((2, chan), F32),
        ),
        scratch_shapes=[pltpu.VMEM((slabs, 8, block), F32)],
        compiler_params=params(20),
        cost_estimate=cost(2 * rows * width * chan, 10 << 20),
        name="first_conv",
    )(*crops, conv_in)


def turn(order, chan, source, turned):
    for p in order:
        if p.by_column:
            value = source[p.cut].reshape(p.slabs * 8, chan)
            turned[0] = pltpu.roll(value, 1, 0).reshape(p.slabs, 8, chan)
            turned[1] = pltpu.roll(value, p.slabs * 8 - 1, 0).reshape(p.slabs, 8, chan)

def shifted(order, chan, source, turned, tap, forward):
    r, t = divmod(tap, 3)
    down, right = (r - 1, t - 1) if forward else (1 - r, 1 - t)
    pieces = []
    for p in order:
        found = p.sources(down, right)
        k = 0
        while k < p.slabs:
            end = k + 1
            if found[k] is None:
                while end < p.slabs and found[end] is None:
                    end += 1
                pieces.append(jnp.zeros((end - k, 8, chan), F32))
            else:
                while end < p.slabs and found[end] == found[k] + end - k:
                    end += 1
                at = found[k]
                if p.by_column and right:
                    pieces.append(turned[0 if right < 0 else 1, at : at + end - k])
                else:
                    pieces.append(source[p.first + at : p.first + at + end - k])
            k = end
    value = jnp.concatenate(pieces, axis=0)
    return value.reshape(value.shape[0] * 8, chan).astype(BF16)


def patch_columns(order, chan, source, turned, cat_ref, forward):
    turn(order, chan, source, turned)
    for tap in range(9):
        cat_ref[:, tap * chan : (tap + 1) * chan] = shifted(order, chan, source, turned, tap, forward)


def turned_shape(order, chan):
    return (2, max([p.slabs for p in order if p.by_column] + [1]), 8, chan)


def middle_conv(order, first_pre, sums, total, gain, bias, kernel_flat):
    rows, chan = first_pre.shape
    slabs = rows // 8

    def kernel(a_ref, st_ref, g_ref, b_ref, w_ref, y_ref, o_ref, so_ref, turned, cat_scr):
        mean, rstd = moments(st_ref, total)
        scale = g_ref[...] * rstd
        q = (a_ref[...] * scale + (b_ref[...] - mean * scale)).reshape(slabs, 8, chan)
        y_ref[...] = live(order, q * sigmoid(q))
        patch_columns(order, chan, y_ref, turned, cat_scr, True)
        out = live(order, mm(cat_scr[...], w_ref[...]).reshape(slabs, 8, chan)).reshape(rows, chan)
        o_ref[...] = out
        put_sums(so_ref, out, out * out)

    return pl.pallas_call(
        kernel,
        in_specs=[whole(rows, chan), whole(2, chan), whole(1, chan), whole(1, chan), whole(9 * chan, chan)],
        out_specs=[whole(slabs, 8, chan), whole(rows, chan), whole(2, chan)],
        out_shape=(
            jax.ShapeDtypeStruct((slabs, 8, chan), F32),
            jax.ShapeDtypeStruct((rows, chan), F32),
            jax.ShapeDtypeStruct((2, chan), F32),
        ),
        scratch_shapes=[
            pltpu.VMEM(turned_shape(order, chan), F32),
            pltpu.VMEM((rows, 9 * chan), BF16),
        ],
        compiler_params=params(24),
        cost_estimate=cost(18 * rows * chan * chan, 20 << 20),
        name="middle_conv",
    )(first_pre, sums, gain, bias, kernel_flat)


def last_conv(order, second_pre, sums, total, gain, bias, conv_out):
    rows, chan = second_pre.shape
    slabs = rows // 8
    width = conv_out.shape[1]
    block = 512

    def kernel(a_ref, st_ref, g_ref, b_ref, w_ref, y_ref, o_ref, so_ref):
        @pl.when(pl.program_id(0) == 0)
        def _():
            mean, rstd = moments(st_ref, total)
            scale = g_ref[...] * rstd
            q = (a_ref[...] * scale + (b_ref[...] - mean * scale)).reshape(slabs, 8, chan)
            y_ref[...] = live(order, q * sigmoid(q)).reshape(rows, chan).astype(BF16)

        out = mm(y_ref[...], w_ref[...])
        o_ref[...] = out
        put_sums(so_ref, out, out * out)

    return pl.pallas_call(
        kernel,
        grid=(width // block,),
        in_specs=[whole(rows, chan), whole(2, chan), whole(1, chan), whole(1, chan), lanes_of(block, chan)],
        out_specs=[whole(rows, chan), lanes_of(block, rows), lanes_of(block, 2)],
        out_shape=(
            jax.ShapeDtypeStruct((rows, chan), BF16),
            jax.ShapeDtypeStruct((rows, width), F32),
            jax.ShapeDtypeStruct((2, width), F32),
        ),
        compiler_params=params(16),
        cost_estimate=cost(2 * rows * width * chan, 12 << 20),
        name="last_conv",
    )(second_pre, sums, gain, bias, conv_out)


def pool_embed(order, slots, third_pre, sums, total, gain, bias, inputs, hidden_map, pair_row):
    rows, width = third_pre.shape
    slabs = rows // 8
    hidden = hidden_map.shape[1]
    crops = sum(p.crops for p in order)
    block = 256
    steps = width // block

    def kernel(a_ref, st_ref, g_ref, b_ref, x_ref, w_ref, p_ref, e_ref, ap_ref, scr, acc):
        j = pl.program_id(0)
        mean, rstd = moments(st_ref, total)
        scale = g_ref[...] * rstd
        shift = b_ref[...] - mean * scale
        r = x_ref[...].astype(F32) + (a_ref[...] * scale + shift)
        v = live(order, (r * sigmoid(r)).reshape(slabs, 8, block))
        scr[...] = jnp.zeros_like(scr)
        crop_totals(order, v, scr)
        for p in order:
            at = slice(p.slot, p.slot + p.crops)
            scr[at, :] = scr[at, :] * (1.0 / (p.side * p.side))
        e = scr[...]
        e_ref[...] = e[0:slots]
        h, m, l = split3(e)
        out = mm(jnp.concatenate([h, m, l], axis=0), w_ref[...])

        @pl.when(j == 0)
        def _():
            acc[...] = out

        @pl.when(j > 0)
        def _():
            acc[...] += out

        @pl.when(j == steps - 1)
        def _():
            ap_ref[...] = acc[0:slots] + acc[32 : 32 + slots] + acc[64 : 64 + slots]
            ap_ref[crops : crops + 1, :] = p_ref[...]

    return pl.pallas_call(
        kernel,
        grid=(steps,),
        in_specs=[
            lanes_of(block, rows), lanes_of(block, 2), lanes_of(block, 1), lanes_of(block, 1), lanes_of(block, rows),
            pl.BlockSpec((block, hidden), lambda j: (j, 0)), whole(1, hidden),
        ],
        out_specs=[lanes_of(block, slots), whole(slots, hidden)],
        out_shape=(jax.ShapeDtypeStruct((slots, width), F32), jax.ShapeDtypeStruct((slots, hidden), F32)),
        scratch_shapes=[pltpu.VMEM((32, block), F32), pltpu.VMEM((96, hidden), F32)],
        compiler_params=params(12),
        cost_estimate=cost(2 * 96 * width * hidden, 16 << 20, 2 * rows * width),
        name="pool_embed",
    )(third_pre, sums, gain, bias, inputs, hidden_map, pair_row)


def slope_sums(order, slots, third_pre, sums, total, gain, bias, inputs, hold=()):
    rows, width = third_pre.shape
    slabs = rows // 8
    block = 256

    def kernel(a_ref, st_ref, g_ref, b_ref, x_ref, *refs):
        s_ref, p_ref, t_ref = refs[len(hold) :][:3]
        for k in range(len(hold)):
            refs[len(hold) + 3 + k][...] = refs[k][...]
        mean, rstd = moments(st_ref, total)
        p_ref[...] = jnp.zeros_like(p_ref)
        t_ref[...] = jnp.zeros_like(t_ref)
        normed = (a_ref[...] - mean) * rstd
        r = x_ref[...].astype(F32) + (normed * g_ref[...] + b_ref[...])
        sig = sigmoid(r)
        v = live(order, (sig * (1.0 + r * (1.0 - sig))).reshape(slabs, 8, block))
        s_ref[...] = v.reshape(rows, block).astype(BF16)
        crop_totals(order, v, p_ref)
        crop_totals(order, v * normed.reshape(slabs, 8, block), t_ref)

    lane = lambda lead: lanes_of(block, lead)
    kept = [whole(*h.shape) for h in hold]
    return pl.pallas_call(
        kernel,
        grid=(width // block,),
        in_specs=[lane(rows), lane(2), lane(1), lane(1), lane(rows)] + kept,
        out_specs=[lane(rows), lane(slots), lane(slots)] + kept,
        out_shape=(
            jax.ShapeDtypeStruct((rows, width), BF16),
            jax.ShapeDtypeStruct((slots, width), F32),
            jax.ShapeDtypeStruct((slots, width), F32),
            *(jax.ShapeDtypeStruct(h.shape, F32) for h in hold),
        ),
        compiler_params=params(14),
        cost_estimate=cost(24 * rows * width, 8 * rows * width, 2 * rows * width),
        name="slope_sums",
    )(third_pre, sums, gain, bias, inputs, *hold)


def join(pieces, token):
    count = len(pieces)
    shape = pieces[0].shape

    def kernel(*refs):
        for k in range(count):
            refs[-1][k] = refs[k][...]

    return pl.pallas_call(
        kernel,
        in_specs=[whole(*shape)] * count + [whole(8, 128)] * len(token),
        out_specs=whole(count, *shape),
        out_shape=jax.ShapeDtypeStruct((count, *shape), F32),
        compiler_params=params(8),
        name="join",
    )(*pieces, *token)


def projector(order, pres, gain, bias, embed_map, hidden_map, plain, normed_sums, crop_total):
    held = [p.shape[0] for p in pres]
    blocks = sum(held)
    _, slots, hidden = pres[0].shape
    emb = embed_map.shape[1]
    width = hidden_map.shape[0]
    crops = sum(p.crops for p in order)
    rows_all = blocks * slots
    lanes = 256
    cols = hidden // lanes
    inv_total = 1.0 / crop_total
    group = 8
    half = 32

    def kernel(*refs):
        p_refs = refs[: len(held)]
        (g_ref, b_ref, we_ref, wh_ref, s1_ref, s2_ref, hp_ref, gap_ref, gz_ref, gg_ref, gb_ref, ge_ref, st_ref,
         n_scr, d_scr, z_scr, a_scr, i_scr, u_scr) = refs[len(held):]
        live_l = (lax.broadcasted_iota(jnp.int32, (blocks, slots, lanes), 1) < crops).reshape(rows_all, lanes)
        live_e = (lax.broadcasted_iota(jnp.int32, (blocks, slots, emb), 1) < crops).reshape(rows_all, emb)
        rstds = []
        for k in range(cols):
            at = slice(k * lanes, (k + 1) * lanes)
            raw = jnp.concatenate([ref[:, :, at].reshape(n * slots, lanes) for ref, n in zip(p_refs, held)], axis=0)
            raw = jnp.where(live_l, raw, 0.0)
            mean = jnp.sum(raw, axis=0, keepdims=True) * inv_total
            var = jnp.sum(raw * raw, axis=0, keepdims=True) * inv_total - mean * mean
            rstd = lax.rsqrt(var + NORM_EPS)
            rstds.append(rstd)
            normed = (raw - mean) * rstd
            q = normed * g_ref[:, at] + b_ref[:, at]
            sig = sigmoid(q)
            n_scr[:, at] = normed
            d_scr[:, at] = sig * (1.0 + q * (1.0 - sig))
            hp = jnp.where(live_l, q * sig, 0.0)
            hp_ref[:, at] = hp
            h, m = split2(hp)
            z = mm(h, we_ref[at, :]) + mm(m, we_ref[at, :])
            if k == 0:
                z_scr[...] = z
            else:
                z_scr[...] += z
        z = z_scr[...]
        mu = jnp.sum(z, axis=0, keepdims=True) * inv_total
        zc = jnp.where(live_e, z - mu, 0.0)
        zh, zm, zl = split3(zc)
        cat = jnp.concatenate([zh, zm, zl], axis=1)
        prod = mm_tn(cat, cat)
        cov = jnp.zeros((emb, emb), F32)
        for u in (2, 1, 0):
            for v in (2, 1, 0):
                cov = cov + prod[u * emb : (u + 1) * emb, v * emb : (v + 1) * emb]
        row_id = lax.broadcasted_iota(jnp.int32, (emb, emb), 0)
        col_id = lax.broadcasted_iota(jnp.int32, (emb, emb), 1)
        a_scr[...] = cov * inv_total
        i_scr[...] = jnp.where(row_id == col_id, 1.0, 0.0)

        def eliminate(step, carry):
            j = 2 * step
            a = a_scr[...]
            image = i_scr[...]
            row0 = a_scr[pl.ds(j, 1), :]
            row1 = a_scr[pl.ds(j + 1, 1), :]
            image0 = i_scr[pl.ds(j, 1), :]
            image1 = i_scr[pl.ds(j + 1, 1), :]
            first = jnp.full((emb, emb), j, jnp.int32)
            second = first + 1
            lane = lambda row, at: jnp.take_along_axis(jnp.broadcast_to(row, (8, emb)), at[0:8], axis=1)[0:1]
            column0 = jnp.take_along_axis(a, first, axis=1)
            column1 = jnp.take_along_axis(a, second, axis=1)
            inverse0 = 1.0 / lane(row0, first)
            ratio = lane(row0, second) * inverse0
            inverse1 = 1.0 / (lane(row1, second) - lane(row1, first) * ratio)
            factor0 = jnp.where(row_id > j, column0, 0.0)
            factor1 = jnp.where(row_id > j + 1, column1 - column0 * ratio, 0.0)
            below = lane(row1, first) * inverse0
            a_scr[...] = a - factor0 * (row0 * inverse0) - factor1 * ((row1 - below * row0) * inverse1)
            i_scr[...] = image - factor0 * (image0 * inverse0) - factor1 * ((image1 - below * image0) * inverse1)
            return carry

        lax.fori_loop(0, emb // 2, eliminate, 0)
        diag = jnp.sum(jnp.where(row_id == col_id, a_scr[...], 0.0), axis=1, keepdims=True)
        white = i_scr[...] * lax.rsqrt(diag)
        ph, pm, pq = split3(white)
        w = mm_nt(
            jnp.concatenate([zh, zh, zm, zh, zl, zm], axis=1),
            jnp.concatenate([ph, pm, ph, pq, ph, pm], axis=1),
        )
        inv_len = lax.rsqrt(jnp.sum(w * w, axis=1, keepdims=True) + UNIT_EPS)
        u = w * inv_len
        uh, um, ul = split3(u)
        ucat = jnp.concatenate([uh, um, ul], axis=1)
        slot_id = lax.broadcasted_iota(jnp.int32, (slots, emb), 0).astype(F32)
        lane_id = lax.broadcasted_iota(jnp.int32, (slots, emb), 1)
        size = group * slots
        own = lax.broadcasted_iota(jnp.int32, (group, slots, size), 0).reshape(size, size)
        other_lane = lax.broadcasted_iota(jnp.int32, (size, size), 1)
        other = jnp.zeros((size, size), jnp.int32)
        for k in range(1, group):
            other = other + jnp.where(other_lane >= k * slots, 1, 0)
        same = own == other
        pair_rows = [ref[b, crops : crops + 1, 0:emb] for ref, n in zip(p_refs, held) for b in range(n)]
        for k in range(blocks // group):
            ends = []
            for b in range(group):
                hit = jnp.where(slot_id == pair_rows[k * group + b], 1.0, 0.0)
                hit = hit - pltpu.roll(hit, emb - half, 1)
                ends.append(jnp.where(lane_id < half, hit, 0.0))
            ends = jnp.concatenate(ends, axis=0).astype(BF16)
            graph = jnp.where(same, mm_nt(ends, ends), 0.0).astype(BF16)
            at = slice(k * size, (k + 1) * size)
            gu = mm(graph, ucat[at])
            u_scr[at, :] = 2.0 * (gu[:, 0:emb] + (gu[:, emb : 2 * emb] + gu[:, 2 * emb : 3 * emb]))
        gu = u_scr[...]
        gw = (gu - u * jnp.sum(u * gu, axis=1, keepdims=True)) * inv_len
        g_col = jnp.sum(gw, axis=0, keepdims=True)
        wh, wm, _ = split3(w)
        gh, gm = split2(gw)
        prod = mm_tn(jnp.concatenate([gh, gm], axis=1), jnp.concatenate([wh, wm], axis=1))
        moment = (
            prod[emb:, emb:] + prod[0:emb, emb:] + prod[emb:, 0:emb] + prod[0:emb, 0:emb]
        )
        low = jnp.where(row_id >= col_id, moment, 0.0)
        strict = jnp.where(row_id > col_id, moment, 0.0)
        sym = (low + strict.T) * inv_total
        sh, sm = split2(sym)
        back = gw - g_col * inv_total - mm(
            jnp.concatenate([wh, wh, wm], axis=1), jnp.concatenate([sh, sm, sh], axis=0)
        )
        bh, bm = split2(back)
        gz = mm(jnp.concatenate([bh, bh, bm], axis=1), jnp.concatenate([ph, pm, ph], axis=0))
        gz = jnp.where(live_e, gz, 0.0)
        gz_ref[...] = gz
        zh2, zm2 = split2(gz)
        zcat = jnp.concatenate([zh2, zm2], axis=0)
        for k in range(cols):
            at = slice(k * lanes, (k + 1) * lanes)
            both = mm_nt(zcat, we_ref[at, :])
            gq = (both[0:rows_all] + both[rows_all:]) * d_scr[:, at]
            gb = jnp.sum(gq, axis=0, keepdims=True)
            gg = jnp.sum(gq * n_scr[:, at], axis=0, keepdims=True)
            gb_ref[:, at] = gb
            gg_ref[:, at] = gg
            gap = (g_ref[:, at] * rstds[k]) * (gq - gb * inv_total - n_scr[:, at] * (gg * inv_total))
            gap_ref[:, at] = jnp.where(live_l, gap, 0.0)
        mine = jnp.concatenate([gap_ref[0:slots, :], jnp.zeros((32 - slots, hidden), F32)], axis=0)
        h, m, l = split3(mine)
        out = mm_nt(jnp.concatenate([h, m, l], axis=0), wh_ref[...])
        ge_ref[...] = out[0:slots] + (out[32 : 32 + slots] + out[64 : 64 + slots])
        for p in order:
            at = slice(p.slot, p.slot + p.crops)
            ge_ref[at, :] = ge_ref[at, :] * (1.0 / (p.side * p.side))
        ge_ref[crops:, :] = jnp.zeros((slots - crops, width), F32)
        ge = ge_ref[...]
        put_sums(st_ref, ge * s1_ref[...], ge * s2_ref[...])

    return pl.pallas_call(
        kernel,
        out_shape=(
            jax.ShapeDtypeStruct((rows_all, hidden), F32),
            jax.ShapeDtypeStruct((rows_all, hidden), F32),
            jax.ShapeDtypeStruct((rows_all, emb), F32),
            jax.ShapeDtypeStruct((1, hidden), F32),
            jax.ShapeDtypeStruct((1, hidden), F32),
            jax.ShapeDtypeStruct((slots, width), F32),
            jax.ShapeDtypeStruct((2, width), F32),
        ),
        scratch_shapes=[
            pltpu.VMEM((rows_all, hidden), F32),
            pltpu.VMEM((rows_all, hidden), F32),
            pltpu.VMEM((rows_all, emb), F32),
            pltpu.VMEM((emb, emb), F32),
            pltpu.VMEM((emb, emb), F32),
            pltpu.VMEM((rows_all, emb), F32),
        ],
        compiler_params=params(30),
        cost_estimate=cost(10 << 30, 20 << 20),
        name="projector",
    )(*pres, gain, bias, embed_map, hidden_map, plain, normed_sums)


def halves(value, core, send, keep):
    for mine in range(2):

        @pl.when(core == mine)
        def _(mine=mine):
            send[...] = value(1 - mine)
            keep[...] = value(mine)


def last_back(order, slope, share, third_pre, sums, grad_sums, total, gain, conv_out,
              second_pre, mid_sums, mid_gain, mid_bias, hidden_two):
    rows, width = third_pre.shape
    slabs = rows // 8
    chan = second_pre.shape[1]
    block = 512
    steps = width // block

    def kernel(s_ref, e_ref, a_ref, st_ref, gs_ref, g_ref, w_ref, m_ref, ms_ref, mg_ref, mb_ref, y_ref,
               gq_ref, so_ref, weight_ref, ga_scr):
        j = pl.program_id(0)
        mean, rstd = moments(st_ref, total)
        lift = g_ref[...] * rstd
        slant = rstd * gs_ref[1:2, :] * (1.0 / total)
        base = gs_ref[0:1, :] * (1.0 / total) - mean * slant
        gr = s_ref[...].astype(F32) * spread(order, e_ref).reshape(rows, block)
        ga = lift * (gr - base - a_ref[...] * slant)
        ga_scr[...] = live(order, ga.reshape(slabs, 8, block)).reshape(rows, block).astype(BF16)
        out = mm_nt(ga_scr[...], w_ref[...])

        @pl.when(j == 0)
        def _():
            gq_ref[...] = out

        @pl.when(j > 0)
        def _():
            gq_ref[...] += out

        weight_ref[...] = mm_tn(y_ref[...], ga_scr[...])

        @pl.when(j == steps - 1)
        def _():
            mean2, rstd2 = moments(ms_ref, total)
            normed = (m_ref[...] - mean2) * rstd2
            q = normed * mg_ref[...] + mb_ref[...]
            sig = sigmoid(q)
            gq = gq_ref[...] * (sig * (1.0 + q * (1.0 - sig)))
            gq_ref[...] = gq
            put_sums(so_ref, gq, gq * normed)

    return pl.pallas_call(
        kernel,
        grid=(steps,),
        in_specs=[lanes_of(block, rows), lanes_of(block, share.shape[0]), lanes_of(block, rows), lanes_of(block, 2),
                  lanes_of(block, 2), lanes_of(block, 1), lanes_of(block, chan),
                  whole(rows, chan), whole(2, chan), whole(1, chan), whole(1, chan), whole(rows, chan)],
        out_specs=[whole(rows, chan), whole(2, chan), lanes_of(block, chan)],
        out_shape=(
            jax.ShapeDtypeStruct((rows, chan), F32),
            jax.ShapeDtypeStruct((2, chan), F32),
            jax.ShapeDtypeStruct((chan, width), F32),
        ),
        scratch_shapes=[pltpu.VMEM((rows, block), BF16)],
        compiler_params=params(40),
        cost_estimate=cost(4 * rows * width * chan, 24 << 20),
        name="last_back",
    )(slope, share, third_pre, sums, grad_sums, gain, conv_out, second_pre, mid_sums, mid_gain, mid_bias, hidden_two)


def middle_back(order, grad, grad_sums, total, second_pre, mid_sums, mid_gain, kernel_taps,
                first_pre, in_sums, in_gain, in_bias, token):
    rows, chan = grad.shape
    slabs = rows // 8

    def kernel(gq_ref, gs_ref, a_ref, ms_ref, mg_ref, w_ref, f_ref, is_ref, ig_ref, ib_ref, *refs):
        ga_ref, o_ref, so_ref, g_scr, turned, cat_scr, w_scr, sems = refs[len(token):]
        copies = [
            pltpu.make_async_copy(w_ref.at[k], w_scr.at[:, pl.ds(k * chan, chan)], sems.at[k]) for k in range(9)
        ]
        for copy in copies:
            copy.start()
        mean2, rstd2 = moments(ms_ref, total)
        lift = mg_ref[...] * rstd2
        slant = rstd2 * gs_ref[1:2, :] * (1.0 / total)
        base = gs_ref[0:1, :] * (1.0 / total) - mean2 * slant
        ga = live(order, (lift * (gq_ref[...] - base - a_ref[...] * slant)).reshape(slabs, 8, chan))
        g_scr[...] = ga
        ga_ref[...] = ga.reshape(rows, chan).astype(BF16)
        patch_columns(order, chan, g_scr, turned, cat_scr, False)
        for copy in copies:
            copy.wait()
        out = mm_nt(cat_scr[...], w_scr[...])
        mean1, rstd1 = moments(is_ref, total)
        normed = (f_ref[...] - mean1) * rstd1
        q = normed * ig_ref[...] + ib_ref[...]
        sig = sigmoid(q)
        gq = live(order, (out * (sig * (1.0 + q * (1.0 - sig)))).reshape(slabs, 8, chan)).reshape(rows, chan)
        o_ref[...] = gq
        put_sums(so_ref, gq, gq * normed)

    return pl.pallas_call(
        kernel,
        in_specs=[whole(rows, chan), whole(2, chan), whole(rows, chan), whole(2, chan), whole(1, chan), ANY,
                  whole(rows, chan), whole(2, chan), whole(1, chan), whole(1, chan)] + [whole(8, 128)] * len(token),
        out_specs=[whole(rows, chan), whole(rows, chan), whole(2, chan)],
        out_shape=(
            jax.ShapeDtypeStruct((rows, chan), BF16),
            jax.ShapeDtypeStruct((rows, chan), F32),
            jax.ShapeDtypeStruct((2, chan), F32),
        ),
        scratch_shapes=[
            pltpu.VMEM((slabs, 8, chan), F32),
            pltpu.VMEM(turned_shape(order, chan), F32),
            pltpu.VMEM((rows, 9 * chan), BF16),
            pltpu.VMEM((chan, 9 * chan), BF16),
            pltpu.SemaphoreType.DMA((9,)),
        ],
        compiler_params=params(28),
        cost_estimate=cost(18 * rows * chan * chan, 20 << 20),
        name="middle_back",
    )(grad, grad_sums, second_pre, mid_sums, mid_gain, kernel_taps, first_pre, in_sums, in_gain, in_bias, *token)


def middle_weight(order, hidden_one, grad, where, nblk, taps, token, hold=()):
    rows, chan = grad.shape
    slabs = rows // 8
    start, count = taps
    own = chan // nblk

    def kernel(at_ref, y_ref, g_ref, *refs):
        send_ref, keep_ref = refs[len(hold) + len(token) :][:2]
        mark, turned, lhs = refs[-3:]
        mark[...] = jnp.zeros_like(mark)
        k = pl.program_id(0)

        @pl.when(k == 0)
        def _():
            turn(order, chan, y_ref, turned)

        for tap in range(count):

            @pl.when(k == tap)
            def _(tap=tap):
                lhs[...] = shifted(order, chan, y_ref, turned, start + tap, True)

        weight = mm_tn(lhs[...], g_ref[...]).reshape(1, nblk // 2, 2, own, chan)
        halves(lambda c: weight[:, :, c], at_ref[0], send_ref, keep_ref)
        if hold:
            refs[-4][...] = refs[0][...]

    half = pl.BlockSpec((1, nblk // 2, own, chan), lambda k: (k, 0, 0, 0))
    kept = [whole(*h.shape) for h in hold]
    return pl.pallas_call(
        kernel,
        grid=(count,),
        in_specs=[SMEM, whole(slabs, 8, chan), whole(rows, chan)] + kept + [whole(8, 128)] * len(token),
        out_specs=[half, half] + kept + [whole(8, 128)],
        out_shape=(jax.ShapeDtypeStruct((count, nblk // 2, own, chan), F32),) * 2
        + tuple(jax.ShapeDtypeStruct(h.shape, F32) for h in hold)
        + (MARK,),
        scratch_shapes=[pltpu.VMEM(turned_shape(order, chan), F32), pltpu.VMEM((rows, chan), BF16)],
        compiler_params=params(14),
        cost_estimate=cost(2 * rows * chan * chan * count, 2 << 20),
        name="middle_weight",
    )(where, hidden_one, grad, *hold, *token)


def first_back(order, grad, grad_sums, total, first_pre, in_sums, in_gain, inputs, where, nblk, token):
    rows, chan = grad.shape
    slabs = rows // 8
    width = inputs.shape[1]
    own = width // nblk
    each = 2 * own
    merge = max(1, 512 // each)
    units = 4

    def kernel(at_ref, gq_ref, gs_ref, f_ref, is_ref, ig_ref, x_ref, *refs):
        ga_ref, send_ref, keep_ref, mark = refs[len(token):]
        mark[...] = jnp.zeros_like(mark)

        @pl.when(pl.program_id(0) == 0)
        def _():
            mean1, rstd1 = moments(is_ref, total)
            lift = ig_ref[...] * rstd1
            slant = rstd1 * gs_ref[1:2, :] * (1.0 / total)
            base = gs_ref[0:1, :] * (1.0 / total) - mean1 * slant
            ga = lift * (gq_ref[...] - base - f_ref[...] * slant)
            ga_ref[...] = live(order, ga.reshape(slabs, 8, chan)).reshape(rows, chan).astype(BF16)

        weight = mm_tn(x_ref[...], ga_ref[...]).reshape(merge, 2, units, own // units, chan)
        halves(lambda c: jnp.swapaxes(weight[:, c], 0, 1), at_ref[0], send_ref, keep_ref)

    half = pl.BlockSpec((units, merge, own // units, chan), lambda j: (0, j, 0, 0))
    return pl.pallas_call(
        kernel,
        grid=(width // (each * merge),),
        in_specs=[SMEM, whole(rows, chan), whole(2, chan), whole(rows, chan), whole(2, chan), whole(1, chan),
                  lanes_of(each * merge, rows)] + [whole(8, 128)] * len(token),
        out_specs=[whole(rows, chan), half, half, whole(8, 128)],
        out_shape=(
            jax.ShapeDtypeStruct((rows, chan), BF16),
            jax.ShapeDtypeStruct((units, nblk // 2, own // units, chan), F32),
            jax.ShapeDtypeStruct((units, nblk // 2, own // units, chan), F32),
            MARK,
        ),
        compiler_params=params(16),
        cost_estimate=cost(2 * rows * width * chan, 10 << 20),
        name="first_back",
    )(where, grad, grad_sums, first_pre, in_sums, in_gain, inputs, *token)


def input_grads(parts, order, slope, share, grad_first, conv_in, token):
    rows, width = slope.shape
    slabs = rows // 8
    chan = grad_first.shape[1]
    block = 512

    def kernel(s_ref, e_ref, g_ref, w_ref, *refs):
        gr = s_ref[...].astype(F32) * spread(order, e_ref).reshape(rows, block)
        gx = (gr + mm_nt(g_ref[...], w_ref[...])).reshape(slabs, 8, block)
        refs[-1][...] = jnp.zeros((8, 128), F32)
        for p, ref in zip(parts, refs[-4:-1]):
            piece = gx[p.cut]
            if p.by_column:
                ref[...] = piece.reshape(p.crops, p.side, 8, block)[:, :, 0 : p.side, :]
            else:
                ref[...] = piece

    out_specs = []
    out_shape = []
    for p in parts:
        if p.by_column:
            out_specs.append(pl.BlockSpec((p.crops, p.side, p.side, block), lambda j: (0, 0, 0, j)))
            out_shape.append(jax.ShapeDtypeStruct((p.crops, p.side, p.side, width), F32))
        else:
            out_specs.append(lanes_of(block, p.slabs, 8))
            out_shape.append(jax.ShapeDtypeStruct((p.slabs, 8, width), F32))
    return pl.pallas_call(
        kernel,
        grid=(width // block,),
        in_specs=[lanes_of(block, rows), lanes_of(block, share.shape[0]), whole(rows, chan),
                  pl.BlockSpec((block, chan), lambda j: (j, 0))] + [whole(8, 128)] * len(token),
        out_specs=out_specs + [whole(8, 128)],
        out_shape=(*out_shape, MARK),
        compiler_params=params(18),
        cost_estimate=cost(2 * rows * width * chan, 14 << 20),
        name="input_grads",
    )(slope, share, grad_first, conv_in, *token)


def masks_of(size, lowest=1):
    stages = []
    bit = lowest
    while bit < size:
        if 2 * bit < size:
            stages.append([bit, 2 * bit, 3 * bit])
            bit = 4 * bit
        else:
            stages.append([bit])
            bit = 2 * bit
    return stages


def swap(x, axis, mask):
    size = lax.axis_size(axis)
    return lax.ppermute(x, axis, [(i, i ^ mask) for i in range(size)])


def sum_stages(x, axis, stages):
    for masks in stages:
        got = [swap(x, axis, m) for m in masks]
        for g in got:
            x = x + g
    return x


def sum_core(x):
    return sum_stages(x, "blk", [[1]])


def sum_near(x):
    return sum_stages(x, "dp", masks_of(lax.axis_size("dp")))


def sum_far(x):
    return sum_stages(x, "blk", masks_of(lax.axis_size("blk"), 2))


def sum_all(x):
    return sum_far(sum_near(sum_core(x)))


def gather_all(x, between=None):
    dp = lax.axis_index("dp")
    blk = lax.axis_index("blk")
    nblk = lax.axis_size("blk")
    ndp = lax.axis_size("dp")
    joined = x[None]
    where = [0]
    for masks in masks_of(nblk, 2):
        joined = join([joined] + [swap(joined, "blk", m) for m in masks], []).reshape(-1, *x.shape)
        where = where + [w ^ m for m in masks for w in where]
    rows = [joined] + [swap(joined, "dp", k) for k in range(1, ndp)]
    extra = ()
    if between is not None:
        *extra, rows[0] = between(joined)
    rows += [swap(r, "blk", 1) for r in rows]
    number = [
        (dp ^ k) * nblk + (blk ^ (w ^ c)) for c in range(2) for k in range(ndp) for w in where
    ]
    return rows, jnp.stack(number), extra


def fold(kernel, count, where, ins, outs, token, hold, name):
    ins_n, outs_n, hold_n = len(ins), len(outs), len(hold)

    def whole_kernel(at_ref, *refs):
        kernel(at_ref, refs[:ins_n], refs[ins_n + hold_n + len(token) :][:outs_n])
        for k in range(hold_n):
            refs[len(refs) - 1 - hold_n + k][...] = refs[ins_n + k][...]
        refs[-1][...] = jnp.zeros((8, 128), F32)

    def unit(shape):
        if len(shape) == 3:
            return pl.BlockSpec((*shape[:2], shape[2] // count), lambda i: (0, 0, i))
        return pl.BlockSpec((1, *shape[1:]), lambda i: (i,) + (0,) * (len(shape) - 1))

    kept = [whole(*h.shape) for h in hold]
    result = pl.pallas_call(
        whole_kernel,
        grid=(count,),
        in_specs=[SMEM] + [unit(x.shape) for x in ins] + kept + [whole(8, 128)] * len(token),
        out_specs=[unit(x) for x in outs] + kept + [whole(8, 128)],
        out_shape=[jax.ShapeDtypeStruct(x, F32) for x in outs] + [jax.ShapeDtypeStruct(h.shape, F32) for h in hold] + [MARK],
        compiler_params=params(12),
        cost_estimate=cost(0, 0),
        name=name,
    )(where, *ins, *hold, *token)
    return result[:outs_n], result[outs_n:-1], result[-1]


def fold_first(keep, got, way, where, token, hold, extra=None):
    t, nz, _, r, n = keep.shape
    h = r // 2 if way == "both" else r
    ways = {"x": [0], "y": [1], "both": [0, 1]}[way]
    more = 0 if extra is None else 1

    def kernel(at_ref, ins, outs):
        x = at_ref[1] & 1
        y = at_ref[1] >> 1
        for k, w in enumerate(ways):
            rows = slice(k * h, k * h + h)
            for o in range(2):
                for out, q in (
                    (outs[2 * k], 2 * (1 - y) + o if w else 2 * o + 1 - x),
                    (outs[2 * k + 1], 2 * y + o if w else 2 * o + x),
                ):
                    out[0, 0:nz, o] = ins[0][0, :, q, rows, :] + ins[1][0, :, q, rows, :]
                    if more:
                        out[0, nz, o] = ins[2][q, rows, :]

    ins = [keep, got] + ([extra.reshape(4, r, t * n)] if more else [])
    return fold(kernel, t, where, ins, [(t, nz + more, 2, h, n)] * (2 * len(ways)), token, hold, "fold_first")


def fold_second(sums, way, where, token, hold):
    t, nz, _, h, n = sums[0].shape
    ways = {"x": [0], "y": [1], "both": [0, 1]}[way]

    def kernel(at_ref, ins, outs):
        for k, w in enumerate(ways):
            at = at_ref[1] & 1 if w else at_ref[1] >> 1
            add = lambda q: ins[2 * k][0, :, q] + ins[2 * k + 1][0, :, q]
            outs[2 * k][0] = add(1 - at)
            outs[2 * k + 1][0] = add(at)

    return fold(kernel, t, where, sums, [(t, nz, h, n)] * len(sums), token, hold, "fold_second")


def far_masks(nz):
    if nz == 4:
        return [1, 3]
    return [1 << k for k in range(nz.bit_length() - 1)]


def span(masks):
    offsets = [0]
    for m in masks:
        offsets = offsets + [o ^ m for o in offsets]
    return offsets


def fold_far_first(chains, masks, where, token, more):
    rest = span(masks[1:])
    ins = [x for chain in chains for x in chain]
    full = len(chains[0]) // 2 * chains[0][0].shape[2]
    n = ins[0].shape[-1]
    total = sum(chain[0].shape[0] for chain in chains)

    def kernel(at_ref, *refs):
        outs = refs[len(ins) + len(token) :]
        send, keep, mark = outs[:3]
        mark[...] = jnp.zeros_like(mark)
        first = at = 0
        for chain in chains:
            t, nz, h, _ = chain[0].shape
            for w in range(len(chain) // 2):
                a, b = refs[at : at + 2]
                at += 2
                rows = slice(w * h, w * h + h)
                for k, o in enumerate(rest):
                    send[first : first + t, k, rows, :] = a[:, at_ref[2] ^ o ^ masks[0]] + b[:, at_ref[2] ^ o ^ masks[0]]
                    keep[first : first + t, k, rows, :] = a[:, at_ref[2] ^ o] + b[:, at_ref[2] ^ o]
                if more:
                    outs[3][first : first + t, rows, :] = a[:, nz - 1] + b[:, nz - 1]
            first += t

    shape = (total, len(rest), full, n)
    whole_shape = [(total, full, n)] if more else []
    return pl.pallas_call(
        kernel,
        in_specs=[SMEM] + [whole(*x.shape) for x in ins] + [whole(8, 128)] * len(token),
        out_specs=[whole(*shape)] * 2 + [whole(8, 128)] + [whole(*x) for x in whole_shape],
        out_shape=[jax.ShapeDtypeStruct(shape, F32)] * 2 + [MARK] + [jax.ShapeDtypeStruct(x, F32) for x in whole_shape],
        compiler_params=params(14),
        cost_estimate=cost(0, 0),
        name="fold_far_first",
    )(where, *ins, *token)


def fold_far(keep, got, step, masks, where, token):
    rest = span(masks[step + 1 :])
    before = span(masks[step:])
    t, _, r, n = keep.shape

    def kernel(at_ref, a, b, *refs):
        send, stay, mark = refs[-3:]
        mark[...] = jnp.zeros_like(mark)
        for k, o in enumerate(rest):
            for out, offset in ((send, o ^ masks[step]), (stay, o)):
                out[:, k] = a[:, before.index(offset)] + b[:, before.index(offset)]

    shape = (t, len(rest), r, n)
    return pl.pallas_call(
        kernel,
        in_specs=[SMEM] + [whole(*keep.shape)] * 2 + [whole(8, 128)] * len(token),
        out_specs=[whole(*shape)] * 2 + [whole(8, 128)],
        out_shape=[jax.ShapeDtypeStruct(shape, F32)] * 2 + [MARK],
        compiler_params=params(12),
        cost_estimate=cost(0, 0),
        name="fold_far",
    )(where, keep, got, *token)


def place(pieces, where):
    t, r, n = pieces[0].shape
    count = len(pieces)

    def kernel(at_ref, *refs):
        for k in range(count):
            refs[-1][:, at_ref[1] ^ k] = refs[k][...]

    return pl.pallas_call(
        kernel,
        in_specs=[SMEM] + [whole(t, r, n)] * count,
        out_specs=whole(t, count, r, n),
        out_shape=jax.ShapeDtypeStruct((t, count, r, n), F32),
        compiler_params=params(8),
        name="place",
    )(where, *pieces)


def total_of(groups, token):
    total = sum(g[0].shape[0] for g in groups)
    r, n = groups[0][0].shape[-2:]
    ins = [x.reshape(x.shape[0], r, n) for g in groups for x in g]

    def kernel(*refs):
        at = row = 0
        for g in groups:
            t = g[0].shape[0]
            out = refs[at][...]
            for k in range(1, len(g)):
                out = out + refs[at + k][...]
            at += len(g)
            refs[-2][row : row + t] = out
            row += t
        refs[-1][...] = jnp.zeros((8, 128), F32)

    return pl.pallas_call(
        kernel,
        in_specs=[whole(*x.shape) for x in ins] + [whole(8, 128)] * len(token),
        out_specs=[whole(total, r, n), whole(8, 128)],
        out_shape=[jax.ShapeDtypeStruct((total, r, n), F32), MARK],
        compiler_params=params(8),
        name="total_of",
    )(*ins, *token)


class Reduce:
    def __init__(self, send, keep, mark, way, where, extra=None):
        self.where = where
        self.extra = extra
        self.mark = mark
        self.way = way
        t, nz, rows, n = keep.shape
        ndp = lax.axis_size("dp")
        cut = (t, nz, ndp, rows // ndp, n)
        self.keep = keep.reshape(cut)
        self.got = swap(send, "blk", 1).reshape(cut)
        self.masks = far_masks(nz)
        self.first_way = {"x": [1], "y": [2], "both": [1, 2]}[way]

    def near(self, folded, masks):
        outs, kept, self.mark = folded
        self.sums = []
        for k, mask in enumerate(masks):
            self.sums += [outs[2 * k + 1], swap(outs[2 * k], "dp", mask)]
        return kept

    def first(self, token=(), hold=()):
        return self.near(fold_first(self.keep, self.got, self.way, self.where, token, hold, self.extra), self.first_way)

    def second(self, token=(), hold=()):
        return self.near(fold_second(self.sums, self.way, self.where, token, hold), [3 - m for m in self.first_way])


class Spread:
    def __init__(self, chains, token=()):
        self.where = chains[0].where
        self.masks = chains[0].masks
        more = chains[0].extra is not None
        folded = fold_far_first([c.sums for c in chains], self.masks, self.where, token, more)
        self.extra = folded[3] if more else None
        self.next(folded[:3], 0)

    def next(self, folded, step):
        send, keep, self.mark = folded
        self.sums = [keep, swap(send, "blk", 2 * self.masks[step])]

    def far(self, token=()):
        for step in range(1, len(self.masks)):
            self.next(fold_far(*self.sums, step, self.masks, self.where, token), step)


class Gather:
    def __init__(self, parts, token=()):
        self.where = parts[0].where
        out, self.mark = total_of([p.sums if isinstance(p, Spread) else [p] for p in parts], token)
        self.pieces = [out] + [swap(out, "dp", k) for k in range(1, lax.axis_size("dp"))]

    def last(self):
        t, r, n = self.pieces[0].shape
        return place(self.pieces, self.where).reshape(t, len(self.pieces) * r, n)


def share_sum(local, where):
    nblk, rows, n = local.shape
    local = local.reshape(1, nblk // 2, 2, rows, n)
    pick = lambda c: lax.dynamic_index_in_dim(local, c, 2, keepdims=False)
    whole_sum = Reduce(pick(1 - where[0]), pick(where[0]), None, "x", where)
    whole_sum.first()
    whole_sum.second()
    out = Spread([whole_sum])
    out.far()
    return Gather([out]).last()[0]


def projector_spread(order, pre, gain, bias, embed_map, hidden_map, plain, normed_sums, crop_total):
    slots = pre.shape[0]
    crops = sum(p.crops for p in order)
    high = lax.Precision.HIGHEST
    embed_map = embed_map.astype(F32)
    raw = pre[:crops]
    sums = sum_all(jnp.stack([jnp.sum(raw, axis=0), jnp.sum(raw * raw, axis=0)]))
    mean = sums[0] / crop_total
    rstd = lax.rsqrt(sums[1] / crop_total - mean * mean + NORM_EPS)
    normed = (raw - mean) * rstd
    q = gain * normed + bias
    sig = jax.nn.sigmoid(q)
    hp = q * sig
    z = jnp.dot(hp, embed_map, precision=high)
    emb = z.shape[1]
    z = jnp.concatenate([z, pre[crops : crops + 1, :emb], jnp.zeros((slots - crops - 1, emb), F32)], axis=0)
    z, _, _ = gather_all(z)
    z = jnp.concatenate(z, axis=0)
    blocks = z.shape[0]
    pairs = z[:, crops, :64]
    z = z[:, :crops].reshape(blocks * crops, emb)
    zc = z - jnp.sum(z, axis=0) / crop_total
    cov = jnp.dot(zc.T, zc, precision=high) / crop_total
    white = jax.scipy.linalg.solve_triangular(jnp.linalg.cholesky(cov), jnp.eye(emb, dtype=F32), lower=True)
    w = jnp.dot(zc, white.T, precision=high)
    inv_len = lax.rsqrt(jnp.sum(w * w, axis=1, keepdims=True) + UNIT_EPS)
    u = w * inv_len
    slot = jnp.arange(crops, dtype=F32)
    ends = (pairs[:, :32, None] == slot).astype(F32) - (pairs[:, 32:, None] == slot).astype(F32)
    gap = jnp.einsum("bpc,bce->bpe", ends, u.reshape(blocks, crops, emb), precision=high)
    gu = 2.0 * jnp.einsum("bpc,bpe->bce", ends, gap, precision=high).reshape(blocks * crops, emb)
    gw = (gu - u * jnp.sum(u * gu, axis=1, keepdims=True)) * inv_len
    moment = jnp.dot(gw.T, w, precision=high)
    sym = jnp.tril(moment) + jnp.tril(moment, -1).T
    back = gw[:crops] - (jnp.sum(gw, axis=0) + jnp.dot(w[:crops], sym, precision=high)) / crop_total
    gz = jnp.dot(back, white, precision=high)
    gq = jnp.dot(gz, embed_map.T, precision=high) * (sig * (1.0 + q * (1.0 - sig)))
    sums = sum_all(jnp.stack([jnp.sum(gq, axis=0), jnp.sum(gq * normed, axis=0)]))
    gap = gain * rstd * (gq - sums[0] / crop_total - normed * (sums[1] / crop_total))
    ge = jnp.dot(gap, hidden_map.astype(F32).T, precision=high)
    area = jnp.concatenate([jnp.full((p.crops, 1), 1.0 / (p.side * p.side), F32) for p in order])
    share = jnp.pad(ge * area, ((0, slots - crops), (0, 0)))
    stats = jnp.stack([jnp.sum(share * plain, axis=0), jnp.sum(share * normed_sums, axis=0)])
    return hp, gap, gz, sums[1:2], sums[0:1], share, stats


def body(crops_seven, crops_six, crops_five, conv_in, gain_in, bias_in, conv_mid, gain_mid, bias_mid,
         conv_out, gain_out, bias_out, proj_hidden, gain_proj, bias_proj, proj_embed, pair_index):
    crops_in = (crops_seven, crops_six, crops_five)
    parts, order, slabs = layout([c.shape for c in crops_in])
    ndp = lax.axis_size("dp")
    nblk = lax.axis_size("blk")
    dp = lax.axis_index("dp")
    blk = lax.axis_index("blk")
    devices = ndp * nblk
    crops = sum(p.crops for p in parts)
    total = float(sum(p.crops * p.side * p.side for p in parts) * devices)
    crop_total = float(crops * devices)
    slots = 24
    width, chan = conv_in.shape
    hidden, emb = proj_embed.shape
    row = lambda v: v.reshape(1, -1)
    where = jnp.stack([blk % 2, dp, blk // 2]).astype(jnp.int32)
    first_crop = 0
    pair_slot = pair_index
    for p in parts:
        mine = (pair_index >= first_crop) & (pair_index < first_crop + p.crops)
        pair_slot = jnp.where(mine, pair_index - first_crop + p.slot, pair_slot)
        first_crop += p.crops
    pair_row = jnp.pad(
        jnp.concatenate([pair_slot[:, 0], pair_slot[:, 1]]).astype(F32), (0, hidden - 2 * pair_index.shape[0])
    )
    laid = [
        c if p.by_column else jnp.transpose(c, (1, 2, 0, 3)).reshape(p.slabs, 8, width) for c, p in zip(crops_in, parts)
    ]

    inputs, first_pre, sums = first_conv(parts, order, slabs, laid, conv_in)
    in_sums = sum_all(sums)
    hidden_one, second_pre, sums = middle_conv(
        order, first_pre, in_sums, total, row(gain_in), row(bias_in), conv_mid.reshape(9 * chan, chan)
    )
    mid_sums = sum_all(sums)
    hidden_two, third_pre, sums = last_conv(order, second_pre, mid_sums, total, row(gain_mid), row(bias_mid), conv_out)
    out_sums = sum_all(sums)
    gain_o, bias_o = row(gain_out), row(bias_out)
    pooled, pre = pool_embed(
        order, slots, third_pre, out_sums, total, gain_o, bias_o, inputs, proj_hidden, row(pair_row)
    )
    small = devices <= 32
    slopes = lambda *hold: slope_sums(
        order, slots, third_pre, out_sums, total, gain_o, bias_o, inputs, hold
    )
    if small:
        pre, number, (slope, plain, normed_sums) = gather_all(pre, slopes)
    else:
        slope, plain, normed_sums = slopes()
    middle = projector if small else projector_spread
    hp, gap, gz, gg_proj, gb_proj, share, sums = middle(
        order, pre, row(gain_proj), row(bias_proj), proj_embed, proj_hidden, plain, normed_sums, crop_total
    )
    out_back = sum_all(sums)
    grad_two, sums, local_out = last_back(
        order, slope, share, third_pre, out_sums, out_back, total, gain_o, conv_out,
        second_pre, mid_sums, row(gain_mid), row(bias_mid), hidden_two
    )
    pooled_all = lax.all_gather(pooled, ("dp", "blk"), axis=0) if small else pooled
    out_part = lax.psum_scatter(local_out, "blk", scatter_dimension=0, tiled=True)
    mid_back = sum_all(sums)
    grad_second, grad_one, sums = middle_back(
        order, grad_two, mid_back, total, second_pre, mid_sums, row(gain_mid), conv_mid.reshape(9, chan, chan),
        first_pre, in_sums, row(gain_in), row(bias_in), [mark_of(pooled_all)]
    )
    send, keep, core, mark = middle_weight(
        order, hidden_one, grad_second, where, nblk, (0, 5), [], [sum_core(sums)]
    )
    m0 = Reduce(send, keep, mark, "both", where)
    (near,) = m0.first(hold=[sum_near(core)])
    in_back = sum_stages(near, "blk", [[1 << k] for k in range(1, nblk.bit_length() - 1)])
    grad_first, send, keep, mark = first_back(
        order, grad_one, in_back, total, first_pre, in_sums, row(gain_in), inputs, where, nblk, []
    )
    i = Reduce(send, keep, mark, "both", where, out_part)
    m1 = Reduce(*middle_weight(order, hidden_one, grad_second, where, nblk, (5, 4), []), "both", where)
    i.first()
    *grads, mark = input_grads(parts, order, slope, share, grad_first, conv_in, [i.mark])
    m0.second()
    m1.first()

    high = lax.Precision.HIGH
    if small:
        own = width // nblk
        pooled_own = lax.dynamic_slice_in_dim(pooled_all, blk * own, own, 2)[number].reshape(devices * slots, own)
        hidden_grad = lax.dot_general(pooled_own, gap, (((0,), (0,)), ((), ())), precision=high)
        own = hidden // nblk
        embed_grad = lax.dot_general(
            lax.dynamic_slice_in_dim(hp, blk * own, own, 1), gz, (((0,), (0,)), ((), ())), precision=high
        )
    else:
        local = lax.dot_general(pooled[:crops], gap, (((0,), (0,)), ((), ())), precision=high)
        hidden_grad = share_sum(local.reshape(nblk, width // nblk, hidden), where)
        local = lax.dot_general(hp, gz, (((0,), (0,)), ((), ())), precision=high)
        embed_grad = share_sum(local.reshape(nblk, hidden // nblk, emb), where)

    i.second([mark])
    last = Spread([i], [])
    far0 = Spread([m0], [mark_of(hidden_grad), mark_of(embed_grad)])
    m1.second()
    last.far()
    far0.far()
    far1 = Spread([m1], [])
    early = Gather([last, last.extra], [])
    far1.far()
    late = Gather([far0, far1], [])
    early = early.last()
    conv_in_grad, out_grad = early[0:4].reshape(width // nblk, chan), early[4:8]
    out_grad = jnp.concatenate(list(out_grad), axis=1)
    mid_grad = late.last()
    grads = [
        g if p.by_column else jnp.transpose(g.reshape(p.side, p.side, 8, width), (2, 0, 1, 3))
        for g, p in zip(grads, parts)
    ]
    return (
        *grads,
        conv_in_grad,
        mid_grad.reshape(3, 3, chan // nblk, chan),
        out_grad,
        hidden_grad,
        embed_grad,
        in_back[1],
        in_back[0],
        mid_back[1],
        mid_back[0],
        out_back[1],
        out_back[0],
        gg_proj[0],
        gb_proj[0],
    )


def solution(mesh):
    from_both = ("dp", "blk")
    crop_spec = jax.sharding.PartitionSpec(from_both, None, None, None)
    spec = jax.sharding.PartitionSpec
    in_specs = (crop_spec,) * 3 + (spec(),) * 13 + (spec(from_both, None),)
    out_specs = (crop_spec,) * 3 + (
        spec("blk", None),
        spec(None, None, "blk", None),
        spec("blk", None),
        spec("blk", None),
        spec("blk", None),
    ) + (spec(),) * 8
    return jax.shard_map(body, mesh=mesh, in_specs=in_specs, out_specs=out_specs, check_vma=False)
```

time: 452 us -> 337 us (0.75); the launches traced: 444 us -> 336 us
  waiting for transfers between devices: 152 us -> 69 us
  other arithmetic: 13.6 us -> 1.76 us
  local copies, waits for them, and re-layouts: 58.5 us -> 46.9 us
  matrix products: 13.9 us -> 3.26 us
  Pallas kernels: 102 us -> 110 us
    ppermute x79 -> x78, waiting for transfers between devices: 152 us -> 68.9 us  [swap(): return lax.ppermute(x, axis, [(i, i ^ mask) for i in range(size)])]
    pallas_call x10 -> x28, Pallas kernels: 75.8 us -> 92.8 us  [the longest x6 19.7 us: fold(): pl.pallas_call(whole_kernel, grid=(count,), in_specs=[SMEM] + [unit(x.sha...]
    dynamic_slice x5 -> x0, local copies, waits for them, and re-layouts: 10.5 us -> none  [the longest x2 10.3 us: pick(): return lax.dynamic_index_in_dim(x, index, axis, keepdims=False)]
    add x27 -> x19, other arithmetic: 10.5 us -> 0.17 us  [sum_stages(): x = x + g]
    pallas_call x1, Pallas kernels: 26 us -> 17.3 us  [projector(): pl.pallas_call(kernel, out_shape=(jax.ShapeDtypeStruct((rows_all, hidden)...]
    dot_general x2 -> x0, matrix products: 7.43 us -> none  [the longest x1 4.51 us: body(): lax.dot_general(hidden_two, grad_third, (((0,), (0,)), ((), ())), preferr...]
    unnamed x90 -> x130, local copies, waits for them, and re-layouts: 36.4 us -> 38.5 us
    ppermute x79 -> x78, starting transfers between devices: 88.8 us -> 88.7 us  [swap(): return lax.ppermute(x, axis, [(i, i ^ mask) for i in range(size)])]
  transfers between devices with their start and end apart: 80 -> 80, of which waited for: 51 -> 50; matrix products, arithmetic and copies ran while one was open for 12% -> 3% of each run, Pallas kernels for 16% -> 27%
where the time goes in v2:
time: 337 us; the launch traced here: 336 us
  Pallas kernels  110 us (33%)
  starting transfers between devices  88.8 us (26%)
  waiting for transfers between devices  69 us (20%)
  local copies, waits for them, and re-layouts  46.9 us (14%)
  between operations  16.1 us (5%)
    ppermute x78, starting transfers between devices, swap(): return lax.ppermute(x, axis, [(i, i ^ mask) for i in range(size)])  88.7 us
    ppermute x78, waiting for transfers between devices, swap(): return lax.ppermute(x, axis, [(i, i ^ mask) for i in range(size)])  68.9 us
    unnamed x130, local copies, waits for them, and re-layouts  38.5 us
    pallas_call x6, Pallas kernels, fold(): pl.pallas_call(whole_kernel, grid=(count,), in_specs=[SMEM] + [unit(x.sha...  19.7 us
    pallas_call x1, Pallas kernels, projector(): pl.pallas_call(kernel, out_shape=(jax.ShapeDtypeStruct((rows_all, hidden)...  17.3 us
    pallas_call x2, Pallas kernels, middle_weight(): pl.pallas_call(kernel, grid=(count,), in_specs=[SMEM, whole(slabs, 8, cha...  10.9 us
    pallas_call x1, Pallas kernels, last_back(): pl.pallas_call(kernel, grid=(steps,), in_specs=[lanes_of(block, rows), la...  10.4 us
    pallas_call x1, Pallas kernels, pool_embed(): pl.pallas_call(kernel, grid=(steps,), in_specs=[lanes_of(block, rows), la...  6.96 us
  transfers between devices with their start and end apart: 80, of which 50 were waited for; matrix products, arithmetic and copies ran while one was open for 3% of the time, Pallas kernels for 27%

profile of v2, /device:TPU:0, one launch (start us, length us, event | category | flops | bytes accessed | tf_op | source)
XLA Modules:
  0.0 336.0 jit_solution(11254042086592644657)
XLA Ops:
  13.5 4.0 %first_conv.1 = (bf16[880,2048]{1,0:T(8,128)(2,1)S(1)}, f32[880,512]{1,0:T(8,128)S(1)}, f32[2,512]{1,0:T(2,128)S(1)}) custom-call(bf16[49,8,2048]{2,1,0:T(8,128)(2,1)S(1)} %bitcast.107, bf16[6,6,6,2048]{3,2,1,0:T(8,128)(2,1)S(1)} %copy-done.29, bf16[25,8,2048]{2,1,0:T(8,128)(2,1)S(1)} %bitcast.112, bf16[2048,512]{1,0:T(8,128)(2,1)S(1)} %copy-done.16), custom_call_target="tpu_custom_call" | custom-call | tf_op jit(solution)/shard_map/first_conv/pallas_call | solution.py:183
  18.8 3.8 %collective-permute-start.3 = (f32[2,512]{1,0:T(2,128)S(1)}, f32[2,512]{1,0:T(2,128)S(1)}, u32[]{:S(2)}, u32[]{:S(2)}) collective-permute-start(f32[2,512]{1,0:T(2,128)S(1)} %add.262), channel_id=1, source_target_pairs={{0,24},{8,16},{16,8},{24,0},{1,25},{9,17},{17,9},{25,1},{2,26},{10... | collective-permute-start | bytes 12296 | tf_op jit(solution)/shard_map/ppermute | solution.py:866
  26.7 3.6 %collective-permute-start.6 = (f32[2,512]{1,0:T(2,128)S(1)}, f32[2,512]{1,0:T(2,128)S(1)}, u32[]{:S(2)}, u32[]{:S(2)}) collective-permute-start(f32[2,512]{1,0:T(2,128)S(1)} %add_add_fusion.10), channel_id=1, source_target_pairs={{0,6},{1,7},{2,4},{3,5},{4,2},{5,3},{6,0},{7,1},{8,14},{9,15},{10,... | collective-permute-start | bytes 12296 | tf_op jit(solution)/shard_map/ppermute | solution.py:866
  35.0 4.4 %middle_conv.1 = (f32[110,8,512]{2,1,0:T(8,128)S(1)}, f32[880,512]{1,0:T(8,128)S(1)}, f32[2,512]{1,0:T(2,128)S(1)}) custom-call(f32[880,512]{1,0:T(8,128)S(1)} %get-tuple-element.97.a_ref.f_ref, f32[2,512]{1,0:T(2,128)S(1)} %add_add_fusion.9.st_ref.is_ref, f32[1,512]{1,0:T(1,128)S(1)} %bitcast.129, f32[1,512]{1,0:T(1,128)S(1)} %bitcast.136, ...), custom_call_target="tpu_custom_call" | custom-call | tf_op jit(solution)/shard_map/middle_conv/pallas_call | solution.py:257
  53.5 3.8 %last_conv.1 = (bf16[880,512]{1,0:T(8,128)(2,1)S(1)}, f32[880,2048]{1,0:T(8,128)S(1)}, f32[2,2048]{1,0:T(2,128)S(1)}) custom-call(f32[880,512]{1,0:T(8,128)S(1)} %get-tuple-element.99.a_ref.m_ref, f32[2,512]{1,0:T(2,128)S(1)} %add_add_fusion.7.st_ref.ms_ref, f32[1,512]{1,0:T(1,128)S(1)} %bitcast.132, f32[1,512]{1,0:T(1,128)S(1)} %bitcast.138, ...), custom_call_target="tpu_custom_call" | custom-call | tf_op jit(solution)/shard_map/last_conv/pallas_call | solution.py:294
  72.8 7.0 %pool_embed.1 = (f32[24,2048]{1,0:T(8,128)}, f32[24,1024]{1,0:T(8,128)S(1)}) custom-call(f32[880,2048]{1,0:T(8,128)S(1)} %get-tuple-element.101.a_ref, f32[2,2048]{1,0:T(2,128)S(1)} %add_add_fusion.2.st_ref, f32[1,2048]{1,0:T(1,128)S(1)} %bitcast.124, f32[1,2048]{1,0:T(1,128)S(1)} %bitcast.127, bf16[880,2048]{1,0:T(8,128)(2,1)S(1)} %get-tuple-element.103.x_ref, ...), custom_call_target="tpu_custom_call" | custom-call | tf_op jit(solution)/shard_map/pool_embed/pallas_call | solution.py:348
  92.1 3.1 copy-done.1
  97.2 6.2 %slope_sums.1 = (bf16[880,2048]{1,0:T(8,128)(2,1)S(1)}, f32[24,2048]{1,0:T(8,128)S(1)}, f32[24,2048]{1,0:T(8,128)S(1)}, f32[4,24,1024]{2,1,0:T(8,128)S(1)}) custom-call(f32[880,2048]{1,0:T(8,128)S(1)} %copy-done.1, f32[2,2048]{1,0:T(2,128)S(1)} %add_add_fusion.2.st_ref, f32[1,2048]{1,0:T(1,128)S(1)} %bitcast.125, f32[1,2048]{1,0:T(1,128)S(1)} %bitcast.128, ...), custom_call_target="tpu_custom_call" | custom-call | tf_op jit(solution)/shard_map/slope_sums/pallas_call | solution.py:386
  104.0 4.0 %collective-permute-done.25.refs_2_ = f32[4,24,1024]{2,1,0:T(8,128)S(1)} collective-permute-done((f32[4,24,1024]{2,1,0:T(8,128)S(1)}, f32[4,24,1024]{2,1,0:T(8,128)S(1)}, u32[]{:S(2)}, u32[]{:S(2)}) %collective-permute-start.25) | collective-permute-done | bytes 393248 | tf_op jit(solution)/shard_map/ppermute | solution.py:866
  110.3 17.3 %projector.1 = (f32[768,1024]{1,0:T(8,128)S(1)}, f32[768,1024]{1,0:T(8,128)S(1)}, f32[768,128]{1,0:T(8,128)S(1)}, f32[1,1024]{1,0:T(1,128)}, f32[1,1024]{1,0:T(1...) custom-call(f32[4,24,1024]{2,1,0:T(8,128)S(1)} %get-tuple-element.106.refs_0_, ...), custom_call_target="tpu_custom_call" | custom-call | tf_op jit(solution)/shard_map/projector/pallas_call | solution.py:577
  140.5 2.9 collective-permute-start.35
  145.6 10.4 %last_back.1 = (f32[880,512]{1,0:T(8,128)S(1)}, f32[2,512]{1,0:T(2,128)S(1)}, f32[512,2048]{1,0:T(8,128)}) custom-call(bf16[880,2048]{1,0:T(8,128)(2,1)S(1)} %get-tuple-element.105.s_ref, f32[24,2048]{1,0:T(8,128)S(1)} %get-tuple-element.109.e_ref, f32[880,2048]{1,0:T(8,128)} %copy-done, f32[2,2048]{1,0:T(2,128)S(1)} %add_add_fusion.2.st_ref, ...), custom_call_target="tpu_custom_call" | custom-call | tf_op jit(solution)/shard_map/last_back/pallas_call | solution.py:651
  177.9 6.0 %middle_back.1 = (bf16[880,512]{1,0:T(8,128)(2,1)S(1)}, f32[880,512]{1,0:T(8,128)S(1)}, f32[2,512]{1,0:T(2,128)S(1)}) custom-call(f32[880,512]{1,0:T(8,128)S(1)} %copy-done.27, f32[2,512]{1,0:T(2,128)S(1)} %add_add_fusion.5.gs_ref, f32[880,512]{1,0:T(8,128)S(1)} %copy-done.11, f32[2,512]{1,0:T(2,128)S(1)} %add_add_fusion.7.st_ref.ms_ref, ...), custom_call_target="tpu_custom_call" | custom-call | tf_op jit(solution)/shard_map/middle_back/pallas_call | solution.py:701
  185.1 5.8 %middle_weight.2 = (f32[5,4,64,512]{3,2,1,0:T(8,128)S(1)}, f32[5,4,64,512]{3,2,1,0:T(8,128)S(1)}, f32[2,512]{1,0:T(2,128)S(1)}, f32[8,128]{1,0:T(8,128)}) custom-call(s32[3]{0:T(128)S(1)} %pad_add_fusion.at_ref, f32[110,8,512]{2,1,0:T(8,128)S(1)} %copy-done.19, bf16[880,512]{1,0:T(8,128)(2,1)S(1)} %get-tuple-element.117.g_ref, f32[2,512]{1,0:T(2,128)S(1)} %add.301.refs_0_), custom_call_target="tpu_custom_call" | custom-call | tf_op jit(solution)/shard_map/middle_weight/pallas_call | solution.py:753
  207.0 5.1 %middle_weight.3 = (f32[4,4,64,512]{3,2,1,0:T(8,128)}, f32[4,4,64,512]{3,2,1,0:T(8,128)S(1)}, f32[8,128]{1,0:T(8,128)}) custom-call(s32[3]{0:T(128)S(1)} %pad_add_fusion.at_ref, f32[110,8,512]{2,1,0:T(8,128)S(1)} %copy-done.19, bf16[880,512]{1,0:T(8,128)(2,1)S(1)} %get-tuple-element.117.g_ref), custom_call_target="tpu_custom_call" | custom-call | tf_op jit(solution)/shard_map/middle_weight/pallas_call | solution.py:753
  212.1 5.4 %first_back.1 = (bf16[880,512]{1,0:T(8,128)(2,1)S(1)}, f32[4,4,64,512]{3,2,1,0:T(8,128)}, f32[4,4,64,512]{3,2,1,0:T(8,128)S(1)}, f32[8,128]{1,0:T(8,128)}) custom-call(s32[3]{0:T(128)S(1)} %pad_add_fusion.at_ref, f32[880,512]{1,0:T(8,128)S(1)} %get-tuple-element.115.gq_ref, f32[2,512]{1,0:T(2,128)S(1)} %add.306.gs_ref, ...), custom_call_target="tpu_custom_call" | custom-call | tf_op jit(solution)/shard_map/first_back/pallas_call | solution.py:794
  223.2 3.7 %fold_first.5 = (f32[4,4,2,8,512]{4,3,2,1,0:T(8,128)}, f32[4,4,2,8,512]{4,3,2,1,0:T(8,128)S(1)}, f32[4,4,2,8,512]{4,3,2,1,0:T(8,128)}, f32[4,4,2,8,512]{4,3,2,1,0:T(8,128)S(1)}, f32[8,128]{1,0:T(8,128)}) custom-call(s32[3]{0:T(128)S(1)} %pad_add_fusion.at_ref, f32[4,4,4,16,512]{4,3,2,1,0:T(8,128)S(1)} %bitcast.106, f32[4,4,4,16,512]{4,3,2,1,0:T(8,128)} %bitcast.74.refs_1_), custom_call_target="tpu_custom_call" | custom-call | tf_op jit(solution)/shard_map/fold_first/pallas_call | solution.py:929
  231.5 3.8 %fold_first.4 = (f32[4,5,2,8,512]{4,3,2,1,0:T(8,128)}, f32[4,5,2,8,512]{4,3,2,1,0:T(8,128)S(1)}, f32[4,5,2,8,512]{4,3,2,1,0:T(8,128)}, f32[4,5,2,8,512]{4,3,2,1,0:T(8,128)S(1)}, f32[8,128]{1,0:T(8,128)S(1)}) custom-call(s32[3]{0:T(128)S(1)} %pad_add_fusion.at_ref, f32[4,4,4,16,512]{4,3,2,1,0:T(8,128)S(1)} %bitcast.105, ...), custom_call_target="tpu_custom_call" | custom-call | tf_op jit(solution)/shard_map/fold_first/pallas_call | solution.py:929
  241.9 3.8 %fold_second.4 = (f32[5,4,8,512]{3,2,1,0:T(8,128)}, f32[5,4,8,512]{3,2,1,0:T(8,128)S(1)}, f32[5,4,8,512]{3,2,1,0:T(8,128)S(1)}, f32[5,4,8,512]{3,2,1,0:T(8,128)S(1)}, f32[8,128]{1,0:T(8,128)}) custom-call(s32[3]{0:T(128)S(1)} %pad_add_fusion.at_ref, f32[5,4,2,8,512]{4,3,2,1,0:T(8,128)S(1)} %copy-done.32, ...), custom_call_target="tpu_custom_call" | custom-call | tf_op jit(solution)/shard_map/fold_second/pallas_call | solution.py:929
  263.6 4.4 %input_grads.1 = (f32[49,8,2048]{2,1,0:T(8,128)}, f32[6,6,6,2048]{3,2,1,0:T(8,128)}, f32[25,8,2048]{2,1,0:T(8,128)}, f32[8,128]{1,0:T(8,128)S(1)}) custom-call(bf16[880,2048]{1,0:T(8,128)(2,1)S(1)} %copy-done.13, f32[24,2048]{1,0:T(8,128)S(1)} %get-tuple-element.109.e_ref, bf16[880,512]{1,0:T(8,128)(2,1)S(1)} %get-tuple-element.123.g_ref, ...), custom_call_target="tpu_custom_call" | custom-call | tf_op jit(solution)/shard_map/input_grads/pallas_call | solution.py:838
  269.0 2.9 fold_second.3
  285.4 3.2 collective-permute-done.66.b
  297.8 4.3 %collective-permute-done.74 = f32[4,1,16,512]{3,2,0,1:T(8,128)S(1)} collective-permute-done((f32[4,1,16,512]{3,2,0,1:T(8,128)S(1)}, f32[4,1,16,512]{3,2,0,1:T(8,128)S(1)}, u32[]{:S(2)}, u32[]{:S(2)}) %collective-permute-start.74) | collective-permute-done | bytes 131104 | tf_op jit(solution)/shard_map/ppermute | solution.py:866
  317.6 3.8 %collective-permute-done.76.refs_2_ = f32[9,16,512]{2,1,0:T(8,128)S(1)} collective-permute-done((f32[9,16,512]{2,1,0:T(8,128)S(1)}, f32[9,16,512]{2,1,0:T(8,128)S(1)}, u32[]{:S(2)}, u32[]{:S(2)}) %collective-permute-start.76) | collective-permute-done | bytes 294944 | tf_op jit(solution)/shard_map/ppermute | solution.py:866
  (337 shorter events, 197.5 us)
Async XLA Ops:
  8.0 163.7 %all-gather.3.cloned.1.call-start = ((), (), s32[]{:S(2)}) async-start(), calls=%async_computation.2 | async-start | bytes 6488064 | tf_op jit(solution)/shard_map/all_gather | solution.py:1274
  79.8 150.7 %reduce-scatter.2.cloned.1.call-start = ((), (), s32[]{:S(2)}) async-start(), calls=%async_computation.1 | async-start | bytes 4718592 | tf_op jit(solution)/shard_map/reduce_scatter | solution.py:1275
  88.6 15.0 %collective-permute-start.26 = (f32[4,24,1024]{2,1,0:T(8,128)S(1)}, f32[4,24,1024]{2,1,0:T(8,128)S(1)}, u32[]{:S(2)}, u32[]{:S(2)}) collective-permute-start(f32[4,24,1024]{2,1,0:T(8,128)S(1)} %bitcast.108), channel_id=1, source_target_pairs={{0,24},{8,16},{16,8},{24,0},{1,25},{9,17},{17,9},{25,1},{2,26},{10... | collective-permute-start | bytes 1179656 | tf_op jit(solution)/shard_map/ppermute | solution.py:866
  90.4 17.6 %collective-permute-start.25 = (f32[4,24,1024]{2,1,0:T(8,128)S(1)}, f32[4,24,1024]{2,1,0:T(8,128)S(1)}, u32[]{:S(2)}, u32[]{:S(2)}) collective-permute-start(f32[4,24,1024]{2,1,0:T(8,128)S(1)} %bitcast.109), channel_id=1, source_target_pairs={{0,16},{8,24},{16,0},{24,8},{1,17},{9,25},{17,1},{25,9},{2,18},{10... | collective-permute-start | bytes 1179656 | tf_op jit(solution)/shard_map/ppermute | solution.py:866
  90.9 17.1 %collective-permute-start.24 = (f32[4,24,1024]{2,1,0:T(8,128)S(1)}, f32[4,24,1024]{2,1,0:T(8,128)S(1)}, u32[]{:S(2)}, u32[]{:S(2)}) collective-permute-start(f32[4,24,1024]{2,1,0:T(8,128)S(1)} %bitcast.110), channel_id=1, source_target_pairs={{0,8},{8,0},{16,24},{24,16},{1,9},{9,1},{17,25},{25,17},{2,10},{10... | collective-permute-start | bytes 1179656 | tf_op jit(solution)/shard_map/ppermute | solution.py:866
  218.9 11.6 %collective-permute-start.52 = (f32[4,4,64,512]{3,2,1,0:T(8,128)}, f32[4,4,64,512]{3,2,1,0:T(8,128)}, u32[]{:S(2)}, u32[]{:S(2)}) collective-permute-start(f32[4,4,64,512]{3,2,1,0:T(8,128)} %get-tuple-element.125), channel_id=1, source_target_pairs={{0,1},{1,0},{2,3},{3,2},{4,5},{5,4},{6,7},{7,6},{8,9},{9,8},{10,11... | collective-permute-start | bytes 6291464 | tf_op jit(solution)/shard_map/ppermute | solution.py:866
  219.4 19.0 %collective-permute-start.62 = (f32[5,4,2,8,512]{4,3,2,1,0:T(8,128)}, f32[5,4,2,8,512]{4,3,2,1,0:T(8,128)}, u32[]{:S(2)}, u32[]{:S(2)}) collective-permute-start(f32[5,4,2,8,512]{4,3,2,1,0:T(8,128)} %get-tuple-element.147), channel_id=1, source_target_pairs={{0,8},{8,0},{16,24},{24,16},{1,9},{9,1},{17,25},{25,17},{2,10},{10... | collective-permute-start | bytes 1966088 | tf_op jit(solution)/shard_map/ppermute | solution.py:866
  220.8 18.9 %collective-permute-start.63 = (f32[5,4,2,8,512]{4,3,2,1,0:T(8,128)}, f32[5,4,2,8,512]{4,3,2,1,0:T(8,128)}, u32[]{:S(2)}, u32[]{:S(2)}) collective-permute-start(f32[5,4,2,8,512]{4,3,2,1,0:T(8,128)} %get-tuple-element.149), channel_id=1, source_target_pairs={{0,16},{8,24},{16,0},{24,8},{1,17},{9,25},{17,1},{25,9},{2,18},{10... | collective-permute-start | bytes 1966088 | tf_op jit(solution)/shard_map/ppermute | solution.py:866
  228.5 25.7 %collective-permute-start.69 = (f32[4,4,2,8,512]{4,3,2,1,0:T(8,128)}, f32[4,4,2,8,512]{4,3,2,1,0:T(8,128)}, u32[]{:S(2)}, u32[]{:S(2)}) collective-permute-start(f32[4,4,2,8,512]{4,3,2,1,0:T(8,128)} %get-tuple-element.164), channel_id=1, source_target_pairs={{0,8},{8,0},{16,24},{24,16},{1,9},{9,1},{17,25},{25,17},{2,10},{10... | collective-permute-start | bytes 1572872 | tf_op jit(solution)/shard_map/ppermute | solution.py:866
  229.6 24.7 %collective-permute-start.70 = (f32[4,4,2,8,512]{4,3,2,1,0:T(8,128)}, f32[4,4,2,8,512]{4,3,2,1,0:T(8,128)}, u32[]{:S(2)}, u32[]{:S(2)}) collective-permute-start(f32[4,4,2,8,512]{4,3,2,1,0:T(8,128)} %get-tuple-element.166), channel_id=1, source_target_pairs={{0,16},{8,24},{16,0},{24,8},{1,17},{9,25},{17,1},{25,9},{2,18},{10... | collective-permute-start | bytes 1572872 | tf_op jit(solution)/shard_map/ppermute | solution.py:866
  237.0 31.0 %collective-permute-start.53 = (f32[4,5,2,8,512]{4,3,2,1,0:T(8,128)}, f32[4,5,2,8,512]{4,3,2,1,0:T(8,128)}, u32[]{:S(2)}, u32[]{:S(2)}) collective-permute-start(f32[4,5,2,8,512]{4,3,2,1,0:T(8,128)} %get-tuple-element.132), channel_id=1, source_target_pairs={{0,8},{8,0},{16,24},{24,16},{1,9},{9,1},{17,25},{25,17},{2,10},{10... | collective-permute-start | bytes 1966088 | tf_op jit(solution)/shard_map/ppermute | solution.py:866
  238.4 30.7 %collective-permute-start.54 = (f32[4,5,2,8,512]{4,3,2,1,0:T(8,128)}, f32[4,5,2,8,512]{4,3,2,1,0:T(8,128)}, u32[]{:S(2)}, u32[]{:S(2)}) collective-permute-start(f32[4,5,2,8,512]{4,3,2,1,0:T(8,128)} %get-tuple-element.134), channel_id=1, source_target_pairs={{0,16},{8,24},{16,0},{24,8},{1,17},{9,25},{17,1},{25,9},{2,18},{10... | collective-permute-start | bytes 1966088 | tf_op jit(solution)/shard_map/ppermute | solution.py:866
  245.7 27.5 %collective-permute-start.64 = (f32[5,4,8,512]{3,2,1,0:T(8,128)}, f32[5,4,8,512]{3,2,1,0:T(8,128)}, u32[]{:S(2)}, u32[]{:S(2)}) collective-permute-start(f32[5,4,8,512]{3,2,1,0:T(8,128)} %get-tuple-element.151), channel_id=1, source_target_pairs={{0,16},{8,24},{16,0},{24,8},{1,17},{9,25},{17,1},{25,9},{2,18},{10... | collective-permute-start | bytes 983048 | tf_op jit(solution)/shard_map/ppermute | solution.py:866
  259.1 22.0 %collective-permute-start.71 = (f32[4,4,8,512]{3,2,1,0:T(8,128)S(1)}, f32[4,4,8,512]{3,2,1,0:T(8,128)S(1)}, u32[]{:S(2)}, u32[]{:S(2)}) collective-permute-start(f32[4,4,8,512]{3,2,1,0:T(8,128)S(1)} %get-tuple-element.168), channel_id=1, source_target_pairs={{0,16},{8,24},{16,0},{24,8},{1,17},{9,25},{17,1},{25,9},{2,18},{10... | collective-permute-start | bytes 786440 | tf_op jit(solution)/shard_map/ppermute | solution.py:866
  259.8 21.3 %collective-permute-start.72 = (f32[4,4,8,512]{3,2,1,0:T(8,128)S(1)}, f32[4,4,8,512]{3,2,1,0:T(8,128)S(1)}, u32[]{:S(2)}, u32[]{:S(2)}) collective-permute-start(f32[4,4,8,512]{3,2,1,0:T(8,128)S(1)} %get-tuple-element.170), channel_id=1, source_target_pairs={{0,8},{8,0},{16,24},{24,16},{1,9},{9,1},{17,25},{25,17},{2,10},{10... | collective-permute-start | bytes 786440 | tf_op jit(solution)/shard_map/ppermute | solution.py:866
  282.3 12.0 %collective-permute-start.73 = (f32[4,2,16,512]{3,2,1,0:T(8,128)S(1)}, f32[4,2,16,512]{3,2,1,0:T(8,128)S(1)}, u32[]{:S(2)}, u32[]{:S(2)}) collective-permute-start(f32[4,2,16,512]{3,2,1,0:T(8,128)S(1)} %get-tuple-element.172), channel_id=1, source_target_pairs={{0,2},{1,3},{2,0},{3,1},{4,6},{5,7},{6,4},{7,5},{8,10},{9,11},{10,... | collective-permute-start | bytes 786440 | tf_op jit(solution)/shard_map/ppermute | solution.py:866
  283.5 20.8 %collective-permute-start.57 = (f32[4,2,16,512]{3,2,1,0:T(8,128)S(1)}, f32[4,2,16,512]{3,2,1,0:T(8,128)S(1)}, u32[]{:S(2)}, u32[]{:S(2)}) collective-permute-start(f32[4,2,16,512]{3,2,1,0:T(8,128)S(1)} %get-tuple-element.141), channel_id=1, source_target_pairs={{0,2},{1,3},{2,0},{3,1},{4,6},{5,7},{6,4},{7,5},{8,10},{9,11},{10,... | collective-permute-start | bytes 786440 | tf_op jit(solution)/shard_map/ppermute | solution.py:866
  289.7 12.4 %collective-permute-start.67 = (f32[5,1,16,512]{3,2,0,1:T(8,128)S(1)}, f32[5,1,16,512]{3,2,0,1:T(8,128)S(1)}, u32[]{:S(2)}, u32[]{:S(2)}) collective-permute-start(f32[5,1,16,512]{3,2,0,1:T(8,128)S(1)} %bitcast.142), channel_id=1, source_target_pairs={{0,6},{1,7},{2,4},{3,5},{4,2},{5,3},{6,0},{7,1},{8,14},{9,15},{10,... | collective-permute-start | bytes 491528 | tf_op jit(solution)/shard_map/ppermute | solution.py:866
  302.8 12.9 %collective-permute-start.77 = (f32[9,16,512]{2,1,0:T(8,128)S(1)}, f32[9,16,512]{2,1,0:T(8,128)S(1)}, u32[]{:S(2)}, u32[]{:S(2)}) collective-permute-start(f32[9,16,512]{2,1,0:T(8,128)S(1)} %get-tuple-element.175.refs_0_), channel_id=1, source_target_pairs={{0,24},{8,16},{16,8},{24,0},{1,25},{9,17},{17,9},{25,1},{2,26},{10... | collective-permute-start | bytes 884744 | tf_op jit(solution)/shard_map/ppermute | solution.py:866
  307.7 13.7 %collective-permute-start.76 = (f32[9,16,512]{2,1,0:T(8,128)S(1)}, f32[9,16,512]{2,1,0:T(8,128)S(1)}, u32[]{:S(2)}, u32[]{:S(2)}) collective-permute-start(f32[9,16,512]{2,1,0:T(8,128)S(1)} %get-tuple-element.175.refs_0_), channel_id=1, source_target_pairs={{0,16},{8,24},{16,0},{24,8},{1,17},{9,25},{17,1},{25,9},{2,18},{10... | collective-permute-start | bytes 884744 | tf_op jit(solution)/shard_map/ppermute | solution.py:866
  309.0 12.4 %collective-permute-start.75 = (f32[9,16,512]{2,1,0:T(8,128)S(1)}, f32[9,16,512]{2,1,0:T(8,128)S(1)}, u32[]{:S(2)}, u32[]{:S(2)}) collective-permute-start(f32[9,16,512]{2,1,0:T(8,128)S(1)} %get-tuple-element.175.refs_0_), channel_id=1, source_target_pairs={{0,8},{8,0},{16,24},{24,16},{1,9},{9,1},{17,25},{25,17},{2,10},{10... | collective-permute-start | bytes 884744 | tf_op jit(solution)/shard_map/ppermute | solution.py:866
  312.9 11.6 %collective-permute-start.61 = (f32[8,16,512]{2,1,0:T(8,128)S(1)}, f32[8,16,512]{2,1,0:T(8,128)S(1)}, u32[]{:S(2)}, u32[]{:S(2)}) collective-permute-start(f32[8,16,512]{2,1,0:T(8,128)S(1)} %get-tuple-element.145.refs_0_), channel_id=1, source_target_pairs={{0,24},{8,16},{16,8},{24,0},{1,25},{9,17},{17,9},{25,1},{2,26},{10... | collective-permute-start | bytes 786440 | tf_op jit(solution)/shard_map/ppermute | solution.py:866
  314.4 11.9 %collective-permute-start.60 = (f32[8,16,512]{2,1,0:T(8,128)S(1)}, f32[8,16,512]{2,1,0:T(8,128)S(1)}, u32[]{:S(2)}, u32[]{:S(2)}) collective-permute-start(f32[8,16,512]{2,1,0:T(8,128)S(1)} %get-tuple-element.145.refs_0_), channel_id=1, source_target_pairs={{0,16},{8,24},{16,0},{24,8},{1,17},{9,25},{17,1},{25,9},{2,18},{10... | collective-permute-start | bytes 786440 | tf_op jit(solution)/shard_map/ppermute | solution.py:866
  315.7 10.6 %collective-permute-start.59 = (f32[8,16,512]{2,1,0:T(8,128)S(1)}, f32[8,16,512]{2,1,0:T(8,128)S(1)}, u32[]{:S(2)}, u32[]{:S(2)}) collective-permute-start(f32[8,16,512]{2,1,0:T(8,128)S(1)} %get-tuple-element.145.refs_0_), channel_id=1, source_target_pairs={{0,8},{8,0},{16,24},{24,16},{1,9},{9,1},{17,25},{25,17},{2,10},{10... | collective-permute-start | bytes 786440 | tf_op jit(solution)/shard_map/ppermute | solution.py:866
  (121 other events, 994.9 us)
Sparse Core Ops, SparseCore 0:
  79.9 75.8 all-gather.2
Sparse Core Ops, SparseCore 1:
  157.3 48.8 reduce-scatter.1

commit v3 on v2

--- a/solution.py
+++ b/solution.py
@@ -20,7 +20,7 @@
 
 
 def cost(flops, moved, special=0):
-    return pl.CostEstimate(flops=0, bytes_accessed=0, transcendentals=0)
+    return pl.CostEstimate(flops=int(flops), bytes_accessed=int(moved), transcendentals=int(special))
 
 
 class Part:
@@ -599,6 +599,61 @@
     )(*pres, gain, bias, embed_map, hidden_map, plain, normed_sums)
 
 
+def projector_weights(pooled_all, order_of, blk, gap, hp, gz, nblk, token):
+    blocks, slots, width = pooled_all.shape
+    rows, hidden = gap.shape
+    emb = gz.shape[1]
+    own, own_hidden = width // nblk, hidden // nblk
+    lanes = 256
+
+    def kernel(at_ref, p_ref, ga_ref, hp_ref, gz_ref, *refs):
+        o_ref, e_ref, mark, scr, high, low = refs[len(token) :]
+
+        @pl.when(pl.program_id(0) == 0)
+        def _():
+            mark[...] = jnp.zeros_like(mark)
+            for b in range(blocks):
+                scr[b * slots : (b + 1) * slots, :] = p_ref[at_ref[1 + b]]
+            h, m = split2(scr[...])
+            high[...] = h
+            low[...] = m
+            hh, hm = split2(hp_ref[...])
+            gh, gm = split2(gz_ref[...])
+            e_ref[...] = mm_tn(hh, gh) + (mm_tn(hh, gm) + mm_tn(hm, gh))
+
+        gh, gm = split2(ga_ref[...])
+        o_ref[...] = mm_tn(high[...], gh) + (mm_tn(high[...], gm) + mm_tn(low[...], gh))
+
+    return pl.pallas_call(
+        kernel,
+        grid_spec=pltpu.PrefetchScalarGridSpec(
+            num_scalar_prefetch=1,
+            grid=(hidden // lanes,),
+            in_specs=[
+                pl.BlockSpec((blocks, slots, own), lambda j, at: (0, 0, at[0])),
+                pl.BlockSpec((rows, lanes), lambda j, at: (0, j)),
+                pl.BlockSpec((rows, own_hidden), lambda j, at: (0, at[0])),
+                pl.BlockSpec((rows, emb), lambda j, at: (0, 0)),
+            ]
+            + [pl.BlockSpec((8, 128), lambda j, at: (0, 0))] * len(token),
+            out_specs=[
+                pl.BlockSpec((own, lanes), lambda j, at: (0, j)),
+                pl.BlockSpec((own_hidden, emb), lambda j, at: (0, 0)),
+                pl.BlockSpec((8, 128), lambda j, at: (0, 0)),
+            ],
+            scratch_shapes=[pltpu.VMEM((rows, own), F32), pltpu.VMEM((rows, own), BF16), pltpu.VMEM((rows, own), BF16)],
+        ),
+        out_shape=(
+            jax.ShapeDtypeStruct((own, hidden), F32),
+            jax.ShapeDtypeStruct((own_hidden, emb), F32),
+            MARK,
+        ),
+        compiler_params=params(58),
+        cost_estimate=cost(2 << 30, 16 << 20),
+        name="projector_weights",
+    )(jnp.concatenate([blk[None], order_of]).astype(jnp.int32), pooled_all, gap, hp, gz, *token)
+
+
 def halves(value, core, send, keep):
     for mine in range(2):
 
@@ -760,7 +815,7 @@
         + (MARK,),
         scratch_shapes=[pltpu.VMEM(turned_shape(order, chan), F32), pltpu.VMEM((rows, chan), BF16)],
         compiler_params=params(14),
-        cost_estimate=cost(2 * rows * chan * chan * count, 2 << 20),
+        cost_estimate=cost(2 * rows * chan * chan * count, 12 << 20),
         name="middle_weight",
     )(where, hidden_one, grad, *hold, *token)
 
@@ -843,7 +898,7 @@
         out_specs=out_specs + [whole(8, 128)],
         out_shape=(*out_shape, MARK),
         compiler_params=params(18),
-        cost_estimate=cost(2 * rows * width * chan, 14 << 20),
+        cost_estimate=cost(2 * rows * width * chan, 16 << 20),
         name="input_grads",
     )(slope, share, grad_first, conv_in, *token)
 
@@ -933,7 +988,7 @@
         out_specs=[unit(x) for x in outs] + kept + [whole(8, 128)],
         out_shape=[jax.ShapeDtypeStruct(x, F32) for x in outs] + [jax.ShapeDtypeStruct(h.shape, F32) for h in hold] + [MARK],
         compiler_params=params(12),
-        cost_estimate=cost(0, 0),
+        cost_estimate=cost(0, 8 << 20),
         name=name,
     )(where, *ins, *hold, *token)
     return result[:outs_n], result[outs_n:-1], result[-1]
@@ -1023,7 +1078,7 @@
         out_specs=[whole(*shape)] * 2 + [whole(8, 128)] + [whole(*x) for x in whole_shape],
         out_shape=[jax.ShapeDtypeStruct(shape, F32)] * 2 + [MARK] + [jax.ShapeDtypeStruct(x, F32) for x in whole_shape],
         compiler_params=params(14),
-        cost_estimate=cost(0, 0),
+        cost_estimate=cost(0, 8 << 20),
         name="fold_far_first",
     )(where, *ins, *token)
 
@@ -1047,27 +1102,56 @@
         out_specs=[whole(*shape)] * 2 + [whole(8, 128)],
         out_shape=[jax.ShapeDtypeStruct(shape, F32)] * 2 + [MARK],
         compiler_params=params(12),
-        cost_estimate=cost(0, 0),
+        cost_estimate=cost(0, 8 << 20),
         name="fold_far",
     )(where, keep, got, *token)
 
 
-def place(pieces, where):
+def place(pieces, where, side=0):
     t, r, n = pieces[0].shape
     count = len(pieces)
+    rest = t - side
 
     def kernel(at_ref, *refs):
         for k in range(count):
-            refs[-1][:, at_ref[1] ^ k] = refs[k][...]
-
-    return pl.pallas_call(
+            to = at_ref[1] ^ k
+            refs[count][:, to] = refs[k][0:rest]
+            for u in range(side):
+                refs[-1][to, :, u * n : (u + 1) * n] = refs[k][rest + u]
+
+    shapes = [(rest, count, r, n)] + ([(count, r, side * n)] if side else [])
+    out = pl.pallas_call(
         kernel,
         in_specs=[SMEM] + [whole(t, r, n)] * count,
-        out_specs=whole(t, count, r, n),
-        out_shape=jax.ShapeDtypeStruct((t, count, r, n), F32),
-        compiler_params=params(8),
+        out_specs=[whole(*x) for x in shapes],
+        out_shape=[jax.ShapeDtypeStruct(x, F32) for x in shapes],
+        compiler_params=params(12),
         name="place",
     )(where, *pieces)
+    first = out[0].reshape(rest, count * r, n)
+    return (first, out[1].reshape(count * r, side * n)) if side else first
+
+
+def place_taps(pieces, where, first, taps, before=None):
+    t, r, n = pieces[0].shape
+    count = len(pieces)
+
+    def kernel(at_ref, *refs):
+        for k in range(count):
+            refs[-2][0, at_ref[1] ^ k] = refs[k][0]
+        refs[-1][...] = jnp.zeros((8, 128), F32)
+
+    kept = [] if before is None else [before]
+    return pl.pallas_call(
+        kernel,
+        grid=(t,),
+        in_specs=[SMEM] + [pl.BlockSpec((1, r, n), lambda i: (i, 0, 0))] * count + [ANY] * len(kept),
+        out_specs=[pl.BlockSpec((1, count, r, n), lambda i: (i + first, 0, 0, 0)), whole(8, 128)],
+        out_shape=[jax.ShapeDtypeStruct((taps, count, r, n), F32), MARK],
+        input_output_aliases={1 + count: 0} if kept else {},
+        compiler_params=params(8),
+        name="place_taps",
+    )(where, *pieces, *kept)
 
 
 def total_of(groups, token):
@@ -1093,6 +1177,7 @@
         out_specs=[whole(total, r, n), whole(8, 128)],
         out_shape=[jax.ShapeDtypeStruct((total, r, n), F32), MARK],
         compiler_params=params(8),
+        cost_estimate=cost(0, 3 << 20),
         name="total_of",
     )(*ins, *token)
 
@@ -1149,10 +1234,6 @@
         out, self.mark = total_of([p.sums if isinstance(p, Spread) else [p] for p in parts], token)
         self.pieces = [out] + [swap(out, "dp", k) for k in range(1, lax.axis_size("dp"))]
 
-    def last(self):
-        t, r, n = self.pieces[0].shape
-        return place(self.pieces, self.where).reshape(t, len(self.pieces) * r, n)
-
 
 def share_sum(local, where):
     nblk, rows, n = local.shape
@@ -1163,7 +1244,7 @@
     whole_sum.second()
     out = Spread([whole_sum])
     out.far()
-    return Gather([out]).last()[0]
+    return place(Gather([out]).pieces, where)[0]
 
 
 def projector_spread(order, pre, gain, bias, embed_map, hidden_map, plain, normed_sums, crop_total):
@@ -1288,45 +1369,41 @@
         order, grad_one, in_back, total, first_pre, in_sums, row(gain_in), inputs, where, nblk, []
     )
     i = Reduce(send, keep, mark, "both", where, out_part)
-    m1 = Reduce(*middle_weight(order, hidden_one, grad_second, where, nblk, (5, 4), []), "both", where)
-    i.first()
-    *grads, mark = input_grads(parts, order, slope, share, grad_first, conv_in, [i.mark])
-    m0.second()
-    m1.first()
-
+    m0.second([mark])
+    m1 = Reduce(*middle_weight(order, hidden_one, grad_second, where, nblk, (5, 4), [m0.mark]), "both", where)
+    i.first([m1.mark])
+    far0 = Spread([m0], [i.mark])
     high = lax.Precision.HIGH
     if small:
-        own = width // nblk
-        pooled_own = lax.dynamic_slice_in_dim(pooled_all, blk * own, own, 2)[number].reshape(devices * slots, own)
-        hidden_grad = lax.dot_general(pooled_own, gap, (((0,), (0,)), ((), ())), precision=high)
-        own = hidden // nblk
-        embed_grad = lax.dot_general(
-            lax.dynamic_slice_in_dim(hp, blk * own, own, 1), gz, (((0,), (0,)), ((), ())), precision=high
+        hidden_grad, embed_grad, mark = projector_weights(
+            pooled_all, number, blk, gap, hp, gz, nblk, [far0.mark]
         )
     else:
         local = lax.dot_general(pooled[:crops], gap, (((0,), (0,)), ((), ())), precision=high)
         hidden_grad = share_sum(local.reshape(nblk, width // nblk, hidden), where)
         local = lax.dot_general(hp, gz, (((0,), (0,)), ((), ())), precision=high)
         embed_grad = share_sum(local.reshape(nblk, hidden // nblk, emb), where)
-
-    i.second([mark])
-    last = Spread([i], [])
-    far0 = Spread([m0], [mark_of(hidden_grad), mark_of(embed_grad)])
-    m1.second()
-    last.far()
-    far0.far()
-    far1 = Spread([m1], [])
-    early = Gather([last, last.extra], [])
-    far1.far()
-    late = Gather([far0, far1], [])
-    early = early.last()
-    conv_in_grad, out_grad = early[0:4].reshape(width // nblk, chan), early[4:8]
-    out_grad = jnp.concatenate(list(out_grad), axis=1)
-    mid_grad = late.last()
+    m1.first([mark])
+    far0.far([m1.mark])
+    *grads, mark = input_grads(parts, order, slope, share, grad_first, conv_in, [far0.mark])
     grads = [
         g if p.by_column else jnp.transpose(g.reshape(p.side, p.side, 8, width), (2, 0, 1, 3))
         for g, p in zip(grads, parts)
     ]
+    i.second([mark])
+    m1.second([i.mark])
+    early = Gather([far0], [m1.mark])
+    last = Spread([i], [early.mark])
+    far1 = Spread([m1], [last.mark])
+    taps = m0.keep.shape[0] + m1.keep.shape[0]
+    mid_grad, mark = place_taps(early.pieces, where, 0, taps)
+    last.far([far1.mark, mark])
+    far1.far([last.mark])
+    middle = Gather([last, last.extra], [far1.mark])
+    late = Gather([far1], [middle.mark])
+    conv_in_grad, out_grad = place(middle.pieces, where, 4)
+    conv_in_grad = conv_in_grad.reshape(width // nblk, chan)
+    mid_grad, _ = place_taps(late.pieces, where, m0.keep.shape[0], taps, mid_grad)
     return (
         *grads,
         conv_in_grad,

time: 337 us -> 323 us (0.958)
  local copies, waits for them, and re-layouts: 46.9 us -> 34.8 us
  starting transfers between devices: 88.8 us -> 95.6 us
  waiting for transfers between devices: 69 us -> 65 us
    pallas_call x0 -> x3, Pallas kernels: none -> 11 us  [the longest x1 6.51 us: projector_weights(): pl.pallas_call(kernel, grid_spec=pltpu.PrefetchScalarGridSpec(num_scalar_...]
    ppermute x78 -> x81, starting transfers between devices: 88.7 us -> 95.5 us  [swap(): return lax.ppermute(x, axis, [(i, i ^ mask) for i in range(size)])]
    unnamed x130 -> x104, local copies, waits for them, and re-layouts: 38.5 us -> 31.7 us
    pallas_call x6, Pallas kernels: 19.7 us -> 13.9 us  [fold(): pl.pallas_call(whole_kernel, grid=(count,), in_specs=[SMEM] + [unit(x.sha...]
    ppermute x78 -> x81, waiting for transfers between devices: 68.9 us -> 64.9 us  [swap(): return lax.ppermute(x, axis, [(i, i ^ mask) for i in range(size)])]
  transfers between devices with their start and end apart: 80 -> 83, of which waited for: 50 -> 56; matrix products, arithmetic and copies ran while one was open for 3% -> 1% of each run, Pallas kernels for 27% -> 28%
where the time goes in v3:
time: 323 us; the launch traced here: 322 us
  Pallas kernels  111 us (34%)
  starting transfers between devices  95.6 us (30%)
  waiting for transfers between devices  65 us (20%)
  local copies, waits for them, and re-layouts  34.8 us (11%)
  between operations  16.1 us (5%)
    ppermute x81, starting transfers between devices, swap(): return lax.ppermute(x, axis, [(i, i ^ mask) for i in range(size)])  95.5 us
    ppermute x81, waiting for transfers between devices, swap(): return lax.ppermute(x, axis, [(i, i ^ mask) for i in range(size)])  64.9 us
    unnamed x104, local copies, waits for them, and re-layouts  31.7 us
    pallas_call x1, Pallas kernels, projector(): pl.pallas_call(kernel, out_shape=(jax.ShapeDtypeStruct((rows_all, hidden)...  17.3 us
    pallas_call x6, Pallas kernels, fold(): pl.pallas_call(whole_kernel, grid=(count,), in_specs=[SMEM] + [unit(x.sha...  13.9 us
    pallas_call x2, Pallas kernels, middle_weight(): pl.pallas_call(kernel, grid=(count,), in_specs=[SMEM, whole(slabs, 8, cha...  10.9 us
    pallas_call x1, Pallas kernels, last_back(): pl.pallas_call(kernel, grid=(steps,), in_specs=[lanes_of(block, rows), la...  10.3 us
    pallas_call x1, Pallas kernels, pool_embed(): pl.pallas_call(kernel, grid=(steps,), in_specs=[lanes_of(block, rows), la...  6.96 us
  transfers between devices with their start and end apart: 83, of which 56 were waited for; matrix products, arithmetic and copies ran while one was open for 1% of the time, Pallas kernels for 28%

profile of v3, /device:TPU:0, one launch (start us, length us, event | category | flops | bytes accessed | tf_op | source)
XLA Modules:
  0.0 322.4 jit_solution(11000819764243589152)
XLA Ops:
  13.5 4.0 %first_conv.1 = (bf16[880,2048]{1,0:T(8,128)(2,1)S(1)}, f32[880,512]{1,0:T(8,128)S(1)}, f32[2,512]{1,0:T(2,128)S(1)}) custom-call(bf16[49,8,2048]{2,1,0:T(8,128)(2,1)S(1)} %bitcast.128, bf16[6,6,6,2048]{3,2,1,0:T(8,128)(2,1)S(1)} %copy-done.41, bf16[25,8,2048]{2,1,0:T(8,128)(2,1)S(1)} %bitcast.129, bf16[2048,512]{1,0:T(8,128)(2,1)S(1)} %copy-done.36), custom_call_target="tpu_custom_call" | custom-call | flops 1845493760 | bytes 10485760 | tf_op jit(solution)/shard_map/first_conv/pallas_call | solution.py:183
  18.8 3.8 %collective-permute-start.3 = (f32[2,512]{1,0:T(2,128)S(1)}, f32[2,512]{1,0:T(2,128)S(1)}, u32[]{:S(2)}, u32[]{:S(2)}) collective-permute-start(f32[2,512]{1,0:T(2,128)S(1)} %add.243), channel_id=1, source_target_pairs={{0,24},{8,16},{16,8},{24,0},{1,25},{9,17},{17,9},{25,1},{2,26},{10... | collective-permute-start | bytes 12296 | tf_op jit(solution)/shard_map/ppermute | solution.py:921
  26.7 3.6 %collective-permute-start.6 = (f32[2,512]{1,0:T(2,128)S(1)}, f32[2,512]{1,0:T(2,128)S(1)}, u32[]{:S(2)}, u32[]{:S(2)}) collective-permute-start(f32[2,512]{1,0:T(2,128)S(1)} %add_add_fusion.10), channel_id=1, source_target_pairs={{0,6},{1,7},{2,4},{3,5},{4,2},{5,3},{6,0},{7,1},{8,14},{9,15},{10,... | collective-permute-start | bytes 12296 | tf_op jit(solution)/shard_map/ppermute | solution.py:921
  32.1 2.7 collective-permute-done.5
  34.9 4.4 %middle_conv.1 = (f32[110,8,512]{2,1,0:T(8,128)S(1)}, f32[880,512]{1,0:T(8,128)S(1)}, f32[2,512]{1,0:T(2,128)S(1)}) custom-call(f32[880,512]{1,0:T(8,128)S(1)} %get-tuple-element.120.a_ref.f_ref, f32[2,512]{1,0:T(2,128)S(1)} %add_add_fusion.9.st_ref.is_ref, f32[1,512]{1,0:T(1,128)S(1)} %bitcast.118, f32[1,512]{1,0:T(1,128)S(1)} %bitcast.135, ...), custom_call_target="tpu_custom_call" | custom-call | flops 4152360960 | bytes 20971520 | tf_op jit(solution)/shard_map/middle_conv/pallas_call | solution.py:257
  53.4 3.8 %last_conv.1 = (bf16[880,512]{1,0:T(8,128)(2,1)S(1)}, f32[880,2048]{1,0:T(8,128)S(1)}, f32[2,2048]{1,0:T(2,128)S(1)}) custom-call(f32[880,512]{1,0:T(8,128)S(1)} %get-tuple-element.122.a_ref.m_ref, f32[2,512]{1,0:T(2,128)S(1)} %add_add_fusion.7.st_ref.ms_ref, f32[1,512]{1,0:T(1,128)S(1)} %bitcast.123, f32[1,512]{1,0:T(1,128)S(1)} %bitcast.121, ...), custom_call_target="tpu_custom_call" | custom-call | flops 1845493760 | bytes 12582912 | tf_op jit(solution)/shard_map/last_conv/pallas_call | solution.py:294
  72.7 7.0 %pool_embed.1 = (f32[24,2048]{1,0:T(8,128)}, f32[24,1024]{1,0:T(8,128)S(1)}) custom-call(f32[880,2048]{1,0:T(8,128)S(1)} %get-tuple-element.124.a_ref, f32[2,2048]{1,0:T(2,128)S(1)} %add_add_fusion.2.st_ref, f32[1,2048]{1,0:T(1,128)S(1)} %bitcast.112, f32[1,2048]{1,0:T(1,128)S(1)} %bitcast.115, bf16[880,2048]{1,0:T(8,128)(2,1)S(1)} %get-tuple-element.126.x_ref, ...), custom_call_target="tpu_custom_call" | custom-call | flops 402653184 | bytes 16777216 | tf_op jit(solution)/shard_map/pool_embed/pallas_call | solution.py:348
  84.9 3.3 %collective-permute-done.22.refs_2_ = f32[1,24,1024]{2,1,0:T(8,128)S(1)} collective-permute-done((f32[1,24,1024]{2,1,0:T(8,128)S(1)}, f32[1,24,1024]{2,1,0:T(8,128)S(1)}, u32[]{:S(2)}, u32[]{:S(2)}) %collective-permute-start.22) | collective-permute-done | bytes 98336 | tf_op jit(solution)/shard_map/ppermute | solution.py:921
  91.8 3.1 copy-done.1
  96.9 6.2 %slope_sums.1 = (bf16[880,2048]{1,0:T(8,128)(2,1)S(1)}, f32[24,2048]{1,0:T(8,128)S(1)}, f32[24,2048]{1,0:T(8,128)S(1)}, f32[4,24,1024]{2,1,0:T(8,128)S(1)}) custom-call(f32[880,2048]{1,0:T(8,128)S(1)} %copy-done.1, f32[2,2048]{1,0:T(2,128)S(1)} %add_add_fusion.2.st_ref, f32[1,2048]{1,0:T(1,128)S(1)} %bitcast.113, f32[1,2048]{1,0:T(1,128)S(1)} %bitcast.116, ...), custom_call_target="tpu_custom_call" | custom-call | flops 43253760 | bytes 14417920 | tf_op jit(solution)/shard_map/slope_sums/pallas_call | solution.py:386
  107.4 17.3 %projector.1 = (f32[768,1024]{1,0:T(8,128)S(1)}, f32[768,1024]{1,0:T(8,128)S(1)}, f32[768,128]{1,0:T(8,128)S(1)}, f32[1,1024]{1,0:T(1,128)}, f32[1,1024]{1,0:T(1...) custom-call(f32[4,24,1024]{2,1,0:T(8,128)S(1)} %get-tuple-element.129.refs_0_, ...), custom_call_target="tpu_custom_call" | custom-call | flops 10737418240 | bytes 20971520 | tf_op jit(solution)/shard_map/projector/pallas_call | solution.py:577
  144.3 10.3 %last_back.1 = (f32[880,512]{1,0:T(8,128)S(1)}, f32[2,512]{1,0:T(2,128)S(1)}, f32[512,2048]{1,0:T(8,128)}) custom-call(bf16[880,2048]{1,0:T(8,128)(2,1)S(1)} %get-tuple-element.128.s_ref, f32[24,2048]{1,0:T(8,128)S(1)} %get-tuple-element.132.e_ref, f32[880,2048]{1,0:T(8,128)} %copy-done, f32[2,2048]{1,0:T(2,128)S(1)} %add_add_fusion.2.st_ref, ...), custom_call_target="tpu_custom_call" | custom-call | flops 3690987520 | bytes 25165824 | tf_op jit(solution)/shard_map/last_back/pallas_call | solution.py:706
  162.7 2.8 collective-permute-start.44
  176.3 6.0 %middle_back.1 = (bf16[880,512]{1,0:T(8,128)(2,1)S(1)}, f32[880,512]{1,0:T(8,128)S(1)}, f32[2,512]{1,0:T(2,128)S(1)}) custom-call(f32[880,512]{1,0:T(8,128)S(1)} %copy-done.39, f32[2,512]{1,0:T(2,128)S(1)} %add_add_fusion.5.gs_ref, f32[880,512]{1,0:T(8,128)S(1)} %copy-done.18, f32[2,512]{1,0:T(2,128)S(1)} %add_add_fusion.7.st_ref.ms_ref, ...), custom_call_target="tpu_custom_call" | custom-call | flops 4152360960 | bytes 20971520 | tf_op jit(solution)/shard_map/middle_back/pallas_call | solution.py:756
  183.5 5.8 %middle_weight.2 = (f32[5,4,64,512]{3,2,1,0:T(8,128)S(1)}, f32[5,4,64,512]{3,2,1,0:T(8,128)S(1)}, f32[2,512]{1,0:T(2,128)S(1)}, f32[8,128]{1,0:T(8,128)}) custom-call(s32[3]{0:T(128)S(1)} %pad_add_fusion.at_ref, f32[110,8,512]{2,1,0:T(8,128)S(1)} %copy-done.50, bf16[880,512]{1,0:T(8,128)(2,1)S(1)} %get-tuple-element.140.g_ref, f32[2,512]{1,0:T(2,128)S(1)} %add.282.refs_0_), custom_call_target="tpu_custom_call" | custom-call | flops 2306867200 | bytes 12582912 | tf_op jit(solution)/shard_map/middle_weight/pallas_call | solution.py:808
  207.4 5.3 %first_back.1 = (bf16[880,512]{1,0:T(8,128)(2,1)S(1)}, f32[4,4,64,512]{3,2,1,0:T(8,128)}, f32[4,4,64,512]{3,2,1,0:T(8,128)S(1)}, f32[8,128]{1,0:T(8,128)S(1)}) custom-call(s32[3]{0:T(128)S(1)} %pad_add_fusion.at_ref, f32[880,512]{1,0:T(8,128)S(1)} %get-tuple-element.138.gq_ref, f32[2,512]{1,0:T(2,128)S(1)} %add.287.gs_ref, f32[880,512]{1,0:T(8,128)S(1)} %copy-done.15, ...), custom_call_target="tpu_custom_call" | custom-call | flops 1845493760 | bytes 10485760 | tf_op jit(solution)/shard_map/first_back/pallas_call | solution.py:849
  218.6 5.1 %middle_weight.3 = (f32[4,4,64,512]{3,2,1,0:T(8,128)}, f32[4,4,64,512]{3,2,1,0:T(8,128)S(1)}, f32[8,128]{1,0:T(8,128)S(1)}) custom-call(s32[3]{0:T(128)S(1)} %pad_add_fusion.at_ref, f32[110,8,512]{2,1,0:T(8,128)S(1)} %copy-done.50, bf16[880,512]{1,0:T(8,128)(2,1)S(1)} %get-tuple-element.140.g_ref, f32[8,128]{1,0:T(8,128)S(1)} %get-tuple-element.159.refs_0_), custom_call_target="tpu_custom_call" | custom-call | flops 1845493760 | bytes 12582912 | tf_op jit(solution)/shard_map/middle_weight/pallas_call | solution.py:808
  229.2 3.7 %fold_first.4 = (f32[4,5,2,8,512]{4,3,2,1,0:T(8,128)}, f32[4,5,2,8,512]{4,3,2,1,0:T(8,128)S(1)}, f32[4,5,2,8,512]{4,3,2,1,0:T(8,128)}, f32[4,5,2,8,512]{4,3,2,1,0:T(8,128)S(1)}, f32[8,128]{1,0:T(8,128)S(1)}) custom-call(s32[3]{0:T(128)S(1)} %pad_add_fusion.at_ref, f32[4,4,4,16,512]{4,3,2,1,0:T(8,128)S(1)} %bitcast.96, ...), custom_call_target="tpu_custom_call" | custom-call | bytes 8388608 | tf_op jit(solution)/shard_map/fold_first/pallas_call | solution.py:984
  239.6 6.5 %projector_weights.1 = (f32[256,1024]{1,0:T(8,128)}, f32[128,128]{1,0:T(8,128)}, f32[8,128]{1,0:T(8,128)}) custom-call(s32[33]{0:T(128)} %concatenate.7.at_ref, f32[32,24,2048]{2,1,0:T(8,128)} %bitcast.137, f32[768,1024]{1,0:T(8,128)} %copy-done.10, f32[768,1024]{1,0:T(8,128)} %copy-done.9, f32[768,128]{1,0:T(8,128)} %copy-done.20, f32[8,128]{1,0:T(8,128)} %copy-done.30), custom_call_target="tpu_custom_call" | custom-call | flops 2147483648 | bytes 16777216 | tf_op jit(solution)/shard_map/projector_weights/pallas_call | solution.py:627
  246.8 3.0 fold_first.5
  253.9 4.4 %input_grads.1 = (f32[49,8,2048]{2,1,0:T(8,128)}, f32[6,6,6,2048]{3,2,1,0:T(8,128)}, f32[25,8,2048]{2,1,0:T(8,128)}, f32[8,128]{1,0:T(8,128)S(1)}) custom-call(bf16[880,2048]{1,0:T(8,128)(2,1)S(1)} %copy-done.8, f32[24,2048]{1,0:T(8,128)S(1)} %copy-done.26, bf16[880,512]{1,0:T(8,128)(2,1)S(1)} %copy-done.43, bf16[2048,512]{1,0:T(8,128)(2,1)S(1)} %copy-done.37, ...), custom_call_target="tpu_custom_call" | custom-call | flops 1845493760 | bytes 16777216 | tf_op jit(solution)/shard_map/input_grads/pallas_call | solution.py:893
  286.0 3.7 %collective-permute-start.72 = (f32[4,1,16,512]{3,2,0,1:T(8,128)S(1)}, f32[4,1,16,512]{3,2,0,1:T(8,128)S(1)}, u32[]{:S(2)}, u32[]{:S(2)}) collective-permute-start(f32[4,1,16,512]{3,2,0,1:T(8,128)S(1)} %bitcast.132), channel_id=1, source_target_pairs={{0,6},{1,7},{2,4},{3,5},{4,2},{5,3},{6,0},{7,1},{8,14},{9,15},{10,... | collective-permute-start | bytes 393224 | tf_op jit(solution)/shard_map/ppermute | solution.py:921
  297.2 3.5 %collective-permute-start.77 = (f32[4,1,16,512]{3,2,0,1:T(8,128)S(1)}, f32[4,1,16,512]{3,2,0,1:T(8,128)S(1)}, u32[]{:S(2)}, u32[]{:S(2)}) collective-permute-start(f32[4,1,16,512]{3,2,0,1:T(8,128)S(1)} %bitcast.131), channel_id=1, source_target_pairs={{0,6},{1,7},{2,4},{3,5},{4,2},{5,3},{6,0},{7,1},{8,14},{9,15},{10,... | collective-permute-start | bytes 393224 | tf_op jit(solution)/shard_map/ppermute | solution.py:921
  301.3 2.8 collective-permute-done.77
  (309 shorter events, 184.4 us)
Async XLA Ops:
  8.0 162.2 %all-gather.3.cloned.1.call-start = ((), (), s32[]{:S(2)}) async-start(), calls=%async_computation.2 | async-start | bytes 6488064 | tf_op jit(solution)/shard_map/all_gather | solution.py:1355
  79.7 146.8 %reduce-scatter.2.cloned.1.call-start = ((), (), s32[]{:S(2)}) async-start(), calls=%async_computation.1 | async-start | bytes 4718592 | tf_op jit(solution)/shard_map/reduce_scatter | solution.py:1356
  88.3 15.0 %collective-permute-start.24 = (f32[4,24,1024]{2,1,0:T(8,128)S(1)}, f32[4,24,1024]{2,1,0:T(8,128)S(1)}, u32[]{:S(2)}, u32[]{:S(2)}) collective-permute-start(f32[4,24,1024]{2,1,0:T(8,128)S(1)} %bitcast.97), channel_id=1, source_target_pairs={{0,8},{8,0},{16,24},{24,16},{1,9},{9,1},{17,25},{25,17},{2,10},{10... | collective-permute-start | bytes 1179656 | tf_op jit(solution)/shard_map/ppermute | solution.py:921
  88.9 15.3 %collective-permute-start.25 = (f32[4,24,1024]{2,1,0:T(8,128)S(1)}, f32[4,24,1024]{2,1,0:T(8,128)S(1)}, u32[]{:S(2)}, u32[]{:S(2)}) collective-permute-start(f32[4,24,1024]{2,1,0:T(8,128)S(1)} %bitcast.98), channel_id=1, source_target_pairs={{0,16},{8,24},{16,0},{24,8},{1,17},{9,25},{17,1},{25,9},{2,18},{10... | collective-permute-start | bytes 1179656 | tf_op jit(solution)/shard_map/ppermute | solution.py:921
  90.4 15.2 %collective-permute-start.26 = (f32[4,24,1024]{2,1,0:T(8,128)S(1)}, f32[4,24,1024]{2,1,0:T(8,128)S(1)}, u32[]{:S(2)}, u32[]{:S(2)}) collective-permute-start(f32[4,24,1024]{2,1,0:T(8,128)S(1)} %bitcast.99), channel_id=1, source_target_pairs={{0,24},{8,16},{16,8},{24,0},{1,25},{9,17},{17,9},{25,1},{2,26},{10... | collective-permute-start | bytes 1179656 | tf_op jit(solution)/shard_map/ppermute | solution.py:921
  198.3 15.6 %collective-permute-start.52 = (f32[5,4,2,8,512]{4,3,2,1,0:T(8,128)S(1)}, f32[5,4,2,8,512]{4,3,2,1,0:T(8,128)S(1)}, u32[]{:S(2)}, u32[]{:S(2)}) collective-permute-start(f32[5,4,2,8,512]{4,3,2,1,0:T(8,128)S(1)} %get-tuple-element.148), channel_id=1, source_target_pairs={{0,8},{8,0},{16,24},{24,16},{1,9},{9,1},{17,25},{25,17},{2,10},{10... | collective-permute-start | bytes 1966088 | tf_op jit(solution)/shard_map/ppermute | solution.py:921
  198.3 16.2 %collective-permute-start.53 = (f32[5,4,2,8,512]{4,3,2,1,0:T(8,128)S(1)}, f32[5,4,2,8,512]{4,3,2,1,0:T(8,128)S(1)}, u32[]{:S(2)}, u32[]{:S(2)}) collective-permute-start(f32[5,4,2,8,512]{4,3,2,1,0:T(8,128)S(1)} %get-tuple-element.150), channel_id=1, source_target_pairs={{0,16},{8,24},{16,0},{24,8},{1,17},{9,25},{17,1},{25,9},{2,18},{10... | collective-permute-start | bytes 1966088 | tf_op jit(solution)/shard_map/ppermute | solution.py:921
  213.6 12.9 %collective-permute-start.56 = (f32[4,4,64,512]{3,2,1,0:T(8,128)}, f32[4,4,64,512]{3,2,1,0:T(8,128)}, u32[]{:S(2)}, u32[]{:S(2)}) collective-permute-start(f32[4,4,64,512]{3,2,1,0:T(8,128)} %get-tuple-element.157), channel_id=1, source_target_pairs={{0,1},{1,0},{2,3},{3,2},{4,5},{5,4},{6,7},{7,6},{8,9},{9,8},{10,11... | collective-permute-start | bytes 6291464 | tf_op jit(solution)/shard_map/ppermute | solution.py:921
  223.7 22.3 %collective-permute-start.58 = (f32[4,4,64,512]{3,2,1,0:T(8,128)}, f32[4,4,64,512]{3,2,1,0:T(8,128)}, u32[]{:S(2)}, u32[]{:S(2)}) collective-permute-start(f32[4,4,64,512]{3,2,1,0:T(8,128)} %get-tuple-element.165), channel_id=1, source_target_pairs={{0,1},{1,0},{2,3},{3,2},{4,5},{5,4},{6,7},{7,6},{8,9},{9,8},{10,11... | collective-permute-start | bytes 6291464 | tf_op jit(solution)/shard_map/ppermute | solution.py:921
  223.7 11.0 %collective-permute-start.54 = (f32[5,4,8,512]{3,2,1,0:T(8,128)}, f32[5,4,8,512]{3,2,1,0:T(8,128)}, u32[]{:S(2)}, u32[]{:S(2)}) collective-permute-start(f32[5,4,8,512]{3,2,1,0:T(8,128)} %get-tuple-element.153), channel_id=1, source_target_pairs={{0,16},{8,24},{16,0},{24,8},{1,17},{9,25},{17,1},{25,9},{2,18},{10... | collective-permute-start | bytes 983048 | tf_op jit(solution)/shard_map/ppermute | solution.py:921
  224.5 10.3 %collective-permute-start.55 = (f32[5,4,8,512]{3,2,1,0:T(8,128)}, f32[5,4,8,512]{3,2,1,0:T(8,128)}, u32[]{:S(2)}, u32[]{:S(2)}) collective-permute-start(f32[5,4,8,512]{3,2,1,0:T(8,128)} %get-tuple-element.155), channel_id=1, source_target_pairs={{0,8},{8,0},{16,24},{24,16},{1,9},{9,1},{17,25},{25,17},{2,10},{10... | collective-permute-start | bytes 983048 | tf_op jit(solution)/shard_map/ppermute | solution.py:921
  232.9 25.3 %collective-permute-start.59 = (f32[4,5,2,8,512]{4,3,2,1,0:T(8,128)}, f32[4,5,2,8,512]{4,3,2,1,0:T(8,128)}, u32[]{:S(2)}, u32[]{:S(2)}) collective-permute-start(f32[4,5,2,8,512]{4,3,2,1,0:T(8,128)} %get-tuple-element.177), channel_id=1, source_target_pairs={{0,8},{8,0},{16,24},{24,16},{1,9},{9,1},{17,25},{25,17},{2,10},{10... | collective-permute-start | bytes 1966088 | tf_op jit(solution)/shard_map/ppermute | solution.py:921
  232.9 25.3 %collective-permute-start.60 = (f32[4,5,2,8,512]{4,3,2,1,0:T(8,128)}, f32[4,5,2,8,512]{4,3,2,1,0:T(8,128)}, u32[]{:S(2)}, u32[]{:S(2)}) collective-permute-start(f32[4,5,2,8,512]{4,3,2,1,0:T(8,128)} %get-tuple-element.179), channel_id=1, source_target_pairs={{0,16},{8,24},{16,0},{24,8},{1,17},{9,25},{17,1},{25,9},{2,18},{10... | collective-permute-start | bytes 1966088 | tf_op jit(solution)/shard_map/ppermute | solution.py:921
  238.5 13.2 %collective-permute-start.57 = (f32[5,2,16,512]{3,2,1,0:T(8,128)S(1)}, f32[5,2,16,512]{3,2,1,0:T(8,128)S(1)}, u32[]{:S(2)}, u32[]{:S(2)}) collective-permute-start(f32[5,2,16,512]{3,2,1,0:T(8,128)S(1)} %get-tuple-element.163), channel_id=1, source_target_pairs={{0,2},{1,3},{2,0},{3,1},{4,6},{5,7},{6,4},{7,5},{8,10},{9,11},{10,... | collective-permute-start | bytes 983048 | tf_op jit(solution)/shard_map/ppermute | solution.py:921
  249.8 15.6 %collective-permute-start.64 = (f32[4,4,2,8,512]{4,3,2,1,0:T(8,128)S(1)}, f32[4,4,2,8,512]{4,3,2,1,0:T(8,128)S(1)}, u32[]{:S(2)}, u32[]{:S(2)}) collective-permute-start(f32[4,4,2,8,512]{4,3,2,1,0:T(8,128)S(1)} %get-tuple-element.188), channel_id=1, source_target_pairs={{0,8},{8,0},{16,24},{24,16},{1,9},{9,1},{17,25},{25,17},{2,10},{10... | collective-permute-start | bytes 1572872 | tf_op jit(solution)/shard_map/ppermute | solution.py:921
  250.8 14.6 %collective-permute-start.65 = (f32[4,4,2,8,512]{4,3,2,1,0:T(8,128)S(1)}, f32[4,4,2,8,512]{4,3,2,1,0:T(8,128)S(1)}, u32[]{:S(2)}, u32[]{:S(2)}) collective-permute-start(f32[4,4,2,8,512]{4,3,2,1,0:T(8,128)S(1)} %get-tuple-element.190), channel_id=1, source_target_pairs={{0,16},{8,24},{16,0},{24,8},{1,17},{9,25},{17,1},{25,9},{2,18},{10... | collective-permute-start | bytes 1572872 | tf_op jit(solution)/shard_map/ppermute | solution.py:921
  260.6 10.7 %collective-permute-start.61 = (f32[4,5,8,512]{3,2,1,0:T(8,128)S(1)}, f32[4,5,8,512]{3,2,1,0:T(8,128)S(1)}, u32[]{:S(2)}, u32[]{:S(2)}) collective-permute-start(f32[4,5,8,512]{3,2,1,0:T(8,128)S(1)} %get-tuple-element.182), channel_id=1, source_target_pairs={{0,16},{8,24},{16,0},{24,8},{1,17},{9,25},{17,1},{25,9},{2,18},{10... | collective-permute-start | bytes 983048 | tf_op jit(solution)/shard_map/ppermute | solution.py:921
  266.2 10.5 %collective-permute-start.67 = (f32[4,4,8,512]{3,2,1,0:T(8,128)S(1)}, f32[4,4,8,512]{3,2,1,0:T(8,128)S(1)}, u32[]{:S(2)}, u32[]{:S(2)}) collective-permute-start(f32[4,4,8,512]{3,2,1,0:T(8,128)S(1)} %get-tuple-element.197), channel_id=1, source_target_pairs={{0,16},{8,24},{16,0},{24,8},{1,17},{9,25},{17,1},{25,9},{2,18},{10... | collective-permute-start | bytes 786440 | tf_op jit(solution)/shard_map/ppermute | solution.py:921
  267.2 11.5 %collective-permute-start.68 = (f32[4,4,8,512]{3,2,1,0:T(8,128)S(1)}, f32[4,4,8,512]{3,2,1,0:T(8,128)S(1)}, u32[]{:S(2)}, u32[]{:S(2)}) collective-permute-start(f32[4,4,8,512]{3,2,1,0:T(8,128)S(1)} %get-tuple-element.199), channel_id=1, source_target_pairs={{0,8},{8,0},{16,24},{24,16},{1,9},{9,1},{17,25},{25,17},{2,10},{10... | collective-permute-start | bytes 786440 | tf_op jit(solution)/shard_map/ppermute | solution.py:921
  272.0 13.5 %collective-permute-start.66 = (f32[4,2,16,512]{3,2,1,0:T(8,128)S(1)}, f32[4,2,16,512]{3,2,1,0:T(8,128)S(1)}, u32[]{:S(2)}, u32[]{:S(2)}) collective-permute-start(f32[4,2,16,512]{3,2,1,0:T(8,128)S(1)} %get-tuple-element.195), channel_id=1, source_target_pairs={{0,2},{1,3},{2,0},{3,1},{4,6},{5,7},{6,4},{7,5},{8,10},{9,11},{10,... | collective-permute-start | bytes 786440 | tf_op jit(solution)/shard_map/ppermute | solution.py:921
  279.2 10.5 %collective-permute-start.73 = (f32[4,2,16,512]{3,2,1,0:T(8,128)S(1)}, f32[4,2,16,512]{3,2,1,0:T(8,128)S(1)}, u32[]{:S(2)}, u32[]{:S(2)}) collective-permute-start(f32[4,2,16,512]{3,2,1,0:T(8,128)S(1)} %get-tuple-element.208), channel_id=1, source_target_pairs={{0,2},{1,3},{2,0},{3,1},{4,6},{5,7},{6,4},{7,5},{8,10},{9,11},{10,... | collective-permute-start | bytes 786440 | tf_op jit(solution)/shard_map/ppermute | solution.py:921
  293.0 14.2 %collective-permute-start.74 = (f32[8,16,512]{2,1,0:T(8,128)S(1)}, f32[8,16,512]{2,1,0:T(8,128)S(1)}, u32[]{:S(2)}, u32[]{:S(2)}) collective-permute-start(f32[8,16,512]{2,1,0:T(8,128)S(1)} %get-tuple-element.211.refs_0_), channel_id=1, source_target_pairs={{0,8},{8,0},{16,24},{24,16},{1,9},{9,1},{17,25},{25,17},{2,10},{10... | collective-permute-start | bytes 786440 | tf_op jit(solution)/shard_map/ppermute | solution.py:921
  295.3 13.5 %collective-permute-start.75 = (f32[8,16,512]{2,1,0:T(8,128)S(1)}, f32[8,16,512]{2,1,0:T(8,128)S(1)}, u32[]{:S(2)}, u32[]{:S(2)}) collective-permute-start(f32[8,16,512]{2,1,0:T(8,128)S(1)} %get-tuple-element.211.refs_0_), channel_id=1, source_target_pairs={{0,16},{8,24},{16,0},{24,8},{1,17},{9,25},{17,1},{25,9},{2,18},{10... | collective-permute-start | bytes 786440 | tf_op jit(solution)/shard_map/ppermute | solution.py:921
  296.2 12.6 %collective-permute-start.76 = (f32[8,16,512]{2,1,0:T(8,128)S(1)}, f32[8,16,512]{2,1,0:T(8,128)S(1)}, u32[]{:S(2)}, u32[]{:S(2)}) collective-permute-start(f32[8,16,512]{2,1,0:T(8,128)S(1)} %get-tuple-element.211.refs_0_), channel_id=1, source_target_pairs={{0,24},{8,16},{16,8},{24,0},{1,25},{9,17},{17,9},{25,1},{2,26},{10... | collective-permute-start | bytes 786440 | tf_op jit(solution)/shard_map/ppermute | solution.py:921
  (111 other events, 848.9 us)
Sparse Core Ops, SparseCore 0:
  79.8 69.9 all-gather.2
Sparse Core Ops, SparseCore 1:
  155.9 49.3 reduce-scatter.1

commit v4 on v3

--- a/solution.py
+++ b/solution.py
@@ -312,7 +312,7 @@
     slabs = rows // 8
     hidden = hidden_map.shape[1]
     crops = sum(p.crops for p in order)
-    block = 256
+    block = 512
     steps = width // block
 
     def kernel(a_ref, st_ref, g_ref, b_ref, x_ref, w_ref, p_ref, e_ref, ap_ref, scr, acc):
@@ -355,7 +355,7 @@
         out_specs=[lanes_of(block, slots), whole(slots, hidden)],
         out_shape=(jax.ShapeDtypeStruct((slots, width), F32), jax.ShapeDtypeStruct((slots, hidden), F32)),
         scratch_shapes=[pltpu.VMEM((32, block), F32), pltpu.VMEM((96, hidden), F32)],
-        compiler_params=params(12),
+        compiler_params=params(20),
         cost_estimate=cost(2 * 96 * width * hidden, 16 << 20, 2 * rows * width),
         name="pool_embed",
     )(third_pre, sums, gain, bias, inputs, hidden_map, pair_row)
@@ -476,29 +476,36 @@
         i_scr[...] = jnp.where(row_id == col_id, 1.0, 0.0)
 
         def eliminate(step, carry):
-            j = 2 * step
+            j = 4 * step
             a = a_scr[...]
             image = i_scr[...]
-            row0 = a_scr[pl.ds(j, 1), :]
-            row1 = a_scr[pl.ds(j + 1, 1), :]
-            image0 = i_scr[pl.ds(j, 1), :]
-            image1 = i_scr[pl.ds(j + 1, 1), :]
-            first = jnp.full((emb, emb), j, jnp.int32)
-            second = first + 1
-            lane = lambda row, at: jnp.take_along_axis(jnp.broadcast_to(row, (8, emb)), at[0:8], axis=1)[0:1]
-            column0 = jnp.take_along_axis(a, first, axis=1)
-            column1 = jnp.take_along_axis(a, second, axis=1)
-            inverse0 = 1.0 / lane(row0, first)
-            ratio = lane(row0, second) * inverse0
-            inverse1 = 1.0 / (lane(row1, second) - lane(row1, first) * ratio)
-            factor0 = jnp.where(row_id > j, column0, 0.0)
-            factor1 = jnp.where(row_id > j + 1, column1 - column0 * ratio, 0.0)
-            below = lane(row1, first) * inverse0
-            a_scr[...] = a - factor0 * (row0 * inverse0) - factor1 * ((row1 - below * row0) * inverse1)
-            i_scr[...] = image - factor0 * (image0 * inverse0) - factor1 * ((image1 - below * image0) * inverse1)
+            at = [jnp.full((emb, emb), j + q, jnp.int32) for q in range(4)]
+            lane = lambda row, q: jnp.take_along_axis(jnp.broadcast_to(row, (8, emb)), at[q][0:8], axis=1)[0:1]
+            rows = [a_scr[pl.ds(j + p, 1), :] for p in range(4)]
+            images = [i_scr[pl.ds(j + p, 1), :] for p in range(4)]
+            entry = [[lane(rows[p], q) for q in range(4)] for p in range(4)]
+            columns = [jnp.take_along_axis(a, at[q], axis=1) for q in range(4)]
+            inverse = []
+            for q in range(4):
+                inverse.append(1.0 / entry[q][q])
+                for p in range(q + 1, 4):
+                    ratio = entry[p][q] * inverse[q]
+                    rows[p] = rows[p] - ratio * rows[q]
+                    images[p] = images[p] - ratio * images[q]
+                    for c in range(q + 1, 4):
+                        entry[p][c] = entry[p][c] - ratio * entry[q][c]
+            for q in range(4):
+                column = columns[q]
+                for p in range(q):
+                    column = column - columns[p] * entry[p][q]
+                columns[q] = jnp.where(row_id > j + q, column * inverse[q], 0.0)
+                a = a - columns[q] * rows[q]
+                image = image - columns[q] * images[q]
+            a_scr[...] = a
+            i_scr[...] = image
             return carry
 
-        lax.fori_loop(0, emb // 2, eliminate, 0)
+        lax.fori_loop(0, emb // 4, eliminate, 0)
         diag = jnp.sum(jnp.where(row_id == col_id, a_scr[...], 0.0), axis=1, keepdims=True)
         white = i_scr[...] * lax.rsqrt(diag)
         ph, pm, pq = split3(white)

time: 323 us -> 322 us (level)
  transfers between devices with their start and end apart: 83 -> 83, of which waited for: 56 -> 53; matrix products, arithmetic and copies ran while one was open for 1% -> 1% of each run, Pallas kernels for 28% -> 28%
where the time goes in v4:
time: 322 us; the launch traced here: 321 us
  Pallas kernels  108 us (34%)
  starting transfers between devices  93.9 us (29%)
  waiting for transfers between devices  67.2 us (21%)
  local copies, waits for them, and re-layouts  34.8 us (11%)
  between operations  16.1 us (5%)
    ppermute x81, starting transfers between devices, swap(): return lax.ppermute(x, axis, [(i, i ^ mask) for i in range(size)])  93.8 us
    ppermute x81, waiting for transfers between devices, swap(): return lax.ppermute(x, axis, [(i, i ^ mask) for i in range(size)])  67.2 us
    unnamed x104, local copies, waits for them, and re-layouts  31.8 us
    pallas_call x1, Pallas kernels, projector(): pl.pallas_call(kernel, out_shape=(jax.ShapeDtypeStruct((rows_all, hidden)...  16 us
    pallas_call x6, Pallas kernels, fold(): pl.pallas_call(whole_kernel, grid=(count,), in_specs=[SMEM] + [unit(x.sha...  14 us
    pallas_call x2, Pallas kernels, middle_weight(): pl.pallas_call(kernel, grid=(count,), in_specs=[SMEM, whole(slabs, 8, cha...  10.9 us
    pallas_call x1, Pallas kernels, last_back(): pl.pallas_call(kernel, grid=(steps,), in_specs=[lanes_of(block, rows), la...  10.3 us
    pallas_call x1, Pallas kernels, projector_weights(): pl.pallas_call(kernel, grid_spec=pltpu.PrefetchScalarGridSpec(num_scalar_...  6.5 us
  transfers between devices with their start and end apart: 83, of which 53 were waited for; matrix products, arithmetic and copies ran while one was open for 1% of the time, Pallas kernels for 28%

profile of v4, /device:TPU:0, one launch (start us, length us, event | category | flops | bytes accessed | tf_op | source)
XLA Modules:
  0.0 320.9 jit_solution(15523303664451527728)
XLA Ops:
  13.5 4.0 %first_conv.1 = (bf16[880,2048]{1,0:T(8,128)(2,1)S(1)}, f32[880,512]{1,0:T(8,128)S(1)}, f32[2,512]{1,0:T(2,128)S(1)}) custom-call(bf16[49,8,2048]{2,1,0:T(8,128)(2,1)S(1)} %bitcast.128, bf16[6,6,6,2048]{3,2,1,0:T(8,128)(2,1)S(1)} %copy-done.41, bf16[25,8,2048]{2,1,0:T(8,128)(2,1)S(1)} %bitcast.129, bf16[2048,512]{1,0:T(8,128)(2,1)S(1)} %copy-done.36), custom_call_target="tpu_custom_call" | custom-call | flops 1845493760 | bytes 10485760 | tf_op jit(solution)/shard_map/first_conv/pallas_call | solution.py:183
  18.8 3.8 %collective-permute-start.3 = (f32[2,512]{1,0:T(2,128)S(1)}, f32[2,512]{1,0:T(2,128)S(1)}, u32[]{:S(2)}, u32[]{:S(2)}) collective-permute-start(f32[2,512]{1,0:T(2,128)S(1)} %add.243), channel_id=1, source_target_pairs={{0,24},{8,16},{16,8},{24,0},{1,25},{9,17},{17,9},{25,1},{2,26},{10... | collective-permute-start | bytes 12296 | tf_op jit(solution)/shard_map/ppermute | solution.py:928
  26.7 3.6 %collective-permute-start.6 = (f32[2,512]{1,0:T(2,128)S(1)}, f32[2,512]{1,0:T(2,128)S(1)}, u32[]{:S(2)}, u32[]{:S(2)}) collective-permute-start(f32[2,512]{1,0:T(2,128)S(1)} %add_add_fusion.10), channel_id=1, source_target_pairs={{0,6},{1,7},{2,4},{3,5},{4,2},{5,3},{6,0},{7,1},{8,14},{9,15},{10,... | collective-permute-start | bytes 12296 | tf_op jit(solution)/shard_map/ppermute | solution.py:928
  34.9 4.4 %middle_conv.1 = (f32[110,8,512]{2,1,0:T(8,128)S(1)}, f32[880,512]{1,0:T(8,128)S(1)}, f32[2,512]{1,0:T(2,128)S(1)}) custom-call(f32[880,512]{1,0:T(8,128)S(1)} %get-tuple-element.120.a_ref.f_ref, f32[2,512]{1,0:T(2,128)S(1)} %add_add_fusion.9.st_ref.is_ref, f32[1,512]{1,0:T(1,128)S(1)} %bitcast.118, f32[1,512]{1,0:T(1,128)S(1)} %bitcast.135, ...), custom_call_target="tpu_custom_call" | custom-call | flops 4152360960 | bytes 20971520 | tf_op jit(solution)/shard_map/middle_conv/pallas_call | solution.py:257
  53.4 3.8 %last_conv.1 = (bf16[880,512]{1,0:T(8,128)(2,1)S(1)}, f32[880,2048]{1,0:T(8,128)S(1)}, f32[2,2048]{1,0:T(2,128)S(1)}) custom-call(f32[880,512]{1,0:T(8,128)S(1)} %get-tuple-element.122.a_ref.m_ref, f32[2,512]{1,0:T(2,128)S(1)} %add_add_fusion.7.st_ref.ms_ref, f32[1,512]{1,0:T(1,128)S(1)} %bitcast.123, f32[1,512]{1,0:T(1,128)S(1)} %bitcast.121, ...), custom_call_target="tpu_custom_call" | custom-call | flops 1845493760 | bytes 12582912 | tf_op jit(solution)/shard_map/last_conv/pallas_call | solution.py:294
  72.7 6.1 %pool_embed.1 = (f32[24,2048]{1,0:T(8,128)}, f32[24,1024]{1,0:T(8,128)S(1)}) custom-call(f32[880,2048]{1,0:T(8,128)S(1)} %get-tuple-element.124.a_ref, f32[2,2048]{1,0:T(2,128)S(1)} %add_add_fusion.2.st_ref, f32[1,2048]{1,0:T(1,128)S(1)} %bitcast.112, f32[1,2048]{1,0:T(1,128)S(1)} %bitcast.115, bf16[880,2048]{1,0:T(8,128)(2,1)S(1)} %get-tuple-element.126.x_ref, ...), custom_call_target="tpu_custom_call" | custom-call | flops 402653184 | bytes 16777216 | tf_op jit(solution)/shard_map/pool_embed/pallas_call | solution.py:348
  84.1 3.3 %collective-permute-done.22.refs_2_ = f32[1,24,1024]{2,1,0:T(8,128)S(1)} collective-permute-done((f32[1,24,1024]{2,1,0:T(8,128)S(1)}, f32[1,24,1024]{2,1,0:T(8,128)S(1)}, u32[]{:S(2)}, u32[]{:S(2)}) %collective-permute-start.22) | collective-permute-done | bytes 98336 | tf_op jit(solution)/shard_map/ppermute | solution.py:928
  91.0 3.1 copy-done.1
  96.1 6.2 %slope_sums.1 = (bf16[880,2048]{1,0:T(8,128)(2,1)S(1)}, f32[24,2048]{1,0:T(8,128)S(1)}, f32[24,2048]{1,0:T(8,128)S(1)}, f32[4,24,1024]{2,1,0:T(8,128)S(1)}) custom-call(f32[880,2048]{1,0:T(8,128)S(1)} %copy-done.1, f32[2,2048]{1,0:T(2,128)S(1)} %add_add_fusion.2.st_ref, f32[1,2048]{1,0:T(1,128)S(1)} %bitcast.113, f32[1,2048]{1,0:T(1,128)S(1)} %bitcast.116, ...), custom_call_target="tpu_custom_call" | custom-call | flops 43253760 | bytes 14417920 | tf_op jit(solution)/shard_map/slope_sums/pallas_call | solution.py:386
  106.6 16.0 %projector.1 = (f32[768,1024]{1,0:T(8,128)S(1)}, f32[768,1024]{1,0:T(8,128)S(1)}, f32[768,128]{1,0:T(8,128)S(1)}, f32[1,1024]{1,0:T(1,128)}, f32[1,1024]{1,0:T(1...) custom-call(f32[4,24,1024]{2,1,0:T(8,128)S(1)} %get-tuple-element.129.refs_0_, ...), custom_call_target="tpu_custom_call" | custom-call | flops 10737418240 | bytes 20971520 | tf_op jit(solution)/shard_map/projector/pallas_call | solution.py:584
  142.6 10.3 %last_back.1 = (f32[880,512]{1,0:T(8,128)S(1)}, f32[2,512]{1,0:T(2,128)S(1)}, f32[512,2048]{1,0:T(8,128)}) custom-call(bf16[880,2048]{1,0:T(8,128)(2,1)S(1)} %get-tuple-element.128.s_ref, f32[24,2048]{1,0:T(8,128)S(1)} %get-tuple-element.132.e_ref, f32[880,2048]{1,0:T(8,128)} %copy-done, f32[2,2048]{1,0:T(2,128)S(1)} %add_add_fusion.2.st_ref, ...), custom_call_target="tpu_custom_call" | custom-call | flops 3690987520 | bytes 25165824 | tf_op jit(solution)/shard_map/last_back/pallas_call | solution.py:713
  174.5 6.0 %middle_back.1 = (bf16[880,512]{1,0:T(8,128)(2,1)S(1)}, f32[880,512]{1,0:T(8,128)S(1)}, f32[2,512]{1,0:T(2,128)S(1)}) custom-call(f32[880,512]{1,0:T(8,128)S(1)} %copy-done.39, f32[2,512]{1,0:T(2,128)S(1)} %add_add_fusion.5.gs_ref, f32[880,512]{1,0:T(8,128)S(1)} %copy-done.18, f32[2,512]{1,0:T(2,128)S(1)} %add_add_fusion.7.st_ref.ms_ref, ...), custom_call_target="tpu_custom_call" | custom-call | flops 4152360960 | bytes 20971520 | tf_op jit(solution)/shard_map/middle_back/pallas_call | solution.py:763
  181.8 5.8 %middle_weight.2 = (f32[5,4,64,512]{3,2,1,0:T(8,128)S(1)}, f32[5,4,64,512]{3,2,1,0:T(8,128)S(1)}, f32[2,512]{1,0:T(2,128)S(1)}, f32[8,128]{1,0:T(8,128)}) custom-call(s32[3]{0:T(128)S(1)} %pad_add_fusion.at_ref, f32[110,8,512]{2,1,0:T(8,128)S(1)} %copy-done.50, bf16[880,512]{1,0:T(8,128)(2,1)S(1)} %get-tuple-element.140.g_ref, f32[2,512]{1,0:T(2,128)S(1)} %add.282.refs_0_), custom_call_target="tpu_custom_call" | custom-call | flops 2306867200 | bytes 12582912 | tf_op jit(solution)/shard_map/middle_weight/pallas_call | solution.py:815
  206.5 5.3 %first_back.1 = (bf16[880,512]{1,0:T(8,128)(2,1)S(1)}, f32[4,4,64,512]{3,2,1,0:T(8,128)}, f32[4,4,64,512]{3,2,1,0:T(8,128)S(1)}, f32[8,128]{1,0:T(8,128)S(1)}) custom-call(s32[3]{0:T(128)S(1)} %pad_add_fusion.at_ref, f32[880,512]{1,0:T(8,128)S(1)} %get-tuple-element.138.gq_ref, f32[2,512]{1,0:T(2,128)S(1)} %add.287.gs_ref, f32[880,512]{1,0:T(8,128)S(1)} %copy-done.15, ...), custom_call_target="tpu_custom_call" | custom-call | flops 1845493760 | bytes 10485760 | tf_op jit(solution)/shard_map/first_back/pallas_call | solution.py:856
  216.8 5.1 %middle_weight.3 = (f32[4,4,64,512]{3,2,1,0:T(8,128)}, f32[4,4,64,512]{3,2,1,0:T(8,128)S(1)}, f32[8,128]{1,0:T(8,128)S(1)}) custom-call(s32[3]{0:T(128)S(1)} %pad_add_fusion.at_ref, f32[110,8,512]{2,1,0:T(8,128)S(1)} %copy-done.50, bf16[880,512]{1,0:T(8,128)(2,1)S(1)} %get-tuple-element.140.g_ref, f32[8,128]{1,0:T(8,128)S(1)} %get-tuple-element.159.refs_0_), custom_call_target="tpu_custom_call" | custom-call | flops 1845493760 | bytes 12582912 | tf_op jit(solution)/shard_map/middle_weight/pallas_call | solution.py:815
  227.0 3.7 %fold_first.4 = (f32[4,5,2,8,512]{4,3,2,1,0:T(8,128)}, f32[4,5,2,8,512]{4,3,2,1,0:T(8,128)S(1)}, f32[4,5,2,8,512]{4,3,2,1,0:T(8,128)}, f32[4,5,2,8,512]{4,3,2,1,0:T(8,128)S(1)}, f32[8,128]{1,0:T(8,128)S(1)}) custom-call(s32[3]{0:T(128)S(1)} %pad_add_fusion.at_ref, f32[4,4,4,16,512]{4,3,2,1,0:T(8,128)S(1)} %bitcast.96, ...), custom_call_target="tpu_custom_call" | custom-call | bytes 8388608 | tf_op jit(solution)/shard_map/fold_first/pallas_call | solution.py:991
  237.8 6.5 %projector_weights.1 = (f32[256,1024]{1,0:T(8,128)}, f32[128,128]{1,0:T(8,128)}, f32[8,128]{1,0:T(8,128)}) custom-call(s32[33]{0:T(128)} %concatenate.7.at_ref, f32[32,24,2048]{2,1,0:T(8,128)} %bitcast.137, f32[768,1024]{1,0:T(8,128)} %copy-done.10, f32[768,1024]{1,0:T(8,128)} %copy-done.9, f32[768,128]{1,0:T(8,128)} %copy-done.20, f32[8,128]{1,0:T(8,128)} %copy-done.30), custom_call_target="tpu_custom_call" | custom-call | flops 2147483648 | bytes 16777216 | tf_op jit(solution)/shard_map/projector_weights/pallas_call | solution.py:634
  245.0 3.0 fold_first.5
  252.6 4.4 %input_grads.1 = (f32[49,8,2048]{2,1,0:T(8,128)}, f32[6,6,6,2048]{3,2,1,0:T(8,128)}, f32[25,8,2048]{2,1,0:T(8,128)}, f32[8,128]{1,0:T(8,128)S(1)}) custom-call(bf16[880,2048]{1,0:T(8,128)(2,1)S(1)} %copy-done.8, f32[24,2048]{1,0:T(8,128)S(1)} %copy-done.26, bf16[880,512]{1,0:T(8,128)(2,1)S(1)} %copy-done.43, bf16[2048,512]{1,0:T(8,128)(2,1)S(1)} %copy-done.37, ...), custom_call_target="tpu_custom_call" | custom-call | flops 1845493760 | bytes 16777216 | tf_op jit(solution)/shard_map/input_grads/pallas_call | solution.py:900
  261.2 3.1 collective-permute-start.63
  285.3 3.4 %collective-permute-start.72 = (f32[4,1,16,512]{3,2,0,1:T(8,128)S(1)}, f32[4,1,16,512]{3,2,0,1:T(8,128)S(1)}, u32[]{:S(2)}, u32[]{:S(2)}) collective-permute-start(f32[4,1,16,512]{3,2,0,1:T(8,128)S(1)} %bitcast.132), channel_id=1, source_target_pairs={{0,6},{1,7},{2,4},{3,5},{4,2},{5,3},{6,0},{7,1},{8,14},{9,15},{10,... | collective-permute-start | bytes 393224 | tf_op jit(solution)/shard_map/ppermute | solution.py:928
  289.2 3.0 collective-permute-done.72
  296.4 3.2 collective-permute-start.77
  300.2 3.1 collective-permute-done.77
  (309 shorter events, 184.8 us)
Async XLA Ops:
  8.0 160.4 %all-gather.3.cloned.1.call-start = ((), (), s32[]{:S(2)}) async-start(), calls=%async_computation.2 | async-start | bytes 6488064 | tf_op jit(solution)/shard_map/all_gather | solution.py:1362
  78.9 145.5 %reduce-scatter.2.cloned.1.call-start = ((), (), s32[]{:S(2)}) async-start(), calls=%async_computation.1 | async-start | bytes 4718592 | tf_op jit(solution)/shard_map/reduce_scatter | solution.py:1363
  87.4 15.0 %collective-permute-start.24 = (f32[4,24,1024]{2,1,0:T(8,128)S(1)}, f32[4,24,1024]{2,1,0:T(8,128)S(1)}, u32[]{:S(2)}, u32[]{:S(2)}) collective-permute-start(f32[4,24,1024]{2,1,0:T(8,128)S(1)} %bitcast.97), channel_id=1, source_target_pairs={{0,8},{8,0},{16,24},{24,16},{1,9},{9,1},{17,25},{25,17},{2,10},{10... | collective-permute-start | bytes 1179656 | tf_op jit(solution)/shard_map/ppermute | solution.py:928
  88.0 15.3 %collective-permute-start.25 = (f32[4,24,1024]{2,1,0:T(8,128)S(1)}, f32[4,24,1024]{2,1,0:T(8,128)S(1)}, u32[]{:S(2)}, u32[]{:S(2)}) collective-permute-start(f32[4,24,1024]{2,1,0:T(8,128)S(1)} %bitcast.98), channel_id=1, source_target_pairs={{0,16},{8,24},{16,0},{24,8},{1,17},{9,25},{17,1},{25,9},{2,18},{10... | collective-permute-start | bytes 1179656 | tf_op jit(solution)/shard_map/ppermute | solution.py:928
  89.6 15.2 %collective-permute-start.26 = (f32[4,24,1024]{2,1,0:T(8,128)S(1)}, f32[4,24,1024]{2,1,0:T(8,128)S(1)}, u32[]{:S(2)}, u32[]{:S(2)}) collective-permute-start(f32[4,24,1024]{2,1,0:T(8,128)S(1)} %bitcast.99), channel_id=1, source_target_pairs={{0,24},{8,16},{16,8},{24,0},{1,25},{9,17},{17,9},{25,1},{2,26},{10... | collective-permute-start | bytes 1179656 | tf_op jit(solution)/shard_map/ppermute | solution.py:928
  195.9 16.8 %collective-permute-start.52 = (f32[5,4,2,8,512]{4,3,2,1,0:T(8,128)S(1)}, f32[5,4,2,8,512]{4,3,2,1,0:T(8,128)S(1)}, u32[]{:S(2)}, u32[]{:S(2)}) collective-permute-start(f32[5,4,2,8,512]{4,3,2,1,0:T(8,128)S(1)} %get-tuple-element.148), channel_id=1, source_target_pairs={{0,8},{8,0},{16,24},{24,16},{1,9},{9,1},{17,25},{25,17},{2,10},{10... | collective-permute-start | bytes 1966088 | tf_op jit(solution)/shard_map/ppermute | solution.py:928
  196.4 16.3 %collective-permute-start.53 = (f32[5,4,2,8,512]{4,3,2,1,0:T(8,128)S(1)}, f32[5,4,2,8,512]{4,3,2,1,0:T(8,128)S(1)}, u32[]{:S(2)}, u32[]{:S(2)}) collective-permute-start(f32[5,4,2,8,512]{4,3,2,1,0:T(8,128)S(1)} %get-tuple-element.150), channel_id=1, source_target_pairs={{0,16},{8,24},{16,0},{24,8},{1,17},{9,25},{17,1},{25,9},{2,18},{10... | collective-permute-start | bytes 1966088 | tf_op jit(solution)/shard_map/ppermute | solution.py:928
  212.7 11.7 %collective-permute-start.56 = (f32[4,4,64,512]{3,2,1,0:T(8,128)}, f32[4,4,64,512]{3,2,1,0:T(8,128)}, u32[]{:S(2)}, u32[]{:S(2)}) collective-permute-start(f32[4,4,64,512]{3,2,1,0:T(8,128)} %get-tuple-element.157), channel_id=1, source_target_pairs={{0,1},{1,0},{2,3},{3,2},{4,5},{5,4},{6,7},{7,6},{8,9},{9,8},{10,11... | collective-permute-start | bytes 6291464 | tf_op jit(solution)/shard_map/ppermute | solution.py:928
  221.9 22.4 %collective-permute-start.58 = (f32[4,4,64,512]{3,2,1,0:T(8,128)}, f32[4,4,64,512]{3,2,1,0:T(8,128)}, u32[]{:S(2)}, u32[]{:S(2)}) collective-permute-start(f32[4,4,64,512]{3,2,1,0:T(8,128)} %get-tuple-element.165), channel_id=1, source_target_pairs={{0,1},{1,0},{2,3},{3,2},{4,5},{5,4},{6,7},{7,6},{8,9},{9,8},{10,11... | collective-permute-start | bytes 6291464 | tf_op jit(solution)/shard_map/ppermute | solution.py:928
  222.5 11.0 %collective-permute-start.54 = (f32[5,4,8,512]{3,2,1,0:T(8,128)}, f32[5,4,8,512]{3,2,1,0:T(8,128)}, u32[]{:S(2)}, u32[]{:S(2)}) collective-permute-start(f32[5,4,8,512]{3,2,1,0:T(8,128)} %get-tuple-element.153), channel_id=1, source_target_pairs={{0,16},{8,24},{16,0},{24,8},{1,17},{9,25},{17,1},{25,9},{2,18},{10... | collective-permute-start | bytes 983048 | tf_op jit(solution)/shard_map/ppermute | solution.py:928
  223.1 10.4 %collective-permute-start.55 = (f32[5,4,8,512]{3,2,1,0:T(8,128)}, f32[5,4,8,512]{3,2,1,0:T(8,128)}, u32[]{:S(2)}, u32[]{:S(2)}) collective-permute-start(f32[5,4,8,512]{3,2,1,0:T(8,128)} %get-tuple-element.155), channel_id=1, source_target_pairs={{0,8},{8,0},{16,24},{24,16},{1,9},{9,1},{17,25},{25,17},{2,10},{10... | collective-permute-start | bytes 983048 | tf_op jit(solution)/shard_map/ppermute | solution.py:928
  230.7 26.3 %collective-permute-start.59 = (f32[4,5,2,8,512]{4,3,2,1,0:T(8,128)}, f32[4,5,2,8,512]{4,3,2,1,0:T(8,128)}, u32[]{:S(2)}, u32[]{:S(2)}) collective-permute-start(f32[4,5,2,8,512]{4,3,2,1,0:T(8,128)} %get-tuple-element.177), channel_id=1, source_target_pairs={{0,8},{8,0},{16,24},{24,16},{1,9},{9,1},{17,25},{25,17},{2,10},{10... | collective-permute-start | bytes 1966088 | tf_op jit(solution)/shard_map/ppermute | solution.py:928
  231.5 25.5 %collective-permute-start.60 = (f32[4,5,2,8,512]{4,3,2,1,0:T(8,128)}, f32[4,5,2,8,512]{4,3,2,1,0:T(8,128)}, u32[]{:S(2)}, u32[]{:S(2)}) collective-permute-start(f32[4,5,2,8,512]{4,3,2,1,0:T(8,128)} %get-tuple-element.179), channel_id=1, source_target_pairs={{0,16},{8,24},{16,0},{24,8},{1,17},{9,25},{17,1},{25,9},{2,18},{10... | collective-permute-start | bytes 1966088 | tf_op jit(solution)/shard_map/ppermute | solution.py:928
  237.2 13.2 %collective-permute-start.57 = (f32[5,2,16,512]{3,2,1,0:T(8,128)S(1)}, f32[5,2,16,512]{3,2,1,0:T(8,128)S(1)}, u32[]{:S(2)}, u32[]{:S(2)}) collective-permute-start(f32[5,2,16,512]{3,2,1,0:T(8,128)S(1)} %get-tuple-element.163), channel_id=1, source_target_pairs={{0,2},{1,3},{2,0},{3,1},{4,6},{5,7},{6,4},{7,5},{8,10},{9,11},{10,... | collective-permute-start | bytes 983048 | tf_op jit(solution)/shard_map/ppermute | solution.py:928
  248.0 16.2 %collective-permute-start.64 = (f32[4,4,2,8,512]{4,3,2,1,0:T(8,128)S(1)}, f32[4,4,2,8,512]{4,3,2,1,0:T(8,128)S(1)}, u32[]{:S(2)}, u32[]{:S(2)}) collective-permute-start(f32[4,4,2,8,512]{4,3,2,1,0:T(8,128)S(1)} %get-tuple-element.188), channel_id=1, source_target_pairs={{0,8},{8,0},{16,24},{24,16},{1,9},{9,1},{17,25},{25,17},{2,10},{10... | collective-permute-start | bytes 1572872 | tf_op jit(solution)/shard_map/ppermute | solution.py:928
  249.5 14.7 %collective-permute-start.65 = (f32[4,4,2,8,512]{4,3,2,1,0:T(8,128)S(1)}, f32[4,4,2,8,512]{4,3,2,1,0:T(8,128)S(1)}, u32[]{:S(2)}, u32[]{:S(2)}) collective-permute-start(f32[4,4,2,8,512]{4,3,2,1,0:T(8,128)S(1)} %get-tuple-element.190), channel_id=1, source_target_pairs={{0,16},{8,24},{16,0},{24,8},{1,17},{9,25},{17,1},{25,9},{2,18},{10... | collective-permute-start | bytes 1572872 | tf_op jit(solution)/shard_map/ppermute | solution.py:928
  259.4 10.9 %collective-permute-start.61 = (f32[4,5,8,512]{3,2,1,0:T(8,128)S(1)}, f32[4,5,8,512]{3,2,1,0:T(8,128)S(1)}, u32[]{:S(2)}, u32[]{:S(2)}) collective-permute-start(f32[4,5,8,512]{3,2,1,0:T(8,128)S(1)} %get-tuple-element.182), channel_id=1, source_target_pairs={{0,16},{8,24},{16,0},{24,8},{1,17},{9,25},{17,1},{25,9},{2,18},{10... | collective-permute-start | bytes 983048 | tf_op jit(solution)/shard_map/ppermute | solution.py:928
  265.0 10.9 %collective-permute-start.67 = (f32[4,4,8,512]{3,2,1,0:T(8,128)S(1)}, f32[4,4,8,512]{3,2,1,0:T(8,128)S(1)}, u32[]{:S(2)}, u32[]{:S(2)}) collective-permute-start(f32[4,4,8,512]{3,2,1,0:T(8,128)S(1)} %get-tuple-element.197), channel_id=1, source_target_pairs={{0,16},{8,24},{16,0},{24,8},{1,17},{9,25},{17,1},{25,9},{2,18},{10... | collective-permute-start | bytes 786440 | tf_op jit(solution)/shard_map/ppermute | solution.py:928
  265.7 11.2 %collective-permute-start.68 = (f32[4,4,8,512]{3,2,1,0:T(8,128)S(1)}, f32[4,4,8,512]{3,2,1,0:T(8,128)S(1)}, u32[]{:S(2)}, u32[]{:S(2)}) collective-permute-start(f32[4,4,8,512]{3,2,1,0:T(8,128)S(1)} %get-tuple-element.199), channel_id=1, source_target_pairs={{0,8},{8,0},{16,24},{24,16},{1,9},{9,1},{17,25},{25,17},{2,10},{10... | collective-permute-start | bytes 786440 | tf_op jit(solution)/shard_map/ppermute | solution.py:928
  270.9 13.8 %collective-permute-start.66 = (f32[4,2,16,512]{3,2,1,0:T(8,128)S(1)}, f32[4,2,16,512]{3,2,1,0:T(8,128)S(1)}, u32[]{:S(2)}, u32[]{:S(2)}) collective-permute-start(f32[4,2,16,512]{3,2,1,0:T(8,128)S(1)} %get-tuple-element.195), channel_id=1, source_target_pairs={{0,2},{1,3},{2,0},{3,1},{4,6},{5,7},{6,4},{7,5},{8,10},{9,11},{10,... | collective-permute-start | bytes 786440 | tf_op jit(solution)/shard_map/ppermute | solution.py:928
  277.5 11.1 %collective-permute-start.73 = (f32[4,2,16,512]{3,2,1,0:T(8,128)S(1)}, f32[4,2,16,512]{3,2,1,0:T(8,128)S(1)}, u32[]{:S(2)}, u32[]{:S(2)}) collective-permute-start(f32[4,2,16,512]{3,2,1,0:T(8,128)S(1)} %get-tuple-element.208), channel_id=1, source_target_pairs={{0,2},{1,3},{2,0},{3,1},{4,6},{5,7},{6,4},{7,5},{8,10},{9,11},{10,... | collective-permute-start | bytes 786440 | tf_op jit(solution)/shard_map/ppermute | solution.py:928
  292.2 13.4 %collective-permute-start.74 = (f32[8,16,512]{2,1,0:T(8,128)S(1)}, f32[8,16,512]{2,1,0:T(8,128)S(1)}, u32[]{:S(2)}, u32[]{:S(2)}) collective-permute-start(f32[8,16,512]{2,1,0:T(8,128)S(1)} %get-tuple-element.211.refs_0_), channel_id=1, source_target_pairs={{0,8},{8,0},{16,24},{24,16},{1,9},{9,1},{17,25},{25,17},{2,10},{10... | collective-permute-start | bytes 786440 | tf_op jit(solution)/shard_map/ppermute | solution.py:928
  294.0 14.0 %collective-permute-start.75 = (f32[8,16,512]{2,1,0:T(8,128)S(1)}, f32[8,16,512]{2,1,0:T(8,128)S(1)}, u32[]{:S(2)}, u32[]{:S(2)}) collective-permute-start(f32[8,16,512]{2,1,0:T(8,128)S(1)} %get-tuple-element.211.refs_0_), channel_id=1, source_target_pairs={{0,16},{8,24},{16,0},{24,8},{1,17},{9,25},{17,1},{25,9},{2,18},{10... | collective-permute-start | bytes 786440 | tf_op jit(solution)/shard_map/ppermute | solution.py:928
  294.8 13.2 %collective-permute-start.76 = (f32[8,16,512]{2,1,0:T(8,128)S(1)}, f32[8,16,512]{2,1,0:T(8,128)S(1)}, u32[]{:S(2)}, u32[]{:S(2)}) collective-permute-start(f32[8,16,512]{2,1,0:T(8,128)S(1)} %get-tuple-element.211.refs_0_), channel_id=1, source_target_pairs={{0,24},{8,16},{16,8},{24,0},{1,25},{9,17},{17,9},{25,1},{2,26},{10... | collective-permute-start | bytes 786440 | tf_op jit(solution)/shard_map/ppermute | solution.py:928
  (111 other events, 849.7 us)
Sparse Core Ops, SparseCore 0:
  79.0 69.3 all-gather.2
Sparse Core Ops, SparseCore 1:
  154.2 50.0 reduce-scatter.1

commit v5 on v4

--- a/solution.py
+++ b/solution.py
@@ -267,7 +267,7 @@
             pltpu.VMEM(turned_shape(order, chan), F32),
             pltpu.VMEM((rows, 9 * chan), BF16),
         ],
-        compiler_params=params(24),
+        compiler_params=params(40),
         cost_estimate=cost(18 * rows * chan * chan, 20 << 20),
         name="middle_conv",
     )(first_pre, sums, gain, bias, kernel_flat)
@@ -1404,9 +1404,9 @@
     far1 = Spread([m1], [last.mark])
     taps = m0.keep.shape[0] + m1.keep.shape[0]
     mid_grad, mark = place_taps(early.pieces, where, 0, taps)
-    last.far([far1.mark, mark])
+    last.far([far1.mark])
     far1.far([last.mark])
-    middle = Gather([last, last.extra], [far1.mark])
+    middle = Gather([last, last.extra], [far1.mark, mark])
     late = Gather([far1], [middle.mark])
     conv_in_grad, out_grad = place(middle.pieces, where, 4)
     conv_in_grad = conv_in_grad.reshape(width // nblk, chan)

time: 322 us -> 317 us (0.984)
  transfers between devices with their start and end apart: 83 -> 83, of which waited for: 53 -> 51; matrix products, arithmetic and copies ran while one was open for 1% -> 1% of each run, Pallas kernels for 28% -> 28%
where the time goes in v5:
time: 317 us; the launch traced here: 316 us
  Pallas kernels  108 us (34%)
  starting transfers between devices  93 us (29%)
  waiting for transfers between devices  64.3 us (20%)
  local copies, waits for them, and re-layouts  33.7 us (11%)
  between operations  16.2 us (5%)
    ppermute x81, starting transfers between devices, swap(): return lax.ppermute(x, axis, [(i, i ^ mask) for i in range(size)])  92.9 us
    ppermute x81, waiting for transfers between devices, swap(): return lax.ppermute(x, axis, [(i, i ^ mask) for i in range(size)])  64.2 us
    unnamed x104, local copies, waits for them, and re-layouts  30.6 us
    pallas_call x1, Pallas kernels, projector(): pl.pallas_call(kernel, out_shape=(jax.ShapeDtypeStruct((rows_all, hidden)...  16 us
    pallas_call x6, Pallas kernels, fold(): pl.pallas_call(whole_kernel, grid=(count,), in_specs=[SMEM] + [unit(x.sha...  14 us
    pallas_call x2, Pallas kernels, middle_weight(): pl.pallas_call(kernel, grid=(count,), in_specs=[SMEM, whole(slabs, 8, cha...  10.9 us
    pallas_call x1, Pallas kernels, last_back(): pl.pallas_call(kernel, grid=(steps,), in_specs=[lanes_of(block, rows), la...  10.3 us
    pallas_call x1, Pallas kernels, projector_weights(): pl.pallas_call(kernel, grid_spec=pltpu.PrefetchScalarGridSpec(num_scalar_...  6.51 us
  transfers between devices with their start and end apart: 83, of which 51 were waited for; matrix products, arithmetic and copies ran while one was open for 1% of the time, Pallas kernels for 28%

profile of v5, /device:TPU:0, one launch (start us, length us, event | category | flops | bytes accessed | tf_op | source)
XLA Modules:
  0.0 315.9 jit_solution(5012470172309929386)
XLA Ops:
  13.5 4.0 %first_conv.1 = (bf16[880,2048]{1,0:T(8,128)(2,1)S(1)}, f32[880,512]{1,0:T(8,128)S(1)}, f32[2,512]{1,0:T(2,128)S(1)}) custom-call(bf16[49,8,2048]{2,1,0:T(8,128)(2,1)S(1)} %bitcast.128, bf16[6,6,6,2048]{3,2,1,0:T(8,128)(2,1)S(1)} %copy-done.41, bf16[25,8,2048]{2,1,0:T(8,128)(2,1)S(1)} %bitcast.129, bf16[2048,512]{1,0:T(8,128)(2,1)S(1)} %copy-done.36), custom_call_target="tpu_custom_call" | custom-call | flops 1845493760 | bytes 10485760 | tf_op jit(solution)/shard_map/first_conv/pallas_call | solution.py:183
  18.8 3.8 %collective-permute-start.3 = (f32[2,512]{1,0:T(2,128)S(1)}, f32[2,512]{1,0:T(2,128)S(1)}, u32[]{:S(2)}, u32[]{:S(2)}) collective-permute-start(f32[2,512]{1,0:T(2,128)S(1)} %add.243), channel_id=1, source_target_pairs={{0,24},{8,16},{16,8},{24,0},{1,25},{9,17},{17,9},{25,1},{2,26},{10... | collective-permute-start | bytes 12296 | tf_op jit(solution)/shard_map/ppermute | solution.py:928
  26.7 3.6 %collective-permute-start.6 = (f32[2,512]{1,0:T(2,128)S(1)}, f32[2,512]{1,0:T(2,128)S(1)}, u32[]{:S(2)}, u32[]{:S(2)}) collective-permute-start(f32[2,512]{1,0:T(2,128)S(1)} %add_add_fusion.10), channel_id=1, source_target_pairs={{0,6},{1,7},{2,4},{3,5},{4,2},{5,3},{6,0},{7,1},{8,14},{9,15},{10,... | collective-permute-start | bytes 12296 | tf_op jit(solution)/shard_map/ppermute | solution.py:928
  34.9 4.4 %middle_conv.1 = (f32[110,8,512]{2,1,0:T(8,128)S(1)}, f32[880,512]{1,0:T(8,128)S(1)}, f32[2,512]{1,0:T(2,128)S(1)}) custom-call(f32[880,512]{1,0:T(8,128)S(1)} %get-tuple-element.120.a_ref.f_ref, f32[2,512]{1,0:T(2,128)S(1)} %add_add_fusion.9.st_ref.is_ref, f32[1,512]{1,0:T(1,128)S(1)} %bitcast.118, f32[1,512]{1,0:T(1,128)S(1)} %bitcast.135, ...), custom_call_target="tpu_custom_call" | custom-call | flops 4152360960 | bytes 20971520 | tf_op jit(solution)/shard_map/middle_conv/pallas_call | solution.py:257
  52.3 3.8 %last_conv.1 = (bf16[880,512]{1,0:T(8,128)(2,1)S(1)}, f32[880,2048]{1,0:T(8,128)S(1)}, f32[2,2048]{1,0:T(2,128)S(1)}) custom-call(f32[880,512]{1,0:T(8,128)S(1)} %get-tuple-element.122.a_ref.m_ref, f32[2,512]{1,0:T(2,128)S(1)} %add_add_fusion.7.st_ref.ms_ref, f32[1,512]{1,0:T(1,128)S(1)} %bitcast.123, f32[1,512]{1,0:T(1,128)S(1)} %bitcast.121, ...), custom_call_target="tpu_custom_call" | custom-call | flops 1845493760 | bytes 12582912 | tf_op jit(solution)/shard_map/last_conv/pallas_call | solution.py:294
  71.6 6.1 %pool_embed.1 = (f32[24,2048]{1,0:T(8,128)}, f32[24,1024]{1,0:T(8,128)S(1)}) custom-call(f32[880,2048]{1,0:T(8,128)S(1)} %get-tuple-element.124.a_ref, f32[2,2048]{1,0:T(2,128)S(1)} %add_add_fusion.2.st_ref, f32[1,2048]{1,0:T(1,128)S(1)} %bitcast.112, f32[1,2048]{1,0:T(1,128)S(1)} %bitcast.115, bf16[880,2048]{1,0:T(8,128)(2,1)S(1)} %get-tuple-element.126.x_ref, ...), custom_call_target="tpu_custom_call" | custom-call | flops 402653184 | bytes 16777216 | tf_op jit(solution)/shard_map/pool_embed/pallas_call | solution.py:348
  82.9 3.3 %collective-permute-done.22.refs_2_ = f32[1,24,1024]{2,1,0:T(8,128)S(1)} collective-permute-done((f32[1,24,1024]{2,1,0:T(8,128)S(1)}, f32[1,24,1024]{2,1,0:T(8,128)S(1)}, u32[]{:S(2)}, u32[]{:S(2)}) %collective-permute-start.22) | collective-permute-done | bytes 98336 | tf_op jit(solution)/shard_map/ppermute | solution.py:928
  89.9 3.1 copy-done.1
  95.0 6.2 %slope_sums.1 = (bf16[880,2048]{1,0:T(8,128)(2,1)S(1)}, f32[24,2048]{1,0:T(8,128)S(1)}, f32[24,2048]{1,0:T(8,128)S(1)}, f32[4,24,1024]{2,1,0:T(8,128)S(1)}) custom-call(f32[880,2048]{1,0:T(8,128)S(1)} %copy-done.1, f32[2,2048]{1,0:T(2,128)S(1)} %add_add_fusion.2.st_ref, f32[1,2048]{1,0:T(1,128)S(1)} %bitcast.113, f32[1,2048]{1,0:T(1,128)S(1)} %bitcast.116, ...), custom_call_target="tpu_custom_call" | custom-call | flops 43253760 | bytes 14417920 | tf_op jit(solution)/shard_map/slope_sums/pallas_call | solution.py:386
  105.4 16.0 %projector.1 = (f32[768,1024]{1,0:T(8,128)S(1)}, f32[768,1024]{1,0:T(8,128)S(1)}, f32[768,128]{1,0:T(8,128)S(1)}, f32[1,1024]{1,0:T(1,128)}, f32[1,1024]{1,0:T(1...) custom-call(f32[4,24,1024]{2,1,0:T(8,128)S(1)} %get-tuple-element.129.refs_0_, ...), custom_call_target="tpu_custom_call" | custom-call | flops 10737418240 | bytes 20971520 | tf_op jit(solution)/shard_map/projector/pallas_call | solution.py:584
  141.4 10.3 %last_back.1 = (f32[880,512]{1,0:T(8,128)S(1)}, f32[2,512]{1,0:T(2,128)S(1)}, f32[512,2048]{1,0:T(8,128)}) custom-call(bf16[880,2048]{1,0:T(8,128)(2,1)S(1)} %get-tuple-element.128.s_ref, f32[24,2048]{1,0:T(8,128)S(1)} %get-tuple-element.132.e_ref, f32[880,2048]{1,0:T(8,128)} %copy-done, f32[2,2048]{1,0:T(2,128)S(1)} %add_add_fusion.2.st_ref, ...), custom_call_target="tpu_custom_call" | custom-call | flops 3690987520 | bytes 25165824 | tf_op jit(solution)/shard_map/last_back/pallas_call | solution.py:713
  173.4 6.0 %middle_back.1 = (bf16[880,512]{1,0:T(8,128)(2,1)S(1)}, f32[880,512]{1,0:T(8,128)S(1)}, f32[2,512]{1,0:T(2,128)S(1)}) custom-call(f32[880,512]{1,0:T(8,128)S(1)} %copy-done.39, f32[2,512]{1,0:T(2,128)S(1)} %add_add_fusion.5.gs_ref, f32[880,512]{1,0:T(8,128)S(1)} %copy-done.18, f32[2,512]{1,0:T(2,128)S(1)} %add_add_fusion.7.st_ref.ms_ref, ...), custom_call_target="tpu_custom_call" | custom-call | flops 4152360960 | bytes 20971520 | tf_op jit(solution)/shard_map/middle_back/pallas_call | solution.py:763
  180.6 5.8 %middle_weight.2 = (f32[5,4,64,512]{3,2,1,0:T(8,128)S(1)}, f32[5,4,64,512]{3,2,1,0:T(8,128)S(1)}, f32[2,512]{1,0:T(2,128)S(1)}, f32[8,128]{1,0:T(8,128)}) custom-call(s32[3]{0:T(128)S(1)} %pad_add_fusion.at_ref, f32[110,8,512]{2,1,0:T(8,128)S(1)} %copy-done.50, bf16[880,512]{1,0:T(8,128)(2,1)S(1)} %get-tuple-element.140.g_ref, f32[2,512]{1,0:T(2,128)S(1)} %add.282.refs_0_), custom_call_target="tpu_custom_call" | custom-call | flops 2306867200 | bytes 12582912 | tf_op jit(solution)/shard_map/middle_weight/pallas_call | solution.py:815
  186.7 2.8 collective-permute-start.49
  197.5 3.0 collective-permute-done.50
  205.1 5.3 %first_back.1 = (bf16[880,512]{1,0:T(8,128)(2,1)S(1)}, f32[4,4,64,512]{3,2,1,0:T(8,128)}, f32[4,4,64,512]{3,2,1,0:T(8,128)S(1)}, f32[8,128]{1,0:T(8,128)S(1)}) custom-call(s32[3]{0:T(128)S(1)} %pad_add_fusion.at_ref, f32[880,512]{1,0:T(8,128)S(1)} %get-tuple-element.138.gq_ref, f32[2,512]{1,0:T(2,128)S(1)} %add.287.gs_ref, f32[880,512]{1,0:T(8,128)S(1)} %copy-done.15, ...), custom_call_target="tpu_custom_call" | custom-call | flops 1845493760 | bytes 10485760 | tf_op jit(solution)/shard_map/first_back/pallas_call | solution.py:856
  215.5 5.1 %middle_weight.3 = (f32[4,4,64,512]{3,2,1,0:T(8,128)}, f32[4,4,64,512]{3,2,1,0:T(8,128)S(1)}, f32[8,128]{1,0:T(8,128)S(1)}) custom-call(s32[3]{0:T(128)S(1)} %pad_add_fusion.at_ref, f32[110,8,512]{2,1,0:T(8,128)S(1)} %copy-done.50, bf16[880,512]{1,0:T(8,128)(2,1)S(1)} %get-tuple-element.140.g_ref, f32[8,128]{1,0:T(8,128)S(1)} %get-tuple-element.159.refs_0_), custom_call_target="tpu_custom_call" | custom-call | flops 1845493760 | bytes 12582912 | tf_op jit(solution)/shard_map/middle_weight/pallas_call | solution.py:815
  226.0 3.7 %fold_first.4 = (f32[4,5,2,8,512]{4,3,2,1,0:T(8,128)}, f32[4,5,2,8,512]{4,3,2,1,0:T(8,128)S(1)}, f32[4,5,2,8,512]{4,3,2,1,0:T(8,128)}, f32[4,5,2,8,512]{4,3,2,1,0:T(8,128)S(1)}, f32[8,128]{1,0:T(8,128)S(1)}) custom-call(s32[3]{0:T(128)S(1)} %pad_add_fusion.at_ref, f32[4,4,4,16,512]{4,3,2,1,0:T(8,128)S(1)} %bitcast.96, ...), custom_call_target="tpu_custom_call" | custom-call | bytes 8388608 | tf_op jit(solution)/shard_map/fold_first/pallas_call | solution.py:991
  236.6 6.5 %projector_weights.1 = (f32[256,1024]{1,0:T(8,128)}, f32[128,128]{1,0:T(8,128)}, f32[8,128]{1,0:T(8,128)}) custom-call(s32[33]{0:T(128)} %concatenate.7.at_ref, f32[32,24,2048]{2,1,0:T(8,128)} %bitcast.137, f32[768,1024]{1,0:T(8,128)} %copy-done.10, f32[768,1024]{1,0:T(8,128)} %copy-done.9, f32[768,128]{1,0:T(8,128)} %copy-done.20, f32[8,128]{1,0:T(8,128)} %copy-done.30), custom_call_target="tpu_custom_call" | custom-call | flops 2147483648 | bytes 16777216 | tf_op jit(solution)/shard_map/projector_weights/pallas_call | solution.py:634
  243.8 3.0 fold_first.5
  251.8 4.4 %input_grads.1 = (f32[49,8,2048]{2,1,0:T(8,128)}, f32[6,6,6,2048]{3,2,1,0:T(8,128)}, f32[25,8,2048]{2,1,0:T(8,128)}, f32[8,128]{1,0:T(8,128)S(1)}) custom-call(bf16[880,2048]{1,0:T(8,128)(2,1)S(1)} %copy-done.8, f32[24,2048]{1,0:T(8,128)S(1)} %copy-done.26, bf16[880,512]{1,0:T(8,128)(2,1)S(1)} %copy-done.43, bf16[2048,512]{1,0:T(8,128)(2,1)S(1)} %copy-done.37, ...), custom_call_target="tpu_custom_call" | custom-call | flops 1845493760 | bytes 16777216 | tf_op jit(solution)/shard_map/input_grads/pallas_call | solution.py:900
  259.9 2.9 collective-permute-start.63
  279.4 2.9 collective-permute-start.69
  294.0 4.2 %collective-permute-done.77 = f32[4,1,16,512]{3,2,0,1:T(8,128)S(1)} collective-permute-done((f32[4,1,16,512]{3,2,0,1:T(8,128)S(1)}, f32[4,1,16,512]{3,2,0,1:T(8,128)S(1)}, u32[]{:S(2)}, u32[]{:S(2)}) %collective-permute-start.77) | collective-permute-done | bytes 131104 | tf_op jit(solution)/shard_map/ppermute | solution.py:928
  (309 shorter events, 179.7 us)
Async XLA Ops:
  8.0 159.3 %all-gather.3.cloned.1.call-start = ((), (), s32[]{:S(2)}) async-start(), calls=%async_computation.2 | async-start | bytes 6488064 | tf_op jit(solution)/shard_map/all_gather | solution.py:1362
  77.7 145.6 %reduce-scatter.2.cloned.1.call-start = ((), (), s32[]{:S(2)}) async-start(), calls=%async_computation.1 | async-start | bytes 4718592 | tf_op jit(solution)/shard_map/reduce_scatter | solution.py:1363
  86.3 15.0 %collective-permute-start.24 = (f32[4,24,1024]{2,1,0:T(8,128)S(1)}, f32[4,24,1024]{2,1,0:T(8,128)S(1)}, u32[]{:S(2)}, u32[]{:S(2)}) collective-permute-start(f32[4,24,1024]{2,1,0:T(8,128)S(1)} %bitcast.97), channel_id=1, source_target_pairs={{0,8},{8,0},{16,24},{24,16},{1,9},{9,1},{17,25},{25,17},{2,10},{10... | collective-permute-start | bytes 1179656 | tf_op jit(solution)/shard_map/ppermute | solution.py:928
  86.9 15.3 %collective-permute-start.25 = (f32[4,24,1024]{2,1,0:T(8,128)S(1)}, f32[4,24,1024]{2,1,0:T(8,128)S(1)}, u32[]{:S(2)}, u32[]{:S(2)}) collective-permute-start(f32[4,24,1024]{2,1,0:T(8,128)S(1)} %bitcast.98), channel_id=1, source_target_pairs={{0,16},{8,24},{16,0},{24,8},{1,17},{9,25},{17,1},{25,9},{2,18},{10... | collective-permute-start | bytes 1179656 | tf_op jit(solution)/shard_map/ppermute | solution.py:928
  88.4 15.2 %collective-permute-start.26 = (f32[4,24,1024]{2,1,0:T(8,128)S(1)}, f32[4,24,1024]{2,1,0:T(8,128)S(1)}, u32[]{:S(2)}, u32[]{:S(2)}) collective-permute-start(f32[4,24,1024]{2,1,0:T(8,128)S(1)} %bitcast.99), channel_id=1, source_target_pairs={{0,24},{8,16},{16,8},{24,0},{1,25},{9,17},{17,9},{25,1},{2,26},{10... | collective-permute-start | bytes 1179656 | tf_op jit(solution)/shard_map/ppermute | solution.py:928
  194.9 16.4 %collective-permute-start.52 = (f32[5,4,2,8,512]{4,3,2,1,0:T(8,128)S(1)}, f32[5,4,2,8,512]{4,3,2,1,0:T(8,128)S(1)}, u32[]{:S(2)}, u32[]{:S(2)}) collective-permute-start(f32[5,4,2,8,512]{4,3,2,1,0:T(8,128)S(1)} %get-tuple-element.148), channel_id=1, source_target_pairs={{0,8},{8,0},{16,24},{24,16},{1,9},{9,1},{17,25},{25,17},{2,10},{10... | collective-permute-start | bytes 1966088 | tf_op jit(solution)/shard_map/ppermute | solution.py:928
  195.3 16.0 %collective-permute-start.53 = (f32[5,4,2,8,512]{4,3,2,1,0:T(8,128)S(1)}, f32[5,4,2,8,512]{4,3,2,1,0:T(8,128)S(1)}, u32[]{:S(2)}, u32[]{:S(2)}) collective-permute-start(f32[5,4,2,8,512]{4,3,2,1,0:T(8,128)S(1)} %get-tuple-element.150), channel_id=1, source_target_pairs={{0,16},{8,24},{16,0},{24,8},{1,17},{9,25},{17,1},{25,9},{2,18},{10... | collective-permute-start | bytes 1966088 | tf_op jit(solution)/shard_map/ppermute | solution.py:928
  211.3 12.1 %collective-permute-start.56 = (f32[4,4,64,512]{3,2,1,0:T(8,128)}, f32[4,4,64,512]{3,2,1,0:T(8,128)}, u32[]{:S(2)}, u32[]{:S(2)}) collective-permute-start(f32[4,4,64,512]{3,2,1,0:T(8,128)} %get-tuple-element.157), channel_id=1, source_target_pairs={{0,1},{1,0},{2,3},{3,2},{4,5},{5,4},{6,7},{7,6},{8,9},{9,8},{10,11... | collective-permute-start | bytes 6291464 | tf_op jit(solution)/shard_map/ppermute | solution.py:928
  220.6 22.5 %collective-permute-start.58 = (f32[4,4,64,512]{3,2,1,0:T(8,128)}, f32[4,4,64,512]{3,2,1,0:T(8,128)}, u32[]{:S(2)}, u32[]{:S(2)}) collective-permute-start(f32[4,4,64,512]{3,2,1,0:T(8,128)} %get-tuple-element.165), channel_id=1, source_target_pairs={{0,1},{1,0},{2,3},{3,2},{4,5},{5,4},{6,7},{7,6},{8,9},{9,8},{10,11... | collective-permute-start | bytes 6291464 | tf_op jit(solution)/shard_map/ppermute | solution.py:928
  221.1 11.0 %collective-permute-start.54 = (f32[5,4,8,512]{3,2,1,0:T(8,128)}, f32[5,4,8,512]{3,2,1,0:T(8,128)}, u32[]{:S(2)}, u32[]{:S(2)}) collective-permute-start(f32[5,4,8,512]{3,2,1,0:T(8,128)} %get-tuple-element.153), channel_id=1, source_target_pairs={{0,16},{8,24},{16,0},{24,8},{1,17},{9,25},{17,1},{25,9},{2,18},{10... | collective-permute-start | bytes 983048 | tf_op jit(solution)/shard_map/ppermute | solution.py:928
  221.9 10.2 %collective-permute-start.55 = (f32[5,4,8,512]{3,2,1,0:T(8,128)}, f32[5,4,8,512]{3,2,1,0:T(8,128)}, u32[]{:S(2)}, u32[]{:S(2)}) collective-permute-start(f32[5,4,8,512]{3,2,1,0:T(8,128)} %get-tuple-element.155), channel_id=1, source_target_pairs={{0,8},{8,0},{16,24},{24,16},{1,9},{9,1},{17,25},{25,17},{2,10},{10... | collective-permute-start | bytes 983048 | tf_op jit(solution)/shard_map/ppermute | solution.py:928
  229.7 26.5 %collective-permute-start.59 = (f32[4,5,2,8,512]{4,3,2,1,0:T(8,128)}, f32[4,5,2,8,512]{4,3,2,1,0:T(8,128)}, u32[]{:S(2)}, u32[]{:S(2)}) collective-permute-start(f32[4,5,2,8,512]{4,3,2,1,0:T(8,128)} %get-tuple-element.177), channel_id=1, source_target_pairs={{0,8},{8,0},{16,24},{24,16},{1,9},{9,1},{17,25},{25,17},{2,10},{10... | collective-permute-start | bytes 1966088 | tf_op jit(solution)/shard_map/ppermute | solution.py:928
  230.3 25.9 %collective-permute-start.60 = (f32[4,5,2,8,512]{4,3,2,1,0:T(8,128)}, f32[4,5,2,8,512]{4,3,2,1,0:T(8,128)}, u32[]{:S(2)}, u32[]{:S(2)}) collective-permute-start(f32[4,5,2,8,512]{4,3,2,1,0:T(8,128)} %get-tuple-element.179), channel_id=1, source_target_pairs={{0,16},{8,24},{16,0},{24,8},{1,17},{9,25},{17,1},{25,9},{2,18},{10... | collective-permute-start | bytes 1966088 | tf_op jit(solution)/shard_map/ppermute | solution.py:928
  235.8 13.8 %collective-permute-start.57 = (f32[5,2,16,512]{3,2,1,0:T(8,128)S(1)}, f32[5,2,16,512]{3,2,1,0:T(8,128)S(1)}, u32[]{:S(2)}, u32[]{:S(2)}) collective-permute-start(f32[5,2,16,512]{3,2,1,0:T(8,128)S(1)} %get-tuple-element.163), channel_id=1, source_target_pairs={{0,2},{1,3},{2,0},{3,1},{4,6},{5,7},{6,4},{7,5},{8,10},{9,11},{10,... | collective-permute-start | bytes 983048 | tf_op jit(solution)/shard_map/ppermute | solution.py:928
  246.8 16.0 %collective-permute-start.64 = (f32[4,4,2,8,512]{4,3,2,1,0:T(8,128)S(1)}, f32[4,4,2,8,512]{4,3,2,1,0:T(8,128)S(1)}, u32[]{:S(2)}, u32[]{:S(2)}) collective-permute-start(f32[4,4,2,8,512]{4,3,2,1,0:T(8,128)S(1)} %get-tuple-element.188), channel_id=1, source_target_pairs={{0,8},{8,0},{16,24},{24,16},{1,9},{9,1},{17,25},{25,17},{2,10},{10... | collective-permute-start | bytes 1572872 | tf_op jit(solution)/shard_map/ppermute | solution.py:928
  248.4 14.4 %collective-permute-start.65 = (f32[4,4,2,8,512]{4,3,2,1,0:T(8,128)S(1)}, f32[4,4,2,8,512]{4,3,2,1,0:T(8,128)S(1)}, u32[]{:S(2)}, u32[]{:S(2)}) collective-permute-start(f32[4,4,2,8,512]{4,3,2,1,0:T(8,128)S(1)} %get-tuple-element.190), channel_id=1, source_target_pairs={{0,16},{8,24},{16,0},{24,8},{1,17},{9,25},{17,1},{25,9},{2,18},{10... | collective-permute-start | bytes 1572872 | tf_op jit(solution)/shard_map/ppermute | solution.py:928
  258.6 10.7 %collective-permute-start.61 = (f32[4,5,8,512]{3,2,1,0:T(8,128)S(1)}, f32[4,5,8,512]{3,2,1,0:T(8,128)S(1)}, u32[]{:S(2)}, u32[]{:S(2)}) collective-permute-start(f32[4,5,8,512]{3,2,1,0:T(8,128)S(1)} %get-tuple-element.182), channel_id=1, source_target_pairs={{0,16},{8,24},{16,0},{24,8},{1,17},{9,25},{17,1},{25,9},{2,18},{10... | collective-permute-start | bytes 983048 | tf_op jit(solution)/shard_map/ppermute | solution.py:928
  259.4 9.8 %collective-permute-start.62 = (f32[4,5,8,512]{3,2,1,0:T(8,128)S(1)}, f32[4,5,8,512]{3,2,1,0:T(8,128)S(1)}, u32[]{:S(2)}, u32[]{:S(2)}) collective-permute-start(f32[4,5,8,512]{3,2,1,0:T(8,128)S(1)} %get-tuple-element.184), channel_id=1, source_target_pairs={{0,8},{8,0},{16,24},{24,16},{1,9},{9,1},{17,25},{25,17},{2,10},{10... | collective-permute-start | bytes 983048 | tf_op jit(solution)/shard_map/ppermute | solution.py:928
  263.6 9.6 %collective-permute-start.67 = (f32[4,4,8,512]{3,2,1,0:T(8,128)S(1)}, f32[4,4,8,512]{3,2,1,0:T(8,128)S(1)}, u32[]{:S(2)}, u32[]{:S(2)}) collective-permute-start(f32[4,4,8,512]{3,2,1,0:T(8,128)S(1)} %get-tuple-element.197), channel_id=1, source_target_pairs={{0,16},{8,24},{16,0},{24,8},{1,17},{9,25},{17,1},{25,9},{2,18},{10... | collective-permute-start | bytes 786440 | tf_op jit(solution)/shard_map/ppermute | solution.py:928
  269.8 9.0 %collective-permute-start.66 = (f32[4,2,16,512]{3,2,1,0:T(8,128)S(1)}, f32[4,2,16,512]{3,2,1,0:T(8,128)S(1)}, u32[]{:S(2)}, u32[]{:S(2)}) collective-permute-start(f32[4,2,16,512]{3,2,1,0:T(8,128)S(1)} %get-tuple-element.195), channel_id=1, source_target_pairs={{0,2},{1,3},{2,0},{3,1},{4,6},{5,7},{6,4},{7,5},{8,10},{9,11},{10,... | collective-permute-start | bytes 786440 | tf_op jit(solution)/shard_map/ppermute | solution.py:928
  273.8 12.8 %collective-permute-start.70 = (f32[4,2,16,512]{3,2,1,0:T(8,128)S(1)}, f32[4,2,16,512]{3,2,1,0:T(8,128)S(1)}, u32[]{:S(2)}, u32[]{:S(2)}) collective-permute-start(f32[4,2,16,512]{3,2,1,0:T(8,128)S(1)} %get-tuple-element.206), channel_id=1, source_target_pairs={{0,2},{1,3},{2,0},{3,1},{4,6},{5,7},{6,4},{7,5},{8,10},{9,11},{10,... | collective-permute-start | bytes 786440 | tf_op jit(solution)/shard_map/ppermute | solution.py:928
  287.2 13.5 %collective-permute-start.74 = (f32[8,16,512]{2,1,0:T(8,128)S(1)}, f32[8,16,512]{2,1,0:T(8,128)S(1)}, u32[]{:S(2)}, u32[]{:S(2)}) collective-permute-start(f32[8,16,512]{2,1,0:T(8,128)S(1)} %get-tuple-element.211.refs_0_), channel_id=1, source_target_pairs={{0,8},{8,0},{16,24},{24,16},{1,9},{9,1},{17,25},{25,17},{2,10},{10... | collective-permute-start | bytes 786440 | tf_op jit(solution)/shard_map/ppermute | solution.py:928
  288.9 14.0 %collective-permute-start.75 = (f32[8,16,512]{2,1,0:T(8,128)S(1)}, f32[8,16,512]{2,1,0:T(8,128)S(1)}, u32[]{:S(2)}, u32[]{:S(2)}) collective-permute-start(f32[8,16,512]{2,1,0:T(8,128)S(1)} %get-tuple-element.211.refs_0_), channel_id=1, source_target_pairs={{0,16},{8,24},{16,0},{24,8},{1,17},{9,25},{17,1},{25,9},{2,18},{10... | collective-permute-start | bytes 786440 | tf_op jit(solution)/shard_map/ppermute | solution.py:928
  289.8 13.0 %collective-permute-start.76 = (f32[8,16,512]{2,1,0:T(8,128)S(1)}, f32[8,16,512]{2,1,0:T(8,128)S(1)}, u32[]{:S(2)}, u32[]{:S(2)}) collective-permute-start(f32[8,16,512]{2,1,0:T(8,128)S(1)} %get-tuple-element.211.refs_0_), channel_id=1, source_target_pairs={{0,24},{8,16},{16,8},{24,0},{1,25},{9,17},{17,9},{25,1},{2,26},{10... | collective-permute-start | bytes 786440 | tf_op jit(solution)/shard_map/ppermute | solution.py:928
  (111 other events, 864.2 us)
Sparse Core Ops, SparseCore 0:
  77.9 69.3 all-gather.2
Sparse Core Ops, SparseCore 1:
  153.0 50.2 reduce-scatter.1
